TPU v7x, 128 devices: a whole 4x4x4 slice. The times are simulated.
128 devices in a mesh: lat: 4 (over x_lo, core), lon: 32 (over y, x_hi, z).
Axes of the slice: x: 4 (x_hi: 2, x_lo: 2; x = x_hi * 2 + x_lo), y: 4, z: 4, core: 2. Of those that a mesh axis runs over, the one named last changes fastest.
Arguments:
- feature: bfloat16 [64, 1024, 256], P('lat', 'lon'), may hold values from -6 to 6
- filters: bfloat16 [64, 9, 25], P('lat'), may hold values from -1.25 to 1.25
- start: int32 [64], P('lat'), may hold values from 0 to 63, as said below
- length: int32 [64], P('lat'), may hold values from 1 to 5, as said below
- weight: bfloat16 [9, 256, 256], replicated, may hold values from -0.125 to 0.125
- cotangent: bfloat16 [64, 1024, 256], P('lat', 'lon'), may hold values from -6 to 6
Outputs:
- mixed: bfloat16 [64, 1024, 256], P('lat', 'lon')
- grad_feature: bfloat16 [64, 1024, 256], P('lat', 'lon')
- grad_weight: float32 [9, 256, 256], replicated
Inputs may be any that keep to these rules, and one draw needn't show every extreme that they name: start[i] >= max(i - 2, 0) and start[i] + length[i] <= min(i + 3, 64). `length`: some row's support has the full 5 rows.
All inputs are finite; a program needn't handle non-finite values.
Results may differ from a plain program's by a relative error of at most 0.0049.
Values may be sent and summed in bfloat16 or wider, within the bound.
No kernel may reach another device: no remote copies, remote signals or barrier semaphores. Data moves between devices by JAX's collectives and lax.ppermute only.
A program may use at most 128 MiB of HBM per device.

v0:
```python
import math

import jax
import jax.numpy as jnp
from jax import lax
from jax.sharding import PartitionSpec as P

LAT_REACH = 2
LON_REACH = 2


def with_halo(array, sides, width, wrap):
    for axis, dim in sides:
        count, length = (lax.axis_size(axis), array.shape[dim])
        up = [(i, (i + 1) % count) for i in range(count if wrap else count - 1)]
        down = [(j, i) for i, j in up]
        last = lax.slice_in_dim(array, length - width, length, axis=dim)
        initial = lax.slice_in_dim(array, 0, width, axis=dim)
        before = lax.ppermute(last, axis, up)
        after = lax.ppermute(initial, axis, down)
        array = jnp.concatenate([before, array, after], axis=dim)
    return array


def shards(feature, filters, start, length, weight, cotangent):
    lat_rows, lon_cells, channels = feature.shape
    basis_count = weight.shape[0]
    band_rows = 2 * LAT_REACH + 1
    lon_taps = 2 * LON_REACH + 1
    row_global = lax.axis_index("lat") * lat_rows + jnp.arange(lat_rows, dtype=jnp.int32)
    source = row_global[:, None] - LAT_REACH + jnp.arange(band_rows, dtype=jnp.int32)[None, :]
    inside = (source >= start[:, None]) & (source < (start + length)[:, None])
    masked = (
        filters.reshape(lat_rows, basis_count, band_rows, lon_taps)
        * inside.astype(jnp.bfloat16)[:, None, :, None]
    )
    masked = masked.reshape(lat_rows, basis_count, band_rows * lon_taps)
    widened = with_halo(feature, (("lon", 1),), LON_REACH, True)
    padded = with_halo(widened, (("lat", 0),), LAT_REACH, False)
    mixing = weight.reshape(basis_count * channels, channels)
    block_rows = math.gcd(lat_rows, 8)
    block_count = lat_rows // block_rows

    def row_step(grad_total, block_index):
        row_first = block_index * block_rows
        rows_in = lax.dynamic_slice_in_dim(padded, row_first, block_rows + 2 * LAT_REACH, 0)
        taps_block = lax.dynamic_slice_in_dim(masked, row_first, block_rows, 0).astype(jnp.float32)
        basis_acc = jnp.zeros((block_rows, lon_cells, basis_count, channels), jnp.float32)
        for lat_tap in range(band_rows):
            for lon_tap in range(lon_taps):
                tap_index = lat_tap * lon_taps + lon_tap
                shifted = rows_in[
                    lat_tap : lat_tap + block_rows, lon_tap : lon_tap + lon_cells
                ].astype(jnp.float32)
                basis_acc = (
                    basis_acc + taps_block[:, None, :, tap_index, None] * shifted[:, :, None, :]
                )
        basis_out = basis_acc.astype(jnp.bfloat16)
        flat = basis_out.reshape(block_rows * lon_cells, basis_count * channels)
        output = jnp.dot(flat, mixing, preferred_element_type=jnp.float32).astype(jnp.bfloat16)
        upstream = lax.dynamic_slice_in_dim(cotangent, row_first, block_rows, 0).reshape(
            block_rows * lon_cells, channels
        )
        grad_back = lax.dot_general(
            upstream, mixing, (((1,), (1,)), ((), ())), preferred_element_type=jnp.float32
        ).astype(jnp.bfloat16)
        grad_total = grad_total + lax.dot_general(
            flat, upstream, (((0,), (0,)), ((), ())), preferred_element_type=jnp.float32
        )
        return (
            grad_total,
            (
                output.reshape(block_rows, lon_cells, channels),
                grad_back.reshape(block_rows, lon_cells, basis_count, channels),
            ),
        )

    grad_total, (outputs, grad_backs) = lax.scan(
        row_step,
        jnp.zeros((basis_count * channels, channels), jnp.float32),
        jnp.arange(block_count, dtype=jnp.int32),
    )
    mixed = outputs.reshape(lat_rows, lon_cells, channels)
    grad_basis = grad_backs.reshape(lat_rows, lon_cells, basis_count, channels)
    summed = lax.psum(grad_total, ("lat", "lon"))
    cell_total = lat_rows * lax.axis_size("lat") * lon_cells * lax.axis_size("lon")
    grad_weight = (summed * (1.0 / math.sqrt(cell_total))).reshape(basis_count, channels, channels)
    grad_wide = with_halo(grad_basis, (("lon", 1),), LON_REACH, True)
    grad_pad = with_halo(grad_wide, (("lat", 0),), LAT_REACH, False)
    taps_pad = with_halo(masked, (("lat", 0),), LAT_REACH, False)
    accum = jnp.zeros((lat_rows, lon_cells, channels), jnp.float32)
    for lat_tap in range(band_rows):
        row_offset = 2 * LAT_REACH - lat_tap
        for lon_tap in range(lon_taps):
            tap_index = lat_tap * lon_taps + lon_tap
            col_offset = 2 * LON_REACH - lon_tap
            accum = accum + jnp.einsum(
                "jk,jlkc->jlc",
                taps_pad[row_offset : row_offset + lat_rows, :, tap_index],
                grad_pad[row_offset : row_offset + lat_rows, col_offset : col_offset + lon_cells],
                preferred_element_type=jnp.float32,
            )
    grad_feature = accum.astype(jnp.bfloat16)
    return (mixed, grad_feature, grad_weight)


def solution(mesh):
    return jax.shard_map(
        shards,
        mesh=mesh,
        in_specs=(
            P("lat", "lon", None),
            P("lat", None, None),
            P("lat"),
            P("lat"),
            P(),
            P("lat", "lon", None),
        ),
        out_specs=(P("lat", "lon", None), P("lat", "lon", None), P()),
        check_vma=False,
    )
```

profile of v0, /device:TPU:1, one launch (start us, length us, event | category | flops | bytes accessed | tf_op | source)
XLA Modules:
  0.0 334.8 jit_solution(9607275959787837621)
XLA Ops:
  8.1 2.5 collective-permute-start
  10.7 7.1 %collective-permute-start.1 = (bf16[16,2,256]{2,1,0:T(2,128)(2,1)S(1)}, bf16[16,2,256]{2,1,0:T(2,128)(2,1)S(1)}, u32[]{:S(2)}, u32[]{:S(2)}) collective-permute-start(bf16[16,2,256]{2,1,0:T(2,128)(2,1)S(1)} %get-tuple-element.200), channel_id=1, source_target_pairs={{1,0},{2,1},{3,2},{4,3},{5,4},{6,5},{7,6},{8,7},{9,8},{10,9},{11,1... | collective-permute-start | bytes 49160 | tf_op jit(solution)/shard_map/ppermute | solution.py:20
  20.5 2.9 collective-permute-start.4
  23.6 2.7 collective-permute-start.8
  33.6 2.4 collective-permute-start.3
  40.7 135.3 %while.15 = (s32[]{:T(128)}, f32[2304,256]{1,0:T(8,128)}, bf16[2,8,32,256]{3,2,1,0:T(8,128)(2,1)}, bf16[2,8,32,9,256]{4,3,2,1,0:T(8,128)(2,1)}, s32[2]{0:T(128)}...) while((s32[]{:T(128)}, f32[2304,256]{1,0:T(8,128)}, ...), condition=%wide.region_1.2_spmd.clone, body=%wide.region_0.1_spmd.clone.sunk | while | flops 950142720 | bytes 169391456 | solution.py:78
  65.8 3.6 %dynamic-slice_convert_fusion.28 = (f32[8,32,256]{2,1,0:T(8,128)}, f32[8,32,256]{2,1,0:T(8,128)}, f32[8,32,256]{2,1,0:T(8,128)}, f32[8,32,256]{2,1,0:T(8,128)}, ...) fusion(bf16[20,36,256]{2,1,0:T(8,128)(2,1)S(1)} %get-tuple-elem, ...), kind=kLoop, calls=%fused_computation.40.clone.1 | loop fusion | flops 1638400 | bytes 10092584 | tf_op jit(solution)/shard_map/while/body/eval_jaxpr/convert_element_type | solution.py:54
  71.6 2.4 broadcast_in_dim.18
  74.0 10.2 %add_convert_fusion.8 = (bf16[8,32,9,256]{3,2,1,0:T(8,128)(2,1)S(1)}, f32[8,32,9,256]{3,2,1,0:T(8,128)S(1)}) fusion(f32[8,32,256]{2,1,0:T(8,128)S(1)} %get-tuple-element.336, f32[8,9]{1,0:T(8,128)} %get-tuple-element.337, f32[8,32,256]{2,1,0:T(8,128)S(1)} %get-tuple-element.338, f32[8,9]{1,0:T(8,128)} %get-tuple-element.339, ...), kind=kLoop, calls=%fused_computation.1.clone.1 | loop fusion | flops 29491200 | bytes 10099744 | tf_op jit(solution)/shard_map/while/body/eval_jaxpr/convert_element_type | solution.py:58
  84.9 2.2 copy.292
  90.3 2.1 copy.284
  93.1 2.1 copy.285
  95.9 2.1 copy.286
  98.8 2.1 copy.287
  101.6 2.1 copy.288
  104.3 2.1 copy.289
  107.1 2.1 copy.290
  109.9 2.1 copy.291
  112.6 2.2 copy.293
  121.0 3.6 %dynamic-slice_convert_fusion.28 = (f32[8,32,256]{2,1,0:T(8,128)}, f32[8,32,256]{2,1,0:T(8,128)}, f32[8,32,256]{2,1,0:T(8,128)}, f32[8,32,256]{2,1,0:T(8,128)}, ...) fusion(bf16[20,36,256]{2,1,0:T(8,128)(2,1)S(1)} %get-tuple-elem, ...), kind=kLoop, calls=%fused_computation.40.clone.1 | loop fusion | flops 1638400 | bytes 10092584 | tf_op jit(solution)/shard_map/while/body/eval_jaxpr/convert_element_type | solution.py:54
  126.8 2.4 broadcast_in_dim.18
  129.3 10.2 %add_convert_fusion.8 = (bf16[8,32,9,256]{3,2,1,0:T(8,128)(2,1)S(1)}, f32[8,32,9,256]{3,2,1,0:T(8,128)S(1)}) fusion(f32[8,32,256]{2,1,0:T(8,128)S(1)} %get-tuple-element.336, f32[8,9]{1,0:T(8,128)} %get-tuple-element.337, f32[8,32,256]{2,1,0:T(8,128)S(1)} %get-tuple-element.338, f32[8,9]{1,0:T(8,128)} %get-tuple-element.339, ...), kind=kLoop, calls=%fused_computation.1.clone.1 | loop fusion | flops 29491200 | bytes 10099744 | tf_op jit(solution)/shard_map/while/body/eval_jaxpr/convert_element_type | solution.py:58
  140.1 2.2 copy.292
  145.7 2.1 copy.284
  148.5 2.1 copy.285
  151.3 2.1 copy.286
  154.1 2.1 copy.287
  156.9 2.1 copy.288
  159.7 2.1 copy.289
  162.5 2.1 copy.290
  165.2 2.1 copy.291
  168.0 2.2 copy.293
  176.0 4.2 %copy.271 = bf16[2,8,32,9,256]{4,1,0,3,2:T(8,128)(2,1)S(1)} copy(bf16[2,8,32,9,256]{4,3,2,1,0:T(8,128)(2,1)} %get-tuple-element.53) | data formatting | bytes 4718592 | tf_op jit(solution)/shard_map/while | solution.py:78
  180.3 7.2 %collective-permute-start.6 = (bf16[16,2,9,256]{3,0,2,1:T(8,128)(2,1)S(1)}, bf16[16,2,9,256]{3,0,2,1:T(8,128)(2,1)S(1)}, u32[]{:S(2)}, u32[]{:S(2)}) collective-permute-start(bf16[16,2,9,256]{3,0,2,1:T(8,128)(2,1)S(1)} %get-tuple-element.196), channel_id=1, source_target_pairs={{1,0},{2,1},{3,2},{4,3},{5,4},{6,5},{7,6},{8,7},{9,8},{10,9},{11,1... | collective-permute-start | bytes 442376 | tf_op jit(solution)/shard_map/ppermute | solution.py:20
  187.5 3.8 %fusion.65 = f32[16,1,32,256]{3,1,2,0:T(1,128)} fusion(bf16[16,32,9,256]{3,2,1,0:T(8,128)(2,1)} %bitcast.42, bf16[16,9,1,1]{1,0,2,3:T(8,128)(2,1)S(1)} %copy-done.63), kind=kOutput, calls=%fused_computation.176 | convolution fusion | flops 2359296 | bytes 2883872 | tf_op jit(solution)/shard_map/jk,jlkc->jlc/dot_general | solution.py:97
  191.8 2.4 collective-permute-start.9
  194.2 2.0 collective-permute-start.7
  196.2 2.3 fusion.51
  198.6 2.5 fusion.28
  201.0 2.5 fusion.26
  203.5 2.5 fusion.22
  206.0 2.5 fusion.24
  208.5 4.9 %maximum_maximum_fusion = (bf16[18,36,9,256]{3,0,2,1:T(8,128)(2,1)S(1)}, bf16[18,36,9,256]{3,0,2,1:T(8,128)(2,1)S(1)}) fusion(bf16[16,2,9,256]{3,0,2,1:T(8,128)(2,1)S(1)} %collective-permute-done.6, bf16[16,32,9,256]{3,0,2,1:T(8,128)(2,1)S(1)} %bitcast.393, bf16[16,2,9,256]{3,0,2,1:T(8,128)(2,1)S(1)} %collective-permute-done.5, ...), kind=kLoop, calls=%fused_computation.119 | loop fusion | flops 23887872 | bytes 9289728 | tf_op jit(solution)/shard_map/concatenate | solution.py:21
  213.4 10.8 %fusion.86 = (bf16[16,32,9,256]{3,0,2,1:T(8,128)(2,1)}, bf16[16,32,9,256]{3,0,2,1:T(8,128)(2,1)}, bf16[16,32,9,256]{3,0,2,1:T(8,128)(2,1)}, bf16[16,32,9,256]{3,...) fusion(bf16[18,36,9,256]{3,0,2,1:T(8,128)(2,1)S(1)} %get-tuple-, ...), kind=kLoop, calls=%fused_computation.224 | loop fusion | bytes 47185920 | tf_op jit(solution)/shard_map/slice | solution.py:100
  224.1 9.9 %fusion.85 = (bf16[16,32,9,256]{3,0,2,1:T(8,128)(2,1)}, bf16[16,32,9,256]{3,0,2,1:T(8,128)(2,1)}, bf16[16,32,9,256]{3,0,2,1:T(8,128)(2,1)}, bf16[16,32,9,256]{3,...) fusion(bf16[18,36,9,256]{3,0,2,1:T(8,128)(2,1)S(1)} %get-tuple-, ...), kind=kLoop, calls=%fused_computation.223 | loop fusion | bytes 47185920 | tf_op jit(solution)/shard_map/slice | solution.py:100
  234.1 3.5 %fusion.48 = f32[16,1,32,256]{3,1,2,0:T(1,128)S(1)} fusion(bf16[16,32,9,256]{3,0,2,1:T(8,128)(2,1)} %get-tuple-element.174, bf16[16,9,1,1]{1,0,2,3:T(8,128)(2,1)S(1)} %copy-done.47), kind=kOutput, calls=%fused_computation.116 | convolution fusion | flops 2359296 | bytes 2883872 | tf_op jit(solution)/shard_map/jk,jlkc->jlc/dot_general | solution.py:97
  272.5 52.0 %all-reduce.2.cloned.1.call-done = f32[2304,256]{1,0:T(8,128)} async-done(((f32[2304,256]{1,0:T(8,128)}), f32[2304,256]{1,0:T(8,128)}) %all-reduce.2.cloned.1.call-update) | async-done | bytes 2359312 | tf_op jit(solution)/shard_map/psum | solution.py:85
  324.5 3.2 broadcast_multiply_fusion.9
  (274 shorter events, 83.7 us)
Async XLA Ops:
  7.2 317.4 %all-reduce.2.cloned.1.call-start = ((), (), s32[]{:S(2)}) async-start(), calls=%async_computation | async-start | bytes 4718592 | tf_op jit(solution)/shard_map/psum | solution.py:85
  8.1 22.8 %collective-permute-start = (bf16[16,2,256]{2,1,0:T(2,128)(2,1)S(1)}, bf16[16,2,256]{2,1,0:T(2,128)(2,1)S(1)}, u32[]{:S(2)}, u32[]{:S(2)}) collective-permute-start(bf16[16,2,256]{2,1,0:T(2,128)(2,1)S(1)} %get-tuple-element.199), channel_id=1, source_target_pairs={{0,1},{1,2},{2,3},{3,4},{4,5},{5,6},{6,7},{7,8},{8,9},{9,10},{10,1... | collective-permute-start | bytes 49160 | tf_op jit(solution)/shard_map/ppermute | solution.py:19
  10.7 20.2 %collective-permute-start.1 = (bf16[16,2,256]{2,1,0:T(2,128)(2,1)S(1)}, bf16[16,2,256]{2,1,0:T(2,128)(2,1)S(1)}, u32[]{:S(2)}, u32[]{:S(2)}) collective-permute-start(bf16[16,2,256]{2,1,0:T(2,128)(2,1)S(1)} %get-tuple-element.200), channel_id=1, source_target_pairs={{1,0},{2,1},{3,2},{4,3},{5,4},{6,5},{7,6},{8,7},{9,8},{10,9},{11,1... | collective-permute-start | bytes 49160 | tf_op jit(solution)/shard_map/ppermute | solution.py:20
  20.5 7.6 %collective-permute-start.4 = (bf16[2,9,25]{1,0,2:T(2,128)(2,1)S(1)}, bf16[2,9,25]{1,0,2:T(2,128)(2,1)S(1)}, u32[]{:S(2)}, u32[]{:S(2)}) collective-permute-start(bf16[2,9,25]{1,0,2:T(2,128)(2,1)S(1)} %bitcast.399), channel_id=1, source_target_pairs={{32,0},{64,32},{96,64},{33,1},{65,33},{97,65},{34,2},{66,34},{98,6... | collective-permute-start | bytes 2708 | tf_op jit(solution)/shard_map/ppermute | solution.py:20
  23.6 5.9 %collective-permute-start.8 = (bf16[2,9,25]{1,0,2:T(2,128)(2,1)S(1)}, bf16[2,9,25]{1,0,2:T(2,128)(2,1)S(1)}, u32[]{:S(2)}, u32[]{:S(2)}) collective-permute-start(bf16[2,9,25]{1,0,2:T(2,128)(2,1)S(1)} %bitcast.398), channel_id=1, source_target_pairs={{0,32},{32,64},{64,96},{1,33},{33,65},{65,97},{2,34},{34,66},{66,9... | collective-permute-start | bytes 2708 | tf_op jit(solution)/shard_map/ppermute | solution.py:19
  31.7 5.7 %collective-permute-start.2 = (bf16[2,36,256]{2,1,0:T(8,128)(2,1)S(1)}, bf16[2,36,256]{2,1,0:T(8,128)(2,1)S(1)}, u32[]{:S(2)}, u32[]{:S(2)}) collective-permute-start(bf16[2,36,256]{2,1,0:T(8,128)(2,1)S(1)} %get-tuple-element.197), channel_id=1, source_target_pairs={{0,32},{32,64},{64,96},{1,33},{33,65},{65,97},{2,34},{34,66},{66,9... | collective-permute-start | bytes 110600 | tf_op jit(solution)/shard_map/ppermute | solution.py:19
  33.6 5.3 %collective-permute-start.3 = (bf16[2,36,256]{2,1,0:T(8,128)(2,1)S(1)}, bf16[2,36,256]{2,1,0:T(8,128)(2,1)S(1)}, u32[]{:S(2)}, u32[]{:S(2)}) collective-permute-start(bf16[2,36,256]{2,1,0:T(8,128)(2,1)S(1)} %get-tuple-element.198), channel_id=1, source_target_pairs={{32,0},{64,32},{96,64},{33,1},{65,33},{97,65},{34,2},{66,34},{98,6... | collective-permute-start | bytes 110600 | tf_op jit(solution)/shard_map/ppermute | solution.py:20
  65.8 4.3 %copy-start = (bf16[2304,256]{1,0:T(8,128)(2,1)S(1)}, bf16[2304,256]{1,0:T(8,128)(2,1)}, u32[]{:S(2)}) copy-start(bf16[2304,256]{1,0:T(8,128)(2,1)} %get-tuple-element.433) | copy-start | bytes 3538948 | tf_op jit(solution)/shard_map/while
  121.0 4.3 %copy-start = (bf16[2304,256]{1,0:T(8,128)(2,1)S(1)}, bf16[2304,256]{1,0:T(8,128)(2,1)}, u32[]{:S(2)}) copy-start(bf16[2304,256]{1,0:T(8,128)(2,1)} %get-tuple-element.433) | copy-start | bytes 3538948 | tf_op jit(solution)/shard_map/while
  176.0 11.5 %copy-start.63 = (bf16[16,9,1,1]{1,0,2,3:T(8,128)(2,1)S(1)}, bf16[16,9,1,1]{1,0,2,3:T(8,128)(2,1)}, u32[]{:S(2)}) copy-start(bf16[16,9,1,1]{1,0,2,3:T(8,128)(2,1)} %get-tuple-element.222) | copy-start | bytes 868
  180.3 11.0 %collective-permute-start.5 = (bf16[16,2,9,256]{3,0,2,1:T(8,128)(2,1)S(1)}, bf16[16,2,9,256]{3,0,2,1:T(8,128)(2,1)S(1)}, u32[]{:S(2)}, u32[]{:S(2)}) collective-permute-start(bf16[16,2,9,256]{3,0,2,1:T(8,128)(2,1)S(1)} %get-tuple-element.195), channel_id=1, source_target_pairs={{0,1},{1,2},{2,3},{3,4},{4,5},{5,6},{6,7},{7,8},{8,9},{9,10},{10,1... | collective-permute-start | bytes 442376 | tf_op jit(solution)/shard_map/ppermute | solution.py:19
  180.3 10.9 %collective-permute-start.6 = (bf16[16,2,9,256]{3,0,2,1:T(8,128)(2,1)S(1)}, bf16[16,2,9,256]{3,0,2,1:T(8,128)(2,1)S(1)}, u32[]{:S(2)}, u32[]{:S(2)}) collective-permute-start(bf16[16,2,9,256]{3,0,2,1:T(8,128)(2,1)S(1)} %get-tuple-element.196), channel_id=1, source_target_pairs={{1,0},{2,1},{3,2},{4,3},{5,4},{6,5},{7,6},{8,7},{9,8},{10,9},{11,1... | collective-permute-start | bytes 442376 | tf_op jit(solution)/shard_map/ppermute | solution.py:20
  191.8 16.7 %collective-permute-start.9 = (bf16[2,36,9,256]{3,0,2,1:T(2,128)(2,1)S(1)}, bf16[2,36,9,256]{3,0,2,1:T(2,128)(2,1)S(1)}, u32[]{:S(2)}, u32[]{:S(2)}) collective-permute-start(bf16[2,36,9,256]{3,0,2,1:T(2,128)(2,1)S(1)} %get-tuple-element.187), channel_id=1, source_target_pairs={{0,32},{32,64},{64,96},{1,33},{33,65},{65,97},{2,34},{34,66},{66,9... | collective-permute-start | bytes 995336 | tf_op jit(solution)/shard_map/ppermute | solution.py:19
  194.2 4.3 %copy-start.62 = (bf16[16,9,1,1]{1,0,2,3:T(8,128)(2,1)S(1)}, bf16[16,9,1,1]{1,0,2,3:T(8,128)(2,1)}, u32[]{:S(2)}) copy-start(bf16[16,9,1,1]{1,0,2,3:T(8,128)(2,1)} %get-tuple-element.224) | copy-start | bytes 868
  194.2 14.3 %collective-permute-start.7 = (bf16[2,36,9,256]{3,0,2,1:T(2,128)(2,1)S(1)}, bf16[2,36,9,256]{3,0,2,1:T(2,128)(2,1)S(1)}, u32[]{:S(2)}, u32[]{:S(2)}) collective-permute-start(bf16[2,36,9,256]{3,0,2,1:T(2,128)(2,1)S(1)} %get-tuple-element.188), channel_id=1, source_target_pairs={{32,0},{64,32},{96,64},{33,1},{65,33},{97,65},{34,2},{66,34},{98,6... | collective-permute-start | bytes 995336 | tf_op jit(solution)/shard_map/ppermute | solution.py:20
  198.5 5.0 %copy-start.57 = (bf16[16,9,1,1]{1,0,2,3:T(8,128)(2,1)S(1)}, bf16[16,9,1,1]{1,0,2,3:T(8,128)(2,1)}, u32[]{:S(2)}) copy-start(bf16[16,9,1,1]{1,0,2,3:T(8,128)(2,1)} %get-tuple-element.219) | copy-start | bytes 868
  201.0 5.0 %copy-start.60 = (bf16[16,9,1,1]{1,0,2,3:T(8,128)(2,1)S(1)}, bf16[16,9,1,1]{1,0,2,3:T(8,128)(2,1)}, u32[]{:S(2)}) copy-start(bf16[16,9,1,1]{1,0,2,3:T(8,128)(2,1)} %get-tuple-element.221) | copy-start | bytes 868
  224.1 9.9 %copy-start.47 = (bf16[16,9,1,1]{1,0,2,3:T(8,128)(2,1)S(1)}, bf16[16,9,1,1]{1,0,2,3:T(8,128)(2,1)}, u32[]{:S(2)}) copy-start(bf16[16,9,1,1]{1,0,2,3:T(8,128)(2,1)} %get-tuple-element.209) | copy-start | bytes 868
  234.0 3.6 %copy-start.24 = (bf16[16,32,9,256]{3,0,2,1:T(8,128)(2,1)S(1)}, bf16[16,32,9,256]{3,0,2,1:T(8,128)(2,1)}, u32[]{:S(2)}) copy-start(bf16[16,32,9,256]{3,0,2,1:T(8,128)(2,1)} %get-tuple-element.175) | copy-start | bytes 7077892
  234.0 3.6 %copy-start.56 = (bf16[16,9,1,1]{1,0,2,3:T(8,128)(2,1)S(1)}, bf16[16,9,1,1]{1,0,2,3:T(8,128)(2,1)}, u32[]{:S(2)}) copy-start(bf16[16,9,1,1]{1,0,2,3:T(8,128)(2,1)} %get-tuple-element.210) | copy-start | bytes 868
  234.0 5.3 %copy-start.23 = (bf16[16,32,9,256]{3,0,2,1:T(8,128)(2,1)S(1)}, bf16[16,32,9,256]{3,0,2,1:T(8,128)(2,1)}, u32[]{:S(2)}) copy-start(bf16[16,32,9,256]{3,0,2,1:T(8,128)(2,1)} %get-tuple-element.176) | copy-start | bytes 7077892
  234.1 5.3 %copy-start.59 = (bf16[16,9,1,1]{1,0,2,3:T(8,128)(2,1)S(1)}, bf16[16,9,1,1]{1,0,2,3:T(8,128)(2,1)}, u32[]{:S(2)}) copy-start(bf16[16,9,1,1]{1,0,2,3:T(8,128)(2,1)} %get-tuple-element.225) | copy-start | bytes 868
  237.6 3.4 %copy-start.22 = (bf16[16,32,9,256]{3,0,2,1:T(8,128)(2,1)S(1)}, bf16[16,32,9,256]{3,0,2,1:T(8,128)(2,1)}, u32[]{:S(2)}) copy-start(bf16[16,32,9,256]{3,0,2,1:T(8,128)(2,1)} %get-tuple-element.177) | copy-start | bytes 7077892
  237.6 3.4 %copy-start.55 = (bf16[16,9,1,1]{1,0,2,3:T(8,128)(2,1)S(1)}, bf16[16,9,1,1]{1,0,2,3:T(8,128)(2,1)}, u32[]{:S(2)}) copy-start(bf16[16,9,1,1]{1,0,2,3:T(8,128)(2,1)} %get-tuple-element.218) | copy-start | bytes 868
  239.4 3.4 %copy-start.21 = (bf16[16,32,9,256]{3,0,2,1:T(8,128)(2,1)S(1)}, bf16[16,32,9,256]{3,0,2,1:T(8,128)(2,1)}, u32[]{:S(2)}) copy-start(bf16[16,32,9,256]{3,0,2,1:T(8,128)(2,1)} %get-tuple-element.178) | copy-start | bytes 7077892
  239.4 3.4 %copy-start.54 = (bf16[16,9,1,1]{1,0,2,3:T(8,128)(2,1)S(1)}, bf16[16,9,1,1]{1,0,2,3:T(8,128)(2,1)}, u32[]{:S(2)}) copy-start(bf16[16,9,1,1]{1,0,2,3:T(8,128)(2,1)} %get-tuple-element.211) | copy-start | bytes 868
  241.1 3.4 %copy-start.20 = (bf16[16,32,9,256]{3,0,2,1:T(8,128)(2,1)S(1)}, bf16[16,32,9,256]{3,0,2,1:T(8,128)(2,1)}, u32[]{:S(2)}) copy-start(bf16[16,32,9,256]{3,0,2,1:T(8,128)(2,1)} %get-tuple-element.179) | copy-start | bytes 7077892
  241.1 3.4 %copy-start.53 = (bf16[16,9,1,1]{1,0,2,3:T(8,128)(2,1)S(1)}, bf16[16,9,1,1]{1,0,2,3:T(8,128)(2,1)}, u32[]{:S(2)}) copy-start(bf16[16,9,1,1]{1,0,2,3:T(8,128)(2,1)} %get-tuple-element.212) | copy-start | bytes 868
  242.8 3.4 %copy-start.19 = (bf16[16,32,9,256]{3,0,2,1:T(8,128)(2,1)S(1)}, bf16[16,32,9,256]{3,0,2,1:T(8,128)(2,1)}, u32[]{:S(2)}) copy-start(bf16[16,32,9,256]{3,0,2,1:T(8,128)(2,1)} %get-tuple-element.180) | copy-start | bytes 7077892
  244.5 3.6 %copy-start.18 = (bf16[16,32,9,256]{3,0,2,1:T(8,128)(2,1)S(1)}, bf16[16,32,9,256]{3,0,2,1:T(8,128)(2,1)}, u32[]{:S(2)}) copy-start(bf16[16,32,9,256]{3,0,2,1:T(8,128)(2,1)} %get-tuple-element.181) | copy-start | bytes 7077892
  244.5 3.6 %copy-start.51 = (bf16[16,9,1,1]{1,0,2,3:T(8,128)(2,1)S(1)}, bf16[16,9,1,1]{1,0,2,3:T(8,128)(2,1)}, u32[]{:S(2)}) copy-start(bf16[16,9,1,1]{1,0,2,3:T(8,128)(2,1)} %get-tuple-element.214) | copy-start | bytes 868
  246.2 3.6 %copy-start.17 = (bf16[16,32,9,256]{3,0,2,1:T(8,128)(2,1)S(1)}, bf16[16,32,9,256]{3,0,2,1:T(8,128)(2,1)}, u32[]{:S(2)}) copy-start(bf16[16,32,9,256]{3,0,2,1:T(8,128)(2,1)} %get-tuple-element.182) | copy-start | bytes 7077892
  246.2 3.6 %copy-start.50 = (bf16[16,9,1,1]{1,0,2,3:T(8,128)(2,1)S(1)}, bf16[16,9,1,1]{1,0,2,3:T(8,128)(2,1)}, u32[]{:S(2)}) copy-start(bf16[16,9,1,1]{1,0,2,3:T(8,128)(2,1)} %get-tuple-element.215) | copy-start | bytes 868
  248.1 3.4 %copy-start.16 = (bf16[16,32,9,256]{3,0,2,1:T(8,128)(2,1)S(1)}, bf16[16,32,9,256]{3,0,2,1:T(8,128)(2,1)}, u32[]{:S(2)}) copy-start(bf16[16,32,9,256]{3,0,2,1:T(8,128)(2,1)} %get-tuple-element.183) | copy-start | bytes 7077892
  249.9 3.4 %copy-start.14 = (bf16[16,32,9,256]{3,0,2,1:T(8,128)(2,1)S(1)}, bf16[16,32,9,256]{3,0,2,1:T(8,128)(2,1)}, u32[]{:S(2)}) copy-start(bf16[16,32,9,256]{3,0,2,1:T(8,128)(2,1)} %get-tuple-element.184) | copy-start | bytes 7077892
  249.9 3.4 %copy-start.48 = (bf16[16,9,1,1]{1,0,2,3:T(8,128)(2,1)S(1)}, bf16[16,9,1,1]{1,0,2,3:T(8,128)(2,1)}, u32[]{:S(2)}) copy-start(bf16[16,9,1,1]{1,0,2,3:T(8,128)(2,1)} %get-tuple-element.217) | copy-start | bytes 868
  251.6 3.4 %copy-start.15 = (bf16[16,32,9,256]{3,0,2,1:T(8,128)(2,1)S(1)}, bf16[16,32,9,256]{3,0,2,1:T(8,128)(2,1)}, u32[]{:S(2)}) copy-start(bf16[16,32,9,256]{3,0,2,1:T(8,128)(2,1)} %get-tuple-element.165) | copy-start | bytes 7077892
  251.6 3.4 %copy-start.46 = (bf16[16,9,1,1]{1,0,2,3:T(8,128)(2,1)S(1)}, bf16[16,9,1,1]{1,0,2,3:T(8,128)(2,1)}, u32[]{:S(2)}) copy-start(bf16[16,9,1,1]{1,0,2,3:T(8,128)(2,1)} %get-tuple-element.201) | copy-start | bytes 868
  253.3 3.4 %copy-start.13 = (bf16[16,32,9,256]{3,0,2,1:T(8,128)(2,1)S(1)}, bf16[16,32,9,256]{3,0,2,1:T(8,128)(2,1)}, u32[]{:S(2)}) copy-start(bf16[16,32,9,256]{3,0,2,1:T(8,128)(2,1)} %get-tuple-element.166) | copy-start | bytes 7077892
  253.3 3.4 %copy-start.58 = (bf16[16,9,1,1]{1,0,2,3:T(8,128)(2,1)S(1)}, bf16[16,9,1,1]{1,0,2,3:T(8,128)(2,1)}, u32[]{:S(2)}) copy-start(bf16[16,9,1,1]{1,0,2,3:T(8,128)(2,1)} %get-tuple-element.220) | copy-start | bytes 868
  255.0 3.4 %copy-start.12 = (bf16[16,32,9,256]{3,0,2,1:T(8,128)(2,1)S(1)}, bf16[16,32,9,256]{3,0,2,1:T(8,128)(2,1)}, u32[]{:S(2)}) copy-start(bf16[16,32,9,256]{3,0,2,1:T(8,128)(2,1)} %get-tuple-element.167) | copy-start | bytes 7077892
  256.7 3.6 %copy-start.11 = (bf16[16,32,9,256]{3,0,2,1:T(8,128)(2,1)S(1)}, bf16[16,32,9,256]{3,0,2,1:T(8,128)(2,1)}, u32[]{:S(2)}) copy-start(bf16[16,32,9,256]{3,0,2,1:T(8,128)(2,1)} %get-tuple-element.168) | copy-start | bytes 7077892
  256.8 3.6 %copy-start.44 = (bf16[16,9,1,1]{1,0,2,3:T(8,128)(2,1)S(1)}, bf16[16,9,1,1]{1,0,2,3:T(8,128)(2,1)}, u32[]{:S(2)}) copy-start(bf16[16,9,1,1]{1,0,2,3:T(8,128)(2,1)} %get-tuple-element.203) | copy-start | bytes 868
  258.5 3.6 %copy-start.43 = (bf16[16,9,1,1]{1,0,2,3:T(8,128)(2,1)S(1)}, bf16[16,9,1,1]{1,0,2,3:T(8,128)(2,1)}, u32[]{:S(2)}) copy-start(bf16[16,9,1,1]{1,0,2,3:T(8,128)(2,1)} %get-tuple-element.204) | copy-start | bytes 868
  265.5 3.4 %copy-start.39 = (bf16[16,9,1,1]{1,0,2,3:T(8,128)(2,1)S(1)}, bf16[16,9,1,1]{1,0,2,3:T(8,128)(2,1)}, u32[]{:S(2)}) copy-start(bf16[16,9,1,1]{1,0,2,3:T(8,128)(2,1)} %get-tuple-element.208) | copy-start | bytes 868
  267.2 3.4 %copy-start.25 = (f32[16,1,32,256]{3,1,2,0:T(1,128)S(1)}, f32[16,1,32,256]{3,1,2,0:T(1,128)}, u32[]{:S(2)}) copy-start(f32[16,1,32,256]{3,1,2,0:T(1,128)} %fusion.65) | copy-start | bytes 1572868
  267.2 3.4 %copy-start.26 = (f32[16,1,32,256]{3,1,2,0:T(1,128)S(1)}, f32[16,1,32,256]{3,1,2,0:T(1,128)}, u32[]{:S(2)}) copy-start(f32[16,1,32,256]{3,1,2,0:T(1,128)} %fusion.28) | copy-start | bytes 1572868
  267.2 3.4 %copy-start.27 = (f32[16,1,32,256]{3,1,2,0:T(1,128)S(1)}, f32[16,1,32,256]{3,1,2,0:T(1,128)}, u32[]{:S(2)}) copy-start(f32[16,1,32,256]{3,1,2,0:T(1,128)} %fusion.26) | copy-start | bytes 1572868
  (51 other events, 118.0 us)
Sparse Core Ops, SparseCore 0:
  176.2 148.3 all-reduce.1
where the time goes:
time: 338 us; the launch traced here: 335 us
  local copies, waits for them, and re-layouts  89.3 us (26%)
  other arithmetic  61.2 us (18%)
  matrix products  57.6 us (17%)
  waiting for transfers between devices  53.6 us (16%)
  starting transfers between devices  31.1 us (9%)
  loops' own time  27 us (8%)
  between operations  15 us (4%)
    psum x1, waiting for transfers between devices, shards(): summed = lax.psum(grad_total, ('lat', 'lon'))  52 us
    dot_general x25, matrix products, shards(): jnp.einsum('jk,jlkc->jlc', taps_pad[row_offset:row_offset + lat_rows, :,...  49.6 us
    while x110, local copies, waits for them, and re-layouts  46.9 us
    another operation x1, loops' own time, shards(): lax.scan(row_step, jnp.zeros((basis_count * channels, channels), jnp.floa...  27 us
    ppermute x5, starting transfers between devices, with_halo(): after = lax.ppermute(initial, axis, down)  21.5 us
    slice x2, local copies, waits for them, and re-layouts, shards(): grad_pad[row_offset:row_offset + lat_rows, col_offset:col_offset + lon_ce...  20.6 us
    convert_element_type x2, other arithmetic, row_step(): basis_out = basis_acc.astype(jnp.bfloat16)  20.5 us
    mul x18, other arithmetic, row_step(): taps_block[:, None, :, tap_index, None] * shifted[:, :, None, :]  10.8 us
  transfers between devices with their start and end apart: 11, of which 2 were waited for; matrix products, arithmetic and copies ran while one was open for 28% of the time, Pallas kernels for 0%

commit v1 on v0

v1 whole, which is shorter than its diff:
```python
import functools
import math

import jax
import numpy as np
import jax.numpy as jnp
from jax import lax
from jax.experimental import pallas as pl
from jax.experimental.pallas import tpu as pltpu
from jax.sharding import Mesh, PartitionSpec as P

AXES = ("xl", "core", "y", "xh", "z")
SIZES = (2, 2, 4, 2, 4)
RING = ("xl", "y", "xh", "z")

ROWS = 16
CELLS = 32
SLOTS = 48
BASIS = 9
CHAN = 256
HALF = 128
BAND = 5
KEEP = 40
bf16 = jnp.bfloat16
f32 = jnp.float32


def moves(lat=False, core=False, lon=0):
    pairs = []
    for xl in range(2):
        for c in range(2):
            for cell in range(32):
                source = (xl * 2 + c) * 32 + cell
                row = (xl ^ int(lat)) * 2 + (c ^ int(core))
                pairs.append((source, row * 32 + (cell + lon) % 32))
    return pairs


def send(x, **way):
    return lax.ppermute(x, AXES, moves(**way))


def vmem(count):
    return [pl.BlockSpec(memory_space=pltpu.VMEM)] * count


SMEM = pl.BlockSpec(memory_space=pltpu.SMEM)


def call(kernel, outs, operands, scratch=(), place=None, flops=0, traffic=0, limit=40):
    shapes = [jax.ShapeDtypeStruct(*o) for o in outs]
    specs = vmem(len(operands))
    args = tuple(operands)
    if place is not None:
        specs = [SMEM] + specs
        args = (place,) + args
    return pl.pallas_call(
        kernel,
        out_shape=shapes,
        in_specs=specs,
        out_specs=vmem(len(outs)),
        scratch_shapes=list(scratch),
        compiler_params=pltpu.CompilerParams(vmem_limit_bytes=limit * 1024 * 1024),
        cost_estimate=pl.CostEstimate(flops=flops, bytes_accessed=traffic, transcendentals=0),
    )(*args)


def edge_kernel(place, fo, fx, co, cx, right, left, rows, corner_r, corner_l):
    xl, core = place[0], place[1]
    for f, (own, other) in enumerate(((fo, fx), (co, cx))):
        for part, ref in enumerate((own, other)):
            span = slice(part * ROWS, (part + 1) * ROWS)
            right[f, span] = ref[:, CELLS - 2 : CELLS, :]
            left[f, span] = ref[:, 0:2, :]
            for side in range(2):
                holder = 1 - side

                @pl.when((xl == side) & (core == (holder if part == 0 else 1 - holder)))
                def _():
                    first = ROWS - 2 if side == 0 else 0
                    rows[f] = ref[first : first + 2]
                    corner_r[f] = ref[first : first + 2, CELLS - 2 : CELLS, :]
                    corner_l[f] = ref[first : first + 2, 0:2, :]


def padded(dst, f, xl, core, own, other, right, left, rows, corner_r, corner_l, lanes):
    width = dst.shape[-1]
    dst[:, CELLS:SLOTS, :] = jnp.zeros((36, SLOTS - CELLS, width), bf16)
    for part, ref in enumerate((own, other)):
        at = pl.ds(2 + ROWS * (core if part == 0 else 1 - core), ROWS)
        span = slice(part * ROWS, (part + 1) * ROWS)
        dst[at, 0:CELLS, :] = ref[:, :, lanes]
        dst[at, CELLS : CELLS + 2, :] = right[f, span, :, lanes]
        dst[at, CELLS + 2 : CELLS + 4, :] = left[f, span, :, lanes]
    edge = pl.ds(34 * (1 - xl), 2)
    dst[edge, 0:CELLS, :] = rows[f, :, :, lanes]
    dst[edge, CELLS : CELLS + 2, :] = corner_r[f, :, :, lanes]
    dst[edge, CELLS + 2 : CELLS + 4, :] = corner_l[f, :, :, lanes]
    dst[pl.ds(34 * xl, 2)] = jnp.zeros((2, SLOTS, width), bf16)


def band_masks(lanes):
    cell = lax.broadcasted_iota(jnp.int32, (CELLS, lanes), 0)
    slot = lax.broadcasted_iota(jnp.int32, (CELLS, lanes), 1) % SLOTS
    place = jnp.where(slot < CELLS + 2, slot, jnp.where(slot < CELLS + 4, slot - 36, 1000))
    return [(place - cell + 2) == s for s in range(BAND)]


def spread(inner, lanes):
    table = np.zeros((inner, BAND, BAND, lanes), np.float32)
    for o in range(inner):
        for s in range(BAND):
            table[o, s, s, o * SLOTS : (o + 1) * SLOTS] = 1.0
    return jnp.asarray(table.reshape(inner * BAND, BAND * lanes), bf16)


def band(block, masks, lanes, row):
    total = jnp.zeros((CELLS, lanes), f32)
    for s in range(BAND):
        line = block[pl.ds(row, 1), s * lanes : (s + 1) * lanes]
        total = jnp.where(masks[s], jnp.broadcast_to(line, (CELLS, lanes)), total)
    return total.astype(bf16)


def forward_band_kernel(taps, table, co, cx, bands, cot_t, lines):
    lines[...] = jnp.dot(taps[...], table[...], preferred_element_type=f32)
    masks = band_masks(CHAN)

    def row(n, carry):
        for k in range(BASIS):
            bands[n, k * CELLS : (k + 1) * CELLS, :] = band(lines, masks, CHAN, n * 16 + k)
        return carry

    lax.fori_loop(0, 2 * ROWS, row, 0)
    cot_t[:, 0:512] = co[...].reshape(512, CHAN).T
    cot_t[:, 512:1024] = cx[...].reshape(512, CHAN).T


def weight_kernel(
    place, fo, fx, right, left, rows, corner_r, corner_l, bands, cot_t, parts, field, basis
):
    xl, core = place[0], place[1]
    lanes = pl.ds(pl.multiple_of(core * HALF, HALF), HALF)
    padded(field, 0, xl, core, fo, fx, right, left, rows, corner_r, corner_l, lanes)

    def row(n, carry):
        first = jnp.where(n < ROWS, core * ROWS + n, (1 - core) * ROWS + n - ROWS)
        window = field[pl.ds(first, BAND)].reshape(BAND * SLOTS, HALF)
        out = jnp.dot(
            bands[n, :, 0 : BAND * SLOTS], window, preferred_element_type=f32
        ).astype(bf16)
        at = pl.ds(pl.multiple_of(n * CELLS, CELLS), CELLS)
        for k in range(BASIS):
            basis[at, k * HALF : (k + 1) * HALF] = out[k * CELLS : (k + 1) * CELLS]
        return carry

    lax.fori_loop(0, 2 * ROWS, row, 0)
    parts[:, 32:KEEP, :] = jnp.zeros((64, 8, HALF), bf16)
    for k in range(BASIS):
        grad = jnp.dot(
            cot_t[...], basis[:, k * HALF : (k + 1) * HALF], preferred_element_type=f32
        ).T
        for side in range(2):
            tiles = grad[:, side * HALF : (side + 1) * HALF].reshape(16, 8, HALF).astype(bf16)
            begin = side * 144 + k * 16
            while_at = 0
            while while_at < 16:
                s, j = divmod(begin + while_at, 64)
                count = min(16 - while_at, 64 - j)
                parts[j : j + count, s * 8 : (s + 1) * 8, :] = tiles[while_at : while_at + count]
                while_at += count


def sum_kernel(scale, parts, out):
    total = jnp.sum(parts[...].astype(f32), axis=0) * scale
    out[...] = jnp.broadcast_to(total.astype(bf16)[None], out.shape)


def place_kernel(place, mine, theirs, out):
    core = place[1]
    for half in range(2):
        for ref, is_mine in ((mine, True), (theirs, False)):

            @pl.when(core == (half if is_mine else 1 - half))
            def _():
                for side in range(2):
                    for k in range(BASIS):
                        begin = side * 144 + k * 16
                        at = 0
                        while at < 16:
                            s, j = divmod(begin + at, 64)
                            count = min(16 - at, 64 - j)
                            tiles = ref[j : j + count, s * 8 : (s + 1) * 8, :].astype(f32)
                            first = half * HALF + at * 8
                            out[
                                k, first : first + count * 8, side * HALF : (side + 1) * HALF
                            ] = tiles.reshape(count * 8, HALF)
                            at += count


def mixed_kernel(
    place, fo, fx, right, left, rows, corner_r, corner_l, bands, weight, out, field, basis
):
    xl, core = place[0], place[1]
    padded(field, 0, xl, core, fo, fx, right, left, rows, corner_r, corner_l, slice(None))

    def row(n, carry):
        window = field[pl.ds(core * ROWS + n, BAND)].reshape(BAND * SLOTS, CHAN)
        part = jnp.dot(
            bands[n, :, 0 : BAND * SLOTS], window, preferred_element_type=f32
        ).astype(bf16)
        at = pl.ds(pl.multiple_of(n * CELLS, CELLS), CELLS)
        for k in range(BASIS):
            basis[at, k * CHAN : (k + 1) * CHAN] = part[k * CELLS : (k + 1) * CELLS]
        return carry

    lax.fori_loop(0, ROWS, row, 0)
    out[...] = (
        jnp.dot(basis[...], weight[...], preferred_element_type=f32)
        .astype(bf16)
        .reshape(ROWS, CELLS, CHAN)
    )


def feature_kernel(
    place,
    co,
    cx,
    right,
    left,
    rows,
    corner_r,
    corner_l,
    taps,
    table,
    weight,
    out,
    field,
    lines,
    grads,
    bands,
    total,
):
    xl, core = place[0], place[1]
    lanes = 512
    near = ROWS + 4
    padded(field, 1, xl, core, co, cx, right, left, rows, corner_r, corner_l, slice(None))
    lines[...] = jnp.dot(taps[...], table[...], preferred_element_type=f32)
    masks = band_masks(lanes)
    for k in range(BASIS):
        for h in range(2):
            upstream = field[pl.ds(core * ROWS + h * 10, 10)].reshape(10 * SLOTS, CHAN)
            back = lax.dot_general(
                upstream,
                weight[k * CHAN : (k + 1) * CHAN, :],
                (((1,), (1,)), ((), ())),
                preferred_element_type=f32,
            )
            grads[h * 10 : (h + 1) * 10, k * SLOTS : (k + 1) * SLOTS, :] = back.astype(
                bf16
            ).reshape(10, SLOTS, CHAN)
    total[...] = jnp.zeros_like(total)

    def row(i, carry):
        for b in range(BAND):
            bands[b * CELLS : (b + 1) * CELLS, :] = band(lines, masks, lanes, i * 8 + b)
        part = jnp.dot(
            bands[:, 0 : BASIS * SLOTS], grads[i], preferred_element_type=f32
        ).reshape(BAND, CELLS, CHAN)
        total[pl.ds(i, BAND)] += part
        return carry

    lax.fori_loop(0, near, row, 0)
    out[...] = total[4 : 4 + ROWS].astype(bf16)


def shards(feature, filters, start, length, weight, cotangent):
    xl, core = lax.axis_index("xl"), lax.axis_index("core")
    place = jnp.stack([xl, core]).astype(jnp.int32)
    lat = xl * 2 + core

    source = (
        lat * ROWS
        + jnp.arange(ROWS, dtype=jnp.int32)[:, None]
        - 2
        + jnp.arange(BAND, dtype=jnp.int32)[None, :]
    )
    inside = (source >= start[:, None]) & (source < (start + length)[:, None])
    masked = filters.reshape(ROWS, BASIS, BAND, BAND) * inside.astype(bf16)[:, None, :, None]

    f_other = send(feature, core=True)
    c_other = send(cotangent, core=True)
    m_other = send(masked, core=True)

    edge = [
        ((2, 32, 2, CHAN), bf16),
        ((2, 32, 2, CHAN), bf16),
        ((2, 2, CELLS, CHAN), bf16),
        ((2, 2, 2, CHAN), bf16),
        ((2, 2, 2, CHAN), bf16),
    ]
    to_right, to_left, rows, corner_r, corner_l = call(
        edge_kernel, edge, (feature, f_other, cotangent, c_other), place=place, traffic=2**20
    )
    left = send(to_right, lon=1)
    right = send(to_left, lon=-1)
    rows = send(rows, lat=True)
    corner_l, corner_r = (
        send(corner_r, lat=True, lon=1),
        send(corner_l, lat=True, lon=-1),
    )
    halo = (right, left, rows, corner_r, corner_l)

    both = jnp.concatenate([masked, m_other], 0)
    flat = jnp.pad(both.reshape(32, BASIS, 25), ((0, 0), (0, 7), (0, 0))).reshape(512, 25)
    bands, cot_t = call(
        forward_band_kernel,
        [((32, BASIS * CELLS, CHAN), bf16), ((CHAN, 1024), bf16)],
        (flat, spread(BAND, CHAN), cotangent, c_other),
        scratch=[pltpu.VMEM((512, BAND * CHAN), f32)],
        flops=2 * 512 * 32 * 1280,
        traffic=6 * 2**20,
    )
    (parts,) = call(
        weight_kernel,
        [((64, KEEP, HALF), bf16)],
        (feature, f_other, *halo, bands, cot_t),
        scratch=[
            pltpu.VMEM((36, SLOTS, HALF), bf16),
            pltpu.VMEM((1024, BASIS * HALF), bf16),
        ],
        place=place,
        flops=2 * 32 * 288 * 256 * 256 + 2 * 1024 * 1152 * 256,
        traffic=7 * 2**20,
    )
    swapped = lax.all_to_all(parts, RING, 0, 0, tiled=True)
    (shared,) = call(
        functools.partial(sum_kernel, 1.0 / math.sqrt(64 * 1024)),
        [((64, KEEP, HALF), bf16)],
        (swapped,),
        traffic=2**20,
    )
    mine = lax.all_to_all(shared, RING, 0, 0, tiled=True)
    theirs = send(mine, core=True)
    (grad_weight,) = call(
        place_kernel, [((BASIS, CHAN, CHAN), f32)], (mine, theirs), place=place, traffic=4 * 2**20
    )

    mixing = weight.reshape(BASIS * CHAN, CHAN)
    (mixed,) = call(
        mixed_kernel,
        [((ROWS, CELLS, CHAN), bf16)],
        (feature, f_other, *halo, bands, mixing),
        scratch=[
            pltpu.VMEM((36, SLOTS, CHAN), bf16),
            pltpu.VMEM((512, BASIS * CHAN), bf16),
        ],
        place=place,
        flops=2 * 16 * 288 * 256 * 256 + 2 * 512 * 2304 * 256,
        traffic=8 * 2**20,
    )

    lowest = jnp.where(core == 0, masked, m_other)
    highest = jnp.where(core == 0, m_other, masked)
    beyond = send(jnp.where(xl == 0, highest[ROWS - 2 :], lowest[:2]), lat=True)
    none = jnp.zeros_like(beyond)
    chip = jnp.concatenate(
        [
            jnp.where(xl == 0, none, beyond),
            lowest,
            highest,
            jnp.where(xl == 0, beyond, none),
        ],
        0,
    )
    near = lax.dynamic_slice_in_dim(chip, core * ROWS, ROWS + 4, 0)[..., ::-1]
    near = jnp.pad(near.transpose(0, 2, 1, 3), ((0, 0), (0, 3), (0, 0), (0, 0)))
    (grad_feature,) = call(
        feature_kernel,
        [((ROWS, CELLS, CHAN), bf16)],
        (
            cotangent,
            c_other,
            *halo,
            near.reshape((ROWS + 4) * 8, BASIS * BAND),
            spread(BASIS, 512),
            mixing,
        ),
        scratch=[
            pltpu.VMEM((36, SLOTS, CHAN), bf16),
            pltpu.VMEM(((ROWS + 4) * 8, BAND * 512), f32),
            pltpu.VMEM((ROWS + 4, BASIS * SLOTS, CHAN), bf16),
            pltpu.VMEM((BAND * CELLS, 512), bf16),
            pltpu.VMEM((ROWS + 8, CELLS, CHAN), f32),
        ],
        place=place,
        flops=2 * 960 * 2304 * 256 + 2 * 20 * 160 * 512 * 256,
        traffic=8 * 2**20,
    )
    return (mixed, grad_feature, grad_weight)


def solution(mesh):
    fine = Mesh(mesh.devices.reshape(SIZES), AXES)
    lat, lon = ("xl", "core"), ("y", "xh", "z")
    return jax.shard_map(
        shards,
        mesh=fine,
        in_specs=(P(lat, lon, None), P(lat, None, None), P(lat), P(lat), P(), P(lat, lon, None)),
        out_specs=(P(lat, lon, None), P(lat, lon, None), P()),
        check_vma=False,
    )
```

time: 338 us -> 116 us (0.34)
  local copies, waits for them, and re-layouts: 89.3 us -> 13.7 us
  matrix products: 57.6 us -> 0 us
  other arithmetic: 61.2 us -> 6.78 us
  waiting for transfers between devices: 53.6 us -> 18.2 us
  Pallas kernels: 0 us -> 28.6 us
  loops' own time: 27 us -> 0 us
  blocking collectives: 0 us -> 17.3 us
  between operations: 15 us -> 0.84 us
    dot_general x31 -> x0, matrix products: 57.6 us -> none  [the longest x25 49.6 us: shards(): jnp.einsum('jk,jlkc->jlc', taps_pad[row_offset:row_offset + lat_rows, :,...]
    psum x1 -> x0, waiting for transfers between devices: 52 us -> none  [shards(): summed = lax.psum(grad_total, ('lat', 'lon'))]
    while x111 -> x0, local copies, waits for them, and re-layouts: 51.1 us -> none
    convert_element_type x8 -> x1, other arithmetic: 31.8 us -> 0.66 us  [shards(): inside.astype(bf16)[:, None, :, None]]
    pallas_call x0 -> x7, Pallas kernels: none -> 28.6 us  [call(): pl.pallas_call(kernel, out_shape=shapes, in_specs=specs, out_specs=vmem(l...]
    another operation x1 -> x0, loops' own time: 27 us -> none  [shards(): lax.scan(row_step, jnp.zeros((basis_count * channels, channels), jnp.floa...]
    slice x7 -> x0, local copies, waits for them, and re-layouts: 22.2 us -> none  [the longest x2 20.6 us: shards(): grad_pad[row_offset:row_offset + lat_rows, col_offset:col_offset + lon_ce...]
    all_to_all x0 -> x1, blocking collectives: none -> 17.3 us  [shards(): swapped = lax.all_to_all(parts, RING, 0, 0, tiled=True)]
  transfers between devices with their start and end apart: 11 -> 11, of which waited for: 2 -> 3; matrix products, arithmetic and copies ran while one was open for 28% -> 13% of each run, Pallas kernels for 0% -> 15%
where the time goes in v1:
time: 116 us; the launch traced here: 115 us
  starting transfers between devices  29.6 us (26%)
  Pallas kernels  28.6 us (25%)
  waiting for transfers between devices  18.2 us (16%)
  blocking collectives  17.3 us (15%)
  local copies, waits for them, and re-layouts  13.7 us (12%)
  other arithmetic  6.78 us (6%)
    pallas_call x7, Pallas kernels, call(): pl.pallas_call(kernel, out_shape=shapes, in_specs=specs, out_specs=vmem(l...  28.6 us
    ppermute x10, starting transfers between devices, send(): return lax.ppermute(x, AXES, moves(**way))  22.7 us
    all_to_all x1, blocking collectives, shards(): swapped = lax.all_to_all(parts, RING, 0, 0, tiled=True)  17.3 us
    all_to_all x1, waiting for transfers between devices, shards(): mine = lax.all_to_all(shared, RING, 0, 0, tiled=True)  10.6 us
    unnamed x31, local copies, waits for them, and re-layouts  8.95 us
    ppermute x10, waiting for transfers between devices, send(): return lax.ppermute(x, AXES, moves(**way))  7.58 us
    all_to_all x1, starting transfers between devices, shards(): mine = lax.all_to_all(shared, RING, 0, 0, tiled=True)  6.87 us
  transfers between devices with their start and end apart: 11, of which 3 were waited for; matrix products, arithmetic and copies ran while one was open for 13% of the time, Pallas kernels for 15%

profile of v1, /device:TPU:1, one launch (start us, length us, event | category | flops | bytes accessed | tf_op | source)
XLA Modules:
  0.0 115.0 jit_solution(6902051235695083465)
XLA Ops:
  0.6 0.0 copy-start.8
  0.6 0.0 copy-start.4
  0.7 1.5 %collective-permute-start = (bf16[16,32,256]{2,1,0:T(8,128)(2,1)}, bf16[16,32,256]{2,1,0:T(8,128)(2,1)S(1)}, u32[]{:S(2)}, u32[]{:S(2)}) collective-permute-start(bf16[16,32,256]{2,1,0:T(8,128)(2,1)} %fo.5), channel_id=1, source_target_pairs={{0,32},{1,33},{2,34},{3,35},{4,36},{5,37},{6,38},{7,39},{8,40},{9,... | collective-permute-start | bytes 786440 | tf_op jit(solution)/shard_map/ppermute | solution.py:40
  2.2 0.1 collective-permute-start.1
  2.3 0.9 copy.12
  3.2 0.1 reshape.80
  3.2 0.0 copy-start.10
  3.2 0.7 add.53
  3.9 0.7 fusion.3
  4.6 0.5 collective-permute-start.7
  5.1 0.1 pad_add_fusion.place
  5.2 0.0 collective-permute-done.1.cx
  5.2 0.0 copy-start.3
  5.2 0.9 copy-done.3
  6.2 0.9 copy-done.5
  7.1 0.7 shard_map.103
  7.8 8.8 %collective-permute-start.2 = (bf16[2,32,2,256]{3,2,1,0:T(2,128)(2,1)S(1)}, bf16[2,32,2,256]{3,2,1,0:T(2,128)(2,1)S(1)}, u32[]{:S(2)}, u32[]{:S(2)}) collective-permute-start(bf16[2,32,2,256]{3,2,1,0:T(2,128)(2,1)S(1)} %get-tuple-element.10), channel_id=1, source_target_pairs={{0,31},{1,0},{2,1},{3,2},{4,3},{5,4},{6,5},{7,6},{8,7},{9,8},{10,9... | collective-permute-start | bytes 196616 | tf_op jit(solution)/shard_map/ppermute | solution.py:40
  16.6 0.3 collective-permute-start.4
  17.0 0.6 copy-done.12
  17.6 0.1 pad_maximum_fusion
  17.7 0.2 copy.16
  18.0 7.2 %collective-permute-start.5 = (bf16[2,2,2,256]{3,2,1,0:T(2,128)(2,1)S(1)}, bf16[2,2,2,256]{3,2,1,0:T(2,128)(2,1)S(1)}, u32[]{:S(2)}, u32[]{:S(2)}) collective-permute-start(bf16[2,2,2,256]{3,2,1,0:T(2,128)(2,1)S(1)} %get-tuple-element.13), channel_id=1, source_target_pairs={{0,95},{1,64},{2,65},{3,66},{4,67},{5,68},{6,69},{7,70},{8,71},{9,... | collective-permute-start | bytes 12296 | tf_op jit(solution)/shard_map/ppermute | solution.py:40
  25.2 0.9 copy-done.6
  26.2 3.5 %shard_map.104 = (bf16[32,288,256]{2,1,0:T(8,128)(2,1)S(1)}, bf16[256,1024]{1,0:T(8,128)(2,1)S(1)}) custom-call(bf16[512,25]{1,0:T(8,128)(2,1)S(1)} %bitcast.13, bf16[25,1280]{1,0:T(8,128)(2,1)S(1)} %copy-done.8, bf16[16,32,256]{2,1,0:T(8,128)(2,1)S(1)} %copy-done.6, bf16[16,32,256]{2,1,0:T(8,128)(2,1)S(1)} %collective-permute-done.1.cx), custom_call_target="tpu_custom_call" | custom-call | flops 41943040 | bytes 6291456 | tf_op jit(solution)/shard_map/pallas_call | solution.py:57
  29.7 3.4 %collective-permute-done.6.corner_l = bf16[2,2,2,256]{3,2,1,0:T(2,128)(2,1)S(1)} collective-permute-done((bf16[2,2,2,256]{3,2,1,0:T(2,128)(2,1)S(1)}, bf16[2,2,2,256]{3,2,1,0:T(2,128)(2,1)S(1)}, u32[]{:S(2)}, u32[]{:S(2)}) %collective-permute-start.6) | collective-permute-done | bytes 4128 | tf_op jit(solution)/shard_map/ppermute | solution.py:40
  33.1 8.3 %shard_map.107 = bf16[64,40,128]{2,1,0:T(8,128)(2,1)S(1)} custom-call(s32[2]{0:T(128)S(1)} %pad_add_fusion.place, bf16[16,32,256]{2,1,0:T(8,128)(2,1)S(1)} %copy-done.4, bf16[16,32,256]{2,1,0:T(8,128)(2,1)S(1)} %collective-permute-done.fx, bf16[2,32,2,256]{3,2,1,0:T(2,128)(2,1)S(1)} %collective-permute-done.2.right, ...), custom_call_target="tpu_custom_call" | custom-call | flops 1811939328 | bytes 7340032 | tf_op jit(solution)/shard_map/pallas_call | solution.py:57
  41.4 0.0 copy-start.11
  41.5 0.0 copy-start.13
  41.5 17.3 %all_to_all.10.parts = bf16[64,40,128]{2,1,0:T(8,128)(2,1)S(1)} all-to-all(bf16[64,40,128]{2,1,0:T(8,128)(2,1)S(1)} %shard_map.107), channel_id=1, replica_groups=mesh['xl'=2,'core'=2,'y'=4,'xh'=2,'z'=4] {'xl','y','xh','z'}, dimensions={0} | all-to-all | bytes 1310720 | tf_op jit(solution)/shard_map/all_to_all | solution.py:336
  58.8 1.0 shard_map.108
  59.7 6.9 %all-to-all-start.1 = ((bf16[64,40,128]{2,1,0:T(8,128)(2,1)}), bf16[64,40,128]{2,1,0:T(8,128)(2,1)S(1)}, u32[]{:S(2)}, u32[]{:S(2)}) async-start(bf16[64,40,128]{2,1,0:T(8,128)(2,1)} %shard_map.108), calls=%async_computation.1 | async-start | bytes 1310720 | tf_op jit(solution)/shard_map/all_to_all | solution.py:343
  66.6 0.7 broadcast_select_fusion.1
  67.4 10.6 %all-to-all-done.1.mine = bf16[64,40,128]{2,1,0:T(8,128)(2,1)S(1)} async-done(((bf16[64,40,128]{2,1,0:T(8,128)(2,1)}), bf16[64,40,128]{2,1,0:T(8,128)(2,1)S(1)}, u32[]{:S(2)}, u32[]{:S(2)}) %all-to-all-start.1) | async-done | bytes 655392 | tf_op jit(solution)/shard_map/all_to_all | solution.py:343
  78.0 3.8 %collective-permute-start.9 = (bf16[64,40,128]{2,1,0:T(8,128)(2,1)S(1)}, bf16[64,40,128]{2,1,0:T(8,128)(2,1)S(1)}, u32[]{:S(2)}, u32[]{:S(2)}) collective-permute-start(bf16[64,40,128]{2,1,0:T(8,128)(2,1)S(1)} %all-to-all-done.1.mine), channel_id=1, source_target_pairs={{0,32},{1,33},{2,34},{3,35},{4,36},{5,37},{6,38},{7,39},{8,40},{9,... | collective-permute-start | bytes 1966088 | tf_op jit(solution)/shard_map/ppermute | solution.py:40
  81.8 1.7 %slice_select_fusion = bf16[2,9,5,5]{0,3,2,1:T(8,128)(2,1)} fusion(bf16[16,9,5,5]{0,3,2,1:T(8,128)(2,1)} %get-tuple-element.18, bf16[16,9,5,5]{0,3,2,1:T(8,128)(2,1)} %get-tuple-element.17, pred[]{:T(512)S(6)} %eq.4), kind=kLoop, calls=%fused_computation.3 | loop fusion | flops 450 | bytes 2701 | tf_op jit(solution)/shard_map/jit(_where)/select_n | solution.py:365
  83.5 0.4 collective-permute-start.8
  83.9 4.2 %collective-permute-done.8 = bf16[2,9,5,5]{0,3,2,1:T(8,128)(2,1)} collective-permute-done((bf16[2,9,5,5]{0,3,2,1:T(8,128)(2,1)}, bf16[2,9,5,5]{0,3,2,1:T(8,128)(2,1)}, u32[]{:S(2)}, u32[]{:S(2)}) %collective-permute-start.8) | collective-permute-done | bytes 932 | tf_op jit(solution)/shard_map/ppermute | solution.py:40
  88.1 0.9 broadcast_select_fusion.3
  89.0 1.9 %dynamic-slice_maximum_fusion = bf16[20,9,5,5]{0,3,2,1:T(8,128)(2,1)} fusion(s32[]{:T(128)S(6)} %select_n.38, bf16[2,9,5,5]{0,3,2,1:T(8,128)(2,1)S(1)} %get-tuple-element.20, bf16[16,9,5,5]{0,3,2,1:T(8,128)(2,1)} %get-tuple-element.17, bf16[16,9,5,5]{0,3,2,1:T(8,128)(2,1)} %get-tuple-element.18, bf16[2,9,5,5]{0,3,2,1:T(8,128)(2,1)S(1)} %get-tuple-element.19), kind=kLoop, calls=%fused_computation | loop fusion | flops 36000 | bytes 25204 | tf_op jit(solution)/shard_map/concatenate | solution.py:367
  90.9 1.6 %rev.3 = bf16[20,9,5,5]{0,3,2,1:T(8,128)(2,1)} reverse(bf16[20,9,5,5]{0,3,2,1:T(8,128)(2,1)} %dynamic-slice_maximum_fusion), dimensions={3} | reverse | bytes 18000 | tf_op jit(solution)/shard_map/rev | solution.py:376
  92.5 2.0 %copy.17 = bf16[20,5,9,5]{1,0,3,2:T(8,128)(2,1)} copy(bf16[20,5,9,5]{0,3,1,2:T(8,128)(2,1)} %bitcast.14) | data formatting | bytes 18000
  94.5 1.7 %pad.9.clone = bf16[20,8,9,5]{1,0,3,2:T(8,128)(2,1)} pad(bf16[20,5,9,5]{1,0,3,2:T(8,128)(2,1)} %copy.17, bf16[]{:T(256)} %constant.25.clone.1), padding=0_0x0_3x0_0x0_0 | pad | bytes 23402 | tf_op jit(solution)/shard_map/jit(_pad)/pad | solution.py:377
  96.2 1.2 %reshape.84 = bf16[160,45]{0,1:T(8,128)(2,1)S(1)} reshape(bf16[20,8,9,5]{1,0,3,2:T(8,128)(2,1)} %pad.9.clone) | data formatting | bytes 28800 | tf_op jit(solution)/shard_map/reshape | solution.py:385
  97.4 0.1 copy.15.taps
  97.5 2.3 %copy-done.1 = bf16[32,288,256]{2,1,0:T(8,128)(2,1)S(1)} copy-done((bf16[32,288,256]{2,1,0:T(8,128)(2,1)S(1)}, bf16[32,288,256]{2,1,0:T(8,128)(2,1)}, u32[]{:S(2)}) %copy-start.1) | copy-done | bytes 4718616
  99.9 5.2 %shard_map.105 = bf16[16,32,256]{2,1,0:T(8,128)(2,1)} custom-call(s32[2]{0:T(128)S(1)} %pad_add_fusion.place, bf16[16,32,256]{2,1,0:T(8,128)(2,1)S(1)} %copy-done.4, bf16[16,32,256]{2,1,0:T(8,128)(2,1)S(1)} %collective-permute-done.fx, bf16[2,32,2,256]{3,2,1,0:T(2,128)(2,1)S(1)} %collective-permute-done.2.right, ...), custom_call_target="tpu_custom_call" | custom-call | flops 1207959552 | bytes 8388608 | tf_op jit(solution)/shard_map/pallas_call | solution.py:57
  105.1 7.8 %shard_map.106 = bf16[16,32,256]{2,1,0:T(8,128)(2,1)} custom-call(s32[2]{0:T(128)S(1)} %pad_add_fusion.place, bf16[16,32,256]{2,1,0:T(8,128)(2,1)S(1)} %copy-done.7, bf16[16,32,256]{2,1,0:T(8,128)(2,1)S(1)} %collective-permute-done.1.cx, bf16[2,32,2,256]{3,2,1,0:T(2,128)(2,1)S(1)} %collective-permute-done.2.right, ...), custom_call_target="tpu_custom_call" | custom-call | flops 1971322880 | bytes 8388608 | tf_op jit(solution)/shard_map/pallas_call | solution.py:57
  112.9 2.1 %shard_map.109 = f32[9,256,256]{2,1,0:T(8,128)} custom-call(s32[2]{0:T(128)S(1)} %pad_add_fusion.place, bf16[64,40,128]{2,1,0:T(8,128)(2,1)S(1)} %all-to-all-done.1.mine, bf16[64,40,128]{2,1,0:T(8,128)(2,1)S(1)} %collective-permute-done.9.theirs), custom_call_target="tpu_custom_call" | custom-call | bytes 4194304 | tf_op jit(solution)/shard_map/pallas_call | solution.py:57
  (30 shorter events, 0.2 us)
Async XLA Ops:
  0.6 24.6 %copy-start.8 = (bf16[25,1280]{1,0:T(8,128)(2,1)S(1)}, bf16[25,1280]{1,0:T(8,128)(2,1)}, u32[]{:S(2)}) copy-start(bf16[25,1280]{1,0:T(8,128)(2,1)} %constant.28.clone.table) | copy-start | bytes 192004
  0.6 32.5 %copy-start.4 = (bf16[16,32,256]{2,1,0:T(8,128)(2,1)S(1)}, bf16[16,32,256]{2,1,0:T(8,128)(2,1)}, u32[]{:S(2)}) copy-start(bf16[16,32,256]{2,1,0:T(8,128)(2,1)} %fo.5) | copy-start | bytes 786436
  0.7 4.6 %collective-permute-start = (bf16[16,32,256]{2,1,0:T(8,128)(2,1)}, bf16[16,32,256]{2,1,0:T(8,128)(2,1)S(1)}, u32[]{:S(2)}, u32[]{:S(2)}) collective-permute-start(bf16[16,32,256]{2,1,0:T(8,128)(2,1)} %fo.5), channel_id=1, source_target_pairs={{0,32},{1,33},{2,34},{3,35},{4,36},{5,37},{6,38},{7,39},{8,40},{9,... | collective-permute-start | bytes 786440 | tf_op jit(solution)/shard_map/ppermute | solution.py:40
  2.2 3.1 %collective-permute-start.1 = (bf16[16,32,256]{2,1,0:T(8,128)(2,1)}, bf16[16,32,256]{2,1,0:T(8,128)(2,1)S(1)}, u32[]{:S(2)}, u32[]{:S(2)}) collective-permute-start(bf16[16,32,256]{2,1,0:T(8,128)(2,1)} %co.5), channel_id=1, source_target_pairs={{0,32},{1,33},{2,34},{3,35},{4,36},{5,37},{6,38},{7,39},{8,40},{9,... | collective-permute-start | bytes 786440 | tf_op jit(solution)/shard_map/ppermute | solution.py:40
  3.2 2.0 %copy-start.10 = (bf16[16,9,5,5]{0,3,2,1:T(8,128)(2,1)}, bf16[16,9,5,5]{0,3,2,1:T(8,128)(2,1)S(1)}, u32[]{:S(2)}) copy-start(bf16[16,9,5,5]{0,3,2,1:T(8,128)(2,1)S(1)} %reshape.80) | copy-start | bytes 21604
  4.6 12.3 %collective-permute-start.7 = (bf16[16,9,5,5]{0,3,2,1:T(8,128)(2,1)S(1)}, bf16[16,9,5,5]{0,3,2,1:T(8,128)(2,1)S(1)}, u32[]{:S(2)}, u32[]{:S(2)}) collective-permute-start(bf16[16,9,5,5]{0,3,2,1:T(8,128)(2,1)S(1)} %broadcast_multiply_fusion), channel_id=1, source_target_pairs={{0,32},{1,33},{2,34},{3,35},{4,36},{5,37},{6,38},{7,39},{8,40},{9,... | collective-permute-start | bytes 21608 | tf_op jit(solution)/shard_map/ppermute | solution.py:40
  5.2 1.0 copy-start.3
  6.2 0.9 copy-start.5
  7.8 25.3 %collective-permute-start.2 = (bf16[2,32,2,256]{3,2,1,0:T(2,128)(2,1)S(1)}, bf16[2,32,2,256]{3,2,1,0:T(2,128)(2,1)S(1)}, u32[]{:S(2)}, u32[]{:S(2)}) collective-permute-start(bf16[2,32,2,256]{3,2,1,0:T(2,128)(2,1)S(1)} %get-tuple-element.10), channel_id=1, source_target_pairs={{0,31},{1,0},{2,1},{3,2},{4,3},{5,4},{6,5},{7,6},{8,7},{9,8},{10,9... | collective-permute-start | bytes 196616 | tf_op jit(solution)/shard_map/ppermute | solution.py:40
  16.6 16.5 %collective-permute-start.3 = (bf16[2,32,2,256]{3,2,1,0:T(2,128)(2,1)S(1)}, bf16[2,32,2,256]{3,2,1,0:T(2,128)(2,1)S(1)}, u32[]{:S(2)}, u32[]{:S(2)}) collective-permute-start(bf16[2,32,2,256]{3,2,1,0:T(2,128)(2,1)S(1)} %get-tuple-element.11), channel_id=1, source_target_pairs={{0,1},{1,2},{2,3},{3,4},{4,5},{5,6},{6,7},{7,8},{8,9},{9,10},{10,1... | collective-permute-start | bytes 196616 | tf_op jit(solution)/shard_map/ppermute | solution.py:40
  16.6 16.5 %collective-permute-start.4 = (bf16[2,2,32,256]{3,2,1,0:T(8,128)(2,1)S(1)}, bf16[2,2,32,256]{3,2,1,0:T(8,128)(2,1)S(1)}, u32[]{:S(2)}, u32[]{:S(2)}) collective-permute-start(bf16[2,2,32,256]{3,2,1,0:T(8,128)(2,1)S(1)} %get-tuple-element.12), channel_id=1, source_target_pairs={{0,64},{1,65},{2,66},{3,67},{4,68},{5,69},{6,70},{7,71},{8,72},{9,... | collective-permute-start | bytes 196616 | tf_op jit(solution)/shard_map/ppermute | solution.py:40
  17.0 0.6 copy-start.12
  18.0 11.7 %collective-permute-start.5 = (bf16[2,2,2,256]{3,2,1,0:T(2,128)(2,1)S(1)}, bf16[2,2,2,256]{3,2,1,0:T(2,128)(2,1)S(1)}, u32[]{:S(2)}, u32[]{:S(2)}) collective-permute-start(bf16[2,2,2,256]{3,2,1,0:T(2,128)(2,1)S(1)} %get-tuple-element.13), channel_id=1, source_target_pairs={{0,95},{1,64},{2,65},{3,66},{4,67},{5,68},{6,69},{7,70},{8,71},{9,... | collective-permute-start | bytes 12296 | tf_op jit(solution)/shard_map/ppermute | solution.py:40
  25.2 7.9 %collective-permute-start.6 = (bf16[2,2,2,256]{3,2,1,0:T(2,128)(2,1)S(1)}, bf16[2,2,2,256]{3,2,1,0:T(2,128)(2,1)S(1)}, u32[]{:S(2)}, u32[]{:S(2)}) collective-permute-start(bf16[2,2,2,256]{3,2,1,0:T(2,128)(2,1)S(1)} %get-tuple-element.14), channel_id=1, source_target_pairs={{0,65},{1,66},{2,67},{3,68},{4,69},{5,70},{6,71},{7,72},{8,73},{9,... | collective-permute-start | bytes 12296 | tf_op jit(solution)/shard_map/ppermute | solution.py:40
  25.2 1.0 copy-start.6
  29.7 11.7 %copy-start = (bf16[32,288,256]{2,1,0:T(8,128)(2,1)}, bf16[32,288,256]{2,1,0:T(8,128)(2,1)S(1)}, u32[]{:S(2)}) copy-start(bf16[32,288,256]{2,1,0:T(8,128)(2,1)S(1)} %get-tuple-element.15.bands) | copy-start | bytes 14155780
  41.4 25.2 %copy-start.11 = (bf16[16,9,5,5]{0,3,2,1:T(8,128)(2,1)S(1)}, bf16[16,9,5,5]{0,3,2,1:T(8,128)(2,1)}, u32[]{:S(2)}) copy-start(bf16[16,9,5,5]{0,3,2,1:T(8,128)(2,1)} %copy-done.10) | copy-start | bytes 21604
  41.5 25.2 %copy-start.13 = (bf16[16,9,5,5]{0,3,2,1:T(8,128)(2,1)S(1)}, bf16[16,9,5,5]{0,3,2,1:T(8,128)(2,1)}, u32[]{:S(2)}) copy-start(bf16[16,9,5,5]{0,3,2,1:T(8,128)(2,1)} %copy-done.12) | copy-start | bytes 21604
  59.7 37.8 %copy-start.2 = (bf16[9,256,256]{2,1,0:T(8,128)(2,1)S(1)}, bf16[9,256,256]{2,1,0:T(8,128)(2,1)}, u32[]{:S(2)}) copy-start(bf16[9,256,256]{2,1,0:T(8,128)(2,1)} %param.12) | copy-start | bytes 3538948
  59.7 18.3 %all-to-all-start.1 = ((bf16[64,40,128]{2,1,0:T(8,128)(2,1)}), bf16[64,40,128]{2,1,0:T(8,128)(2,1)S(1)}, u32[]{:S(2)}, u32[]{:S(2)}) async-start(bf16[64,40,128]{2,1,0:T(8,128)(2,1)} %shard_map.108), calls=%async_computation.1 | async-start | bytes 1310720 | tf_op jit(solution)/shard_map/all_to_all | solution.py:343
  78.0 34.9 %collective-permute-start.9 = (bf16[64,40,128]{2,1,0:T(8,128)(2,1)S(1)}, bf16[64,40,128]{2,1,0:T(8,128)(2,1)S(1)}, u32[]{:S(2)}, u32[]{:S(2)}) collective-permute-start(bf16[64,40,128]{2,1,0:T(8,128)(2,1)S(1)} %all-to-all-done.1.mine), channel_id=1, source_target_pairs={{0,32},{1,33},{2,34},{3,35},{4,36},{5,37},{6,38},{7,39},{8,40},{9,... | collective-permute-start | bytes 1966088 | tf_op jit(solution)/shard_map/ppermute | solution.py:40
  83.5 4.6 %collective-permute-start.8 = (bf16[2,9,5,5]{0,3,2,1:T(8,128)(2,1)}, bf16[2,9,5,5]{0,3,2,1:T(8,128)(2,1)}, u32[]{:S(2)}, u32[]{:S(2)}) collective-permute-start(bf16[2,9,5,5]{0,3,2,1:T(8,128)(2,1)} %slice_select_fusion), channel_id=1, source_target_pairs={{0,64},{1,65},{2,66},{3,67},{4,68},{5,69},{6,70},{7,71},{8,72},{9,... | collective-permute-start | bytes 2708 | tf_op jit(solution)/shard_map/ppermute | solution.py:40
  97.5 2.3 %copy-start.1 = (bf16[32,288,256]{2,1,0:T(8,128)(2,1)S(1)}, bf16[32,288,256]{2,1,0:T(8,128)(2,1)}, u32[]{:S(2)}) copy-start(bf16[32,288,256]{2,1,0:T(8,128)(2,1)} %copy-done) | copy-start | bytes 14155780
  99.8 5.2 %copy-start.7 = (bf16[16,32,256]{2,1,0:T(8,128)(2,1)S(1)}, bf16[16,32,256]{2,1,0:T(8,128)(2,1)}, u32[]{:S(2)}) copy-start(bf16[16,32,256]{2,1,0:T(8,128)(2,1)} %co.5) | copy-start | bytes 786436
  99.9 5.2 %copy-start.9 = (bf16[45,2560]{1,0:T(8,128)(2,1)S(1)}, bf16[45,2560]{1,0:T(8,128)(2,1)}, u32[]{:S(2)}) copy-start(bf16[45,2560]{1,0:T(8,128)(2,1)} %constant.29.clone.table) | copy-start | bytes 691204

commit v2 on v1

v2 whole, which is shorter than its diff:
```python
import functools
import math

import jax
import jax.numpy as jnp
from jax import lax
from jax.experimental import pallas as pl
from jax.experimental.pallas import tpu as pltpu
from jax.sharding import Mesh, PartitionSpec as P

AXES = ("xl", "core", "y", "xh", "z")
SIZES = (2, 2, 4, 2, 4)
RING = ("xl", "y", "xh", "z")

ROWS = 16
CELLS = 32
SLOTS = 48
BASIS = 9
CHAN = 256
HALF = 128
BAND = 5
KEEP = 40
bf16 = jnp.bfloat16
f32 = jnp.float32


def moves(lat=False, core=False, lon=0):
    pairs = []
    for xl in range(2):
        for c in range(2):
            for cell in range(32):
                source = (xl * 2 + c) * 32 + cell
                row = (xl ^ int(lat)) * 2 + (c ^ int(core))
                pairs.append((source, row * 32 + (cell + lon) % 32))
    return pairs


def send(x, **way):
    return lax.ppermute(x, AXES, moves(**way))


def vmem(count):
    return [pl.BlockSpec(memory_space=pltpu.VMEM)] * count


SMEM = pl.BlockSpec(memory_space=pltpu.SMEM)


def call(kernel, outs, operands, scratch=(), place=None, flops=0, traffic=0, limit=40):
    shapes = [jax.ShapeDtypeStruct(*o) for o in outs]
    specs = vmem(len(operands))
    args = tuple(operands)
    if place is not None:
        specs = [SMEM] + specs
        args = (place,) + args
    return pl.pallas_call(
        kernel,
        out_shape=shapes,
        in_specs=specs,
        out_specs=vmem(len(outs)),
        scratch_shapes=list(scratch),
        compiler_params=pltpu.CompilerParams(vmem_limit_bytes=limit * 1024 * 1024),
        cost_estimate=pl.CostEstimate(flops=flops, bytes_accessed=traffic, transcendentals=0),
    )(*args)


def column_kernel(fo, co, right, left):
    for f, ref in enumerate((fo, co)):
        right[f] = ref[:, CELLS - 2 : CELLS, :]
        left[f] = ref[:, 0:2, :]


def boundary(xl, core):
    return [
        ((xl == side) & (core == (1 - side if part == 0 else side)), part, 14 * (1 - side))
        for side in range(2)
        for part in range(2)
    ]


def row_kernel(place, fo, fx, co, cx, ro, rx, lo, lx, to, tx, rows):
    xl, core = place[0], place[1]
    rows[:, :, 36:SLOTS, :] = jnp.zeros((2, 2, SLOTS - 36, CHAN), bf16)
    for chosen, part, first in boundary(xl, core):

        @pl.when(chosen)
        def _():
            span = slice(first, first + 2)
            for f, pair in enumerate(((fo, fx), (co, cx))):
                rows[f, :, 0:CELLS, :] = pair[part][span]
                rows[f, :, CELLS : CELLS + 2, :] = (ro, rx)[part][f, span]
                rows[f, :, CELLS + 2 : CELLS + 4, :] = (lo, lx)[part][f, span]
            rows[1, 0, SLOTS - 2 : SLOTS, :] = (to, tx)[part][span]


def padded(dst, f, xl, core, own, other, ro, rx, lo, lx, rows, lanes):
    width = dst.shape[-1]
    dst[:, 36:SLOTS, :] = jnp.zeros((36, SLOTS - 36, width), bf16)
    for part, (ref, right, left) in enumerate(((own, ro, lo), (other, rx, lx))):
        at = pl.ds(2 + ROWS * (core if part == 0 else 1 - core), ROWS)
        dst[at, 0:CELLS, :] = ref[:, :, lanes]
        dst[at, CELLS : CELLS + 2, :] = right[f, :, :, lanes]
        dst[at, CELLS + 2 : CELLS + 4, :] = left[f, :, :, lanes]
    if rows is None:
        dst[0:2] = jnp.zeros((2, SLOTS, width), bf16)
        dst[34:36] = jnp.zeros((2, SLOTS, width), bf16)
    else:
        dst[pl.ds(34 * (1 - xl), 2), 0:36, :] = rows[f, :, 0:36, lanes]
        dst[pl.ds(34 * xl, 2)] = jnp.zeros((2, SLOTS, width), bf16)


def over(index, divisor):
    return ((index.astype(f32) + 0.5) * (1.0 / divisor)).astype(jnp.int32)


def split_taps(index):
    k = over(index, 25)
    tap = index - 25 * k
    b = over(tap, 5)
    return k, b, tap - 5 * b


def iota(shape, axis):
    return lax.broadcasted_iota(jnp.int32, shape, axis)


def band_masks(lanes):
    cell = iota((CELLS, lanes), 0)
    lane = iota((CELLS, lanes), 1)
    slot = lane - SLOTS * over(lane, SLOTS)
    place = jnp.where(slot < CELLS + 2, slot, jnp.where(slot < CELLS + 4, slot - 36, 1000))
    return [(place - cell + 2) == s for s in range(BAND)]


def band(block, masks, lanes, row):
    total = jnp.zeros((CELLS, lanes), f32)
    for s in range(BAND):
        line = block[pl.ds(row, 1), s * lanes : (s + 1) * lanes]
        total = jnp.where(masks[s], jnp.broadcast_to(line, (CELLS, lanes)), total)
    return total.astype(bf16)


def one_hot(row, group, offset, count, total):
    column = iota((total, count), 1)
    return (over(row, group) == column + offset).astype(f32).astype(bf16)


def spread(rep, keep, row_key, lanes, inner):
    lane = iota((1, BAND * lanes), 1)
    s = over(lane, lanes)
    o = over(lane - lanes * s, SLOTS)
    lane_key = jnp.where(o < inner, o * BAND + s, -2)
    table = jnp.where(row_key == lane_key, 1.0, 0.0).astype(bf16)
    kept = jnp.where(keep, rep, 0.0).astype(bf16)
    return jnp.dot(kept, table, preferred_element_type=f32)


def forward_band_kernel(to, tx, co, cx, bands, cot_t, lines):
    row = iota((512, 1), 0)
    rep = jnp.dot(one_hot(row, 16, 0, 16, 512), to[...], preferred_element_type=f32)
    rep += jnp.dot(one_hot(row, 16, 16, 16, 512), tx[...], preferred_element_type=f32)
    k, _, _ = split_taps(iota((1, CHAN), 1))
    _, b, s = split_taps(iota((CHAN, 1), 0))
    lines[...] = spread(rep, k == row - 16 * over(row, 16), b * BAND + s, CHAN, BAND)
    masks = band_masks(CHAN)

    def step(n, carry):
        for k in range(BASIS):
            bands[n, k * CELLS : (k + 1) * CELLS, :] = band(lines, masks, CHAN, n * 16 + k)
        return carry

    lax.fori_loop(0, 2 * ROWS, step, 0)
    cot_t[:, 0:512] = co[...].reshape(512, CHAN).T
    cot_t[:, 512:1024] = cx[...].reshape(512, CHAN).T


def weight_kernel(place, fo, fx, ro, rx, lo, lx, bands, cot_t, grad, field, basis):
    xl, core = place[0], place[1]
    lanes = pl.ds(pl.multiple_of(core * HALF, HALF), HALF)
    padded(field, 0, xl, core, fo, fx, ro, rx, lo, lx, None, lanes)

    def step(n, carry):
        first = jnp.where(n < ROWS, core * ROWS + n, (1 - core) * ROWS + n - ROWS)
        window = field[pl.ds(first, BAND)].reshape(BAND * SLOTS, HALF)
        out = jnp.dot(
            bands[n, :, 0 : BAND * SLOTS], window, preferred_element_type=f32
        ).astype(bf16)
        at = pl.ds(pl.multiple_of(n * CELLS, CELLS), CELLS)
        for k in range(BASIS):
            basis[at, k * HALF : (k + 1) * HALF] = out[k * CELLS : (k + 1) * CELLS]
        return carry

    lax.fori_loop(0, 2 * ROWS, step, 0)
    for chosen, part, first in boundary(xl, core):

        @pl.when(chosen)
        def _():
            at = (part * ROWS + first) * CELLS
            basis[at : at + 2 * CELLS, :] = jnp.zeros((2 * CELLS, BASIS * HALF), bf16)

    for k in range(BASIS):
        grad[k] = jnp.dot(
            cot_t[...], basis[:, k * HALF : (k + 1) * HALF], preferred_element_type=f32
        )


def runs(k, side):
    begin, at = side * 144 + k * 16, 0
    while at < 16:
        s, j = divmod(begin + at, 64)
        count = min(16 - at, 64 - j)
        yield at, s * 8, j, count
        at += count


def weight_end_kernel(
    place, fo, fx, co, cx, ro, rx, lo, lx, rows, bands, grad, parts, field, cot, tile
):
    xl, core = place[0], place[1]
    lanes = pl.ds(pl.multiple_of(core * HALF, HALF), HALF)
    field[:, 36:SLOTS, :] = jnp.zeros((6, SLOTS - 36, HALF), bf16)
    field[pl.ds(4 * (1 - xl), 2), 0:36, :] = rows[0, :, 0:36, lanes]
    for chosen, part, first in boundary(xl, core):

        @pl.when(chosen)
        def _():
            ref, right, left = ((fo, ro, lo), (fx, rx, lx))[part]
            at = 2 if first == 0 else 0
            span = slice(0, 4) if first == 0 else slice(12, 16)
            field[at : at + 4, 0:CELLS, :] = ref[span, :, lanes]
            field[at : at + 4, CELLS : CELLS + 2, :] = right[0, span, :, lanes]
            field[at : at + 4, CELLS + 2 : CELLS + 4, :] = left[0, span, :, lanes]
            cot[...] = (co, cx)[part][first : first + 2].reshape(2 * CELLS, CHAN).T
            tile[...] = bands[part * ROWS + first : part * ROWS + first + 2]

    basis = []
    for r in range(2):
        window = field[r : r + BAND].reshape(BAND * SLOTS, HALF)
        basis.append(
            jnp.dot(tile[r, :, 0 : BAND * SLOTS], window, preferred_element_type=f32).astype(bf16)
        )
    parts[:, 32:KEEP, :] = jnp.zeros((64, 8, HALF), bf16)
    for k in range(BASIS):
        cells = jnp.concatenate([x[k * CELLS : (k + 1) * CELLS] for x in basis], 0)
        total = (grad[k] + jnp.dot(cot[...], cells, preferred_element_type=f32)).T
        for side in range(2):
            tiles = total[:, side * HALF : (side + 1) * HALF].reshape(16, 8, HALF).astype(bf16)
            for at, s, j, count in runs(k, side):
                parts[j : j + count, s : s + 8, :] = tiles[at : at + count]


def sum_kernel(scale, parts, out):
    total = jnp.sum(parts[...].astype(f32), axis=0) * scale
    out[...] = jnp.broadcast_to(total.astype(bf16)[None], out.shape)


def place_kernel(place, mine, theirs, out):
    core = place[1]
    for half in range(2):
        for ref, is_mine in ((mine, True), (theirs, False)):

            @pl.when(core == (half if is_mine else 1 - half))
            def _():
                for side in range(2):
                    for k in range(BASIS):
                        for at, s, j, count in runs(k, side):
                            tiles = ref[j : j + count, s : s + 8, :].astype(f32)
                            first = half * HALF + at * 8
                            out[
                                k, first : first + count * 8, side * HALF : (side + 1) * HALF
                            ] = tiles.reshape(count * 8, HALF)


def mixed_kernel(place, fo, fx, ro, rx, lo, lx, rows, bands, weight, out, field, basis):
    xl, core = place[0], place[1]
    padded(field, 0, xl, core, fo, fx, ro, rx, lo, lx, rows, slice(None))

    def step(n, carry):
        window = field[pl.ds(core * ROWS + n, BAND)].reshape(BAND * SLOTS, CHAN)
        part = jnp.dot(
            bands[n, :, 0 : BAND * SLOTS], window, preferred_element_type=f32
        ).astype(bf16)
        at = pl.ds(pl.multiple_of(n * CELLS, CELLS), CELLS)
        for k in range(BASIS):
            basis[at, k * CHAN : (k + 1) * CHAN] = part[k * CELLS : (k + 1) * CELLS]
        return carry

    lax.fori_loop(0, ROWS, step, 0)
    out[...] = (
        jnp.dot(basis[...], weight[...], preferred_element_type=f32)
        .astype(bf16)
        .reshape(ROWS, CELLS, CHAN)
    )


def feature_kernel(
    place, co, cx, ro, rx, lo, lx, rows, to, tx, weight, out, field, lines, grads, bands, total
):
    xl, core = place[0], place[1]
    lanes = 512
    near = ROWS + 4
    padded(field, 1, xl, core, co, cx, ro, rx, lo, lx, rows, slice(None))

    count = near * 8
    row = iota((count, 1), 0)
    beyond = 34 * (1 - xl) - core * ROWS
    other = 2 + (1 - 2 * core) * ROWS
    rep = jnp.dot(one_hot(row, 8, 2, 16, count), to[...], preferred_element_type=f32)
    rep += jnp.dot(one_hot(row, 8, other, 16, count), tx[...], preferred_element_type=f32)
    rep += jnp.dot(
        one_hot(row, 8, beyond, 2, count),
        rows[1, 0, SLOTS - 2 : SLOTS, :],
        preferred_element_type=f32,
    )
    _, b, _ = split_taps(iota((1, CHAN), 1))
    k, _, s = split_taps(iota((CHAN, 1), 0))
    lines[...] = spread(rep, b == row - 8 * over(row, 8), k * BAND + 4 - s, lanes, BASIS)
    masks = band_masks(lanes)
    for k in range(BASIS):
        for h in range(2):
            upstream = field[pl.ds(core * ROWS + h * 10, 10)].reshape(10 * SLOTS, CHAN)
            back = lax.dot_general(
                upstream,
                weight[k * CHAN : (k + 1) * CHAN, :],
                (((1,), (1,)), ((), ())),
                preferred_element_type=f32,
            )
            grads[h * 10 : (h + 1) * 10, k * SLOTS : (k + 1) * SLOTS, :] = back.astype(
                bf16
            ).reshape(10, SLOTS, CHAN)
    total[...] = jnp.zeros_like(total)

    def step(i, carry):
        for b in range(BAND):
            bands[b * CELLS : (b + 1) * CELLS, :] = band(lines, masks, lanes, i * 8 + b)
        part = jnp.dot(
            bands[:, 0 : BASIS * SLOTS], grads[i], preferred_element_type=f32
        ).reshape(BAND, CELLS, CHAN)
        total[pl.ds(i, BAND)] += part
        return carry

    lax.fori_loop(0, near, step, 0)
    out[...] = total[4 : 4 + ROWS].astype(bf16)


def shards(feature, filters, start, length, weight, cotangent):
    xl, core = lax.axis_index("xl"), lax.axis_index("core")
    place = jnp.stack([xl, core]).astype(jnp.int32)
    lat = xl * 2 + core

    column = ((2, ROWS, 2, CHAN), bf16)
    to_right, to_left = call(
        column_kernel, [column, column], (feature, cotangent), traffic=2**19
    )
    lo = send(to_right, lon=1)
    ro = send(to_left, lon=-1)

    band_row = (jnp.arange(225, dtype=jnp.int32) % 25) // 5
    source = lat * ROWS + jnp.arange(ROWS, dtype=jnp.int32)[:, None] - 2 + band_row[None, :]
    inside = (source >= start[:, None]) & (source < (start + length)[:, None])
    masked = jnp.pad(filters.reshape(ROWS, 225) * inside.astype(bf16), ((0, 0), (0, 31)))

    fx = send(feature, core=True)
    cx = send(cotangent, core=True)
    tx = send(masked, core=True)
    bands, cot_t = call(
        forward_band_kernel,
        [((32, BASIS * CELLS, CHAN), bf16), ((CHAN, 1024), bf16)],
        (masked, tx, cotangent, cx),
        scratch=[pltpu.VMEM((512, BAND * CHAN), f32)],
        flops=2 * 512 * 256 * 1280,
        traffic=6 * 2**20,
    )
    lo, ro, bands = lax.optimization_barrier((lo, ro, bands))
    lx = send(lo, core=True)
    rx = send(ro, core=True)
    halo = (ro, rx, lo, lx)

    (rows,) = call(
        row_kernel,
        [((2, 2, SLOTS, CHAN), bf16)],
        (feature, fx, cotangent, cx, *halo, masked, tx),
        place=place,
        traffic=2**20,
    )
    rows = send(rows, lat=True)
    (grad,) = call(
        weight_kernel,
        [((BASIS, CHAN, HALF), f32)],
        (feature, fx, *halo, bands, cot_t),
        scratch=[
            pltpu.VMEM((36, SLOTS, HALF), bf16),
            pltpu.VMEM((1024, BASIS * HALF), bf16),
        ],
        place=place,
        flops=2 * 32 * 288 * 256 * 256 + 2 * 1024 * 1152 * 256,
        traffic=7 * 2**20,
    )
    rows, grad = lax.optimization_barrier((rows, grad))
    (parts,) = call(
        weight_end_kernel,
        [((64, KEEP, HALF), bf16)],
        (feature, fx, cotangent, cx, *halo, rows, bands, grad),
        scratch=[
            pltpu.VMEM((6, SLOTS, HALF), bf16),
            pltpu.VMEM((CHAN, 2 * CELLS), bf16),
            pltpu.VMEM((2, BASIS * CELLS, CHAN), bf16),
        ],
        place=place,
        flops=2 * 64 * 1152 * 256,
        traffic=3 * 2**20,
    )
    mixing = weight.reshape(BASIS * CHAN, CHAN)

    swapped = lax.all_to_all(parts, RING, 0, 0, tiled=True)
    _, mixing_after = lax.optimization_barrier((parts, mixing))
    (mixed,) = call(
        mixed_kernel,
        [((ROWS, CELLS, CHAN), bf16)],
        (feature, fx, *halo, rows, bands, mixing_after),
        scratch=[
            pltpu.VMEM((36, SLOTS, CHAN), bf16),
            pltpu.VMEM((512, BASIS * CHAN), bf16),
        ],
        place=place,
        flops=2 * 16 * 288 * 256 * 256 + 2 * 512 * 2304 * 256,
        traffic=8 * 2**20,
    )
    swapped, mixed = lax.optimization_barrier((swapped, mixed))
    (shared,) = call(
        functools.partial(sum_kernel, 1.0 / math.sqrt(64 * 1024)),
        [((64, KEEP, HALF), bf16)],
        (swapped,),
        traffic=2**20,
    )

    mine = lax.all_to_all(shared, RING, 0, 0, tiled=True)
    _, mixing_later = lax.optimization_barrier((shared, mixing))
    (grad_feature,) = call(
        feature_kernel,
        [((ROWS, CELLS, CHAN), bf16)],
        (cotangent, cx, *halo, rows, masked, tx, mixing_later),
        scratch=[
            pltpu.VMEM((36, SLOTS, CHAN), bf16),
            pltpu.VMEM(((ROWS + 4) * 8, BAND * 512), f32),
            pltpu.VMEM((ROWS + 4, BASIS * SLOTS, CHAN), bf16),
            pltpu.VMEM((BAND * CELLS, 512), bf16),
            pltpu.VMEM((ROWS + 8, CELLS, CHAN), f32),
        ],
        place=place,
        flops=2 * 960 * 2304 * 256 + 2 * 20 * 160 * 512 * 256,
        traffic=8 * 2**20,
    )
    mine, grad_feature = lax.optimization_barrier((mine, grad_feature))
    theirs = send(mine, core=True)
    (grad_weight,) = call(
        place_kernel, [((BASIS, CHAN, CHAN), f32)], (mine, theirs), place=place, traffic=4 * 2**20
    )
    return (mixed, grad_feature, grad_weight)


def solution(mesh):
    fine = Mesh(mesh.devices.reshape(SIZES), AXES)
    lat, lon = ("xl", "core"), ("y", "xh", "z")
    return jax.shard_map(
        shards,
        mesh=fine,
        in_specs=(P(lat, lon, None), P(lat, None, None), P(lat), P(lat), P(), P(lat, lon, None)),
        out_specs=(P(lat, lon, None), P(lat, lon, None), P()),
        check_vma=False,
    )
```

time: 116 us -> 81.7 us (0.70)
  blocking collectives: 17.3 us -> 0 us
  waiting for transfers between devices: 18.2 us -> 11 us
  local copies, waits for them, and re-layouts: 13.7 us -> 8 us
  other arithmetic: 6.78 us -> 1.5 us
  Pallas kernels: 28.6 us -> 31.2 us
    all_to_all x1 -> x0, blocking collectives: 17.3 us -> none  [shards(): swapped = lax.all_to_all(parts, RING, 0, 0, tiled=True)]
    all_to_all x0 -> x1, starting transfers between devices: none -> 7.34 us  [shards(): swapped = lax.all_to_all(parts, RING, 0, 0, tiled=True)]
    all_to_all x1, waiting for transfers between devices: 10.6 us -> 3.29 us  [shards(): mine = lax.all_to_all(shared, RING, 0, 0, tiled=True)]
    ppermute x10 -> x9, starting transfers between devices: 22.7 us -> 15.7 us  [send(): return lax.ppermute(x, AXES, moves(**way))]
    all_to_all x0 -> x1, waiting for transfers between devices: none -> 5.01 us  [shards(): swapped = lax.all_to_all(parts, RING, 0, 0, tiled=True)]
    ppermute x10 -> x9, waiting for transfers between devices: 7.58 us -> 2.72 us  [send(): return lax.ppermute(x, AXES, moves(**way))]
    select_n x3 -> x1, other arithmetic: 3.31 us -> 0.02 us  [shards(): band_row = jnp.arange(225, dtype=jnp.int32) % 25 // 5]
    pallas_call x7 -> x9, Pallas kernels: 28.6 us -> 31.2 us  [call(): pl.pallas_call(kernel, out_shape=shapes, in_specs=specs, out_specs=vmem(l...]
  transfers between devices with their start and end apart: 11 -> 11, of which waited for: 3 -> 5; matrix products, arithmetic and copies ran while one was open for 13% -> 3% of each run, Pallas kernels for 15% -> 31%
where the time goes in v2:
time: 81.7 us; the launch traced here: 81.1 us
  Pallas kernels  31.2 us (38%)
  starting transfers between devices  28.6 us (35%)
  waiting for transfers between devices  11 us (13%)
  local copies, waits for them, and re-layouts  8 us (10%)
  other arithmetic  1.5 us (2%)
    pallas_call x9, Pallas kernels, call(): pl.pallas_call(kernel, out_shape=shapes, in_specs=specs, out_specs=vmem(l...  31.2 us
    ppermute x9, starting transfers between devices, send(): return lax.ppermute(x, AXES, moves(**way))  15.7 us
    unnamed x21, local copies, waits for them, and re-layouts  7.88 us
    all_to_all x1, starting transfers between devices, shards(): swapped = lax.all_to_all(parts, RING, 0, 0, tiled=True)  7.34 us
    all_to_all x1, starting transfers between devices, shards(): mine = lax.all_to_all(shared, RING, 0, 0, tiled=True)  5.57 us
    all_to_all x1, waiting for transfers between devices, shards(): swapped = lax.all_to_all(parts, RING, 0, 0, tiled=True)  5.01 us
    all_to_all x1, waiting for transfers between devices, shards(): mine = lax.all_to_all(shared, RING, 0, 0, tiled=True)  3.29 us
    ppermute x9, waiting for transfers between devices, send(): return lax.ppermute(x, AXES, moves(**way))  2.72 us
  transfers between devices with their start and end apart: 11, of which 5 were waited for; matrix products, arithmetic and copies ran while one was open for 3% of the time, Pallas kernels for 31%

profile of v2, /device:TPU:1, one launch (start us, length us, event | category | flops | bytes accessed | tf_op | source)
XLA Modules:
  0.0 81.1 jit_solution(4590738533232053763)
XLA Ops:
  0.6 1.5 %collective-permute-start = (bf16[16,32,256]{2,1,0:T(8,128)(2,1)}, bf16[16,32,256]{2,1,0:T(8,128)(2,1)S(1)}, u32[]{:S(2)}, u32[]{:S(2)}) collective-permute-start(bf16[16,32,256]{2,1,0:T(8,128)(2,1)} %fo.9), channel_id=1, source_target_pairs={{0,32},{1,33},{2,34},{3,35},{4,36},{5,37},{6,38},{7,39},{8,40},{9,... | collective-permute-start | bytes 786440 | tf_op jit(solution)/shard_map/ppermute | solution.py:39
  2.1 0.1 collective-permute-start.1
  2.3 0.8 copy.10
  3.1 0.1 reshape.38
  3.2 0.7 add.60
  3.8 0.7 fusion.1
  4.6 0.5 collective-permute-start.4
  5.1 0.9 %copy-done.2 = bf16[16,32,256]{2,1,0:T(8,128)(2,1)S(1)} copy-done((bf16[16,32,256]{2,1,0:T(8,128)(2,1)S(1)}, bf16[16,32,256]{2,1,0:T(8,128)(2,1)}, u32[]{:S(2)}) %copy-start.2) | copy-done | bytes 262168
  6.0 0.9 %copy-done.5 = bf16[16,32,256]{2,1,0:T(8,128)(2,1)S(1)} copy-done((bf16[16,32,256]{2,1,0:T(8,128)(2,1)S(1)}, bf16[16,32,256]{2,1,0:T(8,128)(2,1)}, u32[]{:S(2)}) %copy-start.5) | copy-done | bytes 262168
  7.0 0.1 shard_map.85
  7.0 1.8 %collective-permute-start.2 = (bf16[2,16,2,256]{3,2,1,0:T(2,128)(2,1)S(1)}, bf16[2,16,2,256]{3,2,1,0:T(2,128)(2,1)S(1)}, u32[]{:S(2)}, u32[]{:S(2)}) collective-permute-start(bf16[2,16,2,256]{3,2,1,0:T(2,128)(2,1)S(1)} %get-tuple-element.18), channel_id=1, source_target_pairs={{0,1},{1,2},{2,3},{3,4},{4,5},{5,6},{6,7},{7,8},{8,9},{9,10},{10,1... | collective-permute-start | bytes 98312 | tf_op jit(solution)/shard_map/ppermute | solution.py:39
  8.8 7.1 %collective-permute-start.3 = (bf16[2,16,2,256]{3,2,1,0:T(2,128)(2,1)S(1)}, bf16[2,16,2,256]{3,2,1,0:T(2,128)(2,1)S(1)}, u32[]{:S(2)}, u32[]{:S(2)}) collective-permute-start(bf16[2,16,2,256]{3,2,1,0:T(2,128)(2,1)S(1)} %get-tuple-element.19), channel_id=1, source_target_pairs={{0,31},{1,0},{2,1},{3,2},{4,3},{5,4},{6,5},{7,6},{8,7},{9,8},{10,9... | collective-permute-start | bytes 98312 | tf_op jit(solution)/shard_map/ppermute | solution.py:39
  15.9 0.0 collective-permute-done.4.tx
  15.9 0.0 collective-permute-done.1.cx
  16.0 0.9 %copy-done.6 = bf16[16,32,256]{2,1,0:T(8,128)(2,1)S(1)} copy-done((bf16[16,32,256]{2,1,0:T(8,128)(2,1)S(1)}, bf16[16,32,256]{2,1,0:T(8,128)(2,1)}, u32[]{:S(2)}) %copy-start.6) | copy-done | bytes 262168
  16.9 3.8 %shard_map.86 = (bf16[32,288,256]{2,1,0:T(8,128)(2,1)S(1)}, bf16[256,1024]{1,0:T(8,128)(2,1)S(1)}) custom-call(bf16[16,256]{1,0:T(8,128)(2,1)S(1)} %pad.4.to, bf16[16,256]{1,0:T(8,128)(2,1)S(1)} %collective-permute-done.4.tx, bf16[16,32,256]{2,1,0:T(8,128)(2,1)S(1)} %copy-done.6, bf16[16,32,256]{2,1,0:T(8,128)(2,1)S(1)} %collective-permute-done.1.cx), custom_call_target="tpu_custom_call" | custom-call | flops 335544320 | bytes 6291456 | tf_op jit(solution)/shard_map/pallas_call | solution.py:56
  20.7 0.0 copy-start
  20.8 0.0 collective-permute-done.2.lo
  20.8 0.0 collective-permute-done.3.ro
  20.8 0.4 collective-permute-start.5
  21.2 0.1 collective-permute-start.6
  21.4 0.1 pad_add_fusion.place
  21.4 0.0 collective-permute-done.fx
  21.4 0.6 collective-permute-done.5.rx
  22.1 0.3 collective-permute-done.6.lx
  22.4 0.9 %copy-done.3 = bf16[16,32,256]{2,1,0:T(8,128)(2,1)S(1)} copy-done((bf16[16,32,256]{2,1,0:T(8,128)(2,1)S(1)}, bf16[16,32,256]{2,1,0:T(8,128)(2,1)}, u32[]{:S(2)}) %copy-start.3) | copy-done | bytes 262168
  23.4 0.9 %copy-done.7 = bf16[16,32,256]{2,1,0:T(8,128)(2,1)S(1)} copy-done((bf16[16,32,256]{2,1,0:T(8,128)(2,1)S(1)}, bf16[16,32,256]{2,1,0:T(8,128)(2,1)}, u32[]{:S(2)}) %copy-start.7) | copy-done | bytes 262168
  24.3 0.6 shard_map.87
  24.9 0.4 collective-permute-start.7
  25.3 8.2 %shard_map.88.grad = f32[9,256,128]{2,1,0:T(8,128)S(1)} custom-call(s32[2]{0:T(128)S(1)} %pad_add_fusion.place, bf16[16,32,256]{2,1,0:T(8,128)(2,1)S(1)} %copy-done.3, bf16[16,32,256]{2,1,0:T(8,128)(2,1)S(1)} %collective-permute-done.fx, bf16[2,16,2,256]{3,2,1,0:T(2,128)(2,1)S(1)} %collective-permute-done.3.ro, ...), custom_call_target="tpu_custom_call" | custom-call | flops 1811939328 | bytes 7340032 | tf_op jit(solution)/shard_map/pallas_call | solution.py:56
  33.5 0.0 copy-start.4
  33.5 0.0 copy-start.9
  33.6 0.0 collective-permute-done.7.rows
  33.6 2.0 %shard_map.89 = bf16[64,40,128]{2,1,0:T(8,128)(2,1)} custom-call(s32[2]{0:T(128)S(1)} %pad_add_fusion.place, bf16[16,32,256]{2,1,0:T(8,128)(2,1)S(1)} %copy-done.3, bf16[16,32,256]{2,1,0:T(8,128)(2,1)S(1)} %collective-permute-done.fx, bf16[16,32,256]{2,1,0:T(8,128)(2,1)S(1)} %copy-done.8, bf16[16,32,256]{2,1,0:T(8,128)(2,1)S(1)} %collective-permute-done.1.cx, ...), custom_call_target="tpu_custom_call" | custom-call | flops 37748736 | bytes 3145728 | tf_op jit(solution)/shard_map/pallas_call | solution.py:56
  35.6 7.3 %all-to-all-start = ((bf16[64,40,128]{2,1,0:T(8,128)(2,1)}), bf16[64,40,128]{2,1,0:T(8,128)(2,1)S(1)}, u32[]{:S(2)}, u32[]{:S(2)}) async-start(bf16[64,40,128]{2,1,0:T(8,128)(2,1)} %shard_map.89), calls=%async_computation | async-start | bytes 1310720 | tf_op jit(solution)/shard_map/all_to_all | solution.py:415
  43.0 0.0 copy-done.4
  43.0 0.0 copy-done.9
  43.0 0.0 copy-start.1
  43.0 2.3 %copy-done.1 = bf16[32,288,256]{2,1,0:T(8,128)(2,1)S(1)} copy-done((bf16[32,288,256]{2,1,0:T(8,128)(2,1)S(1)}, bf16[32,288,256]{2,1,0:T(8,128)(2,1)}, u32[]{:S(2)}) %copy-start.1) | copy-done | bytes 4718616
  45.3 5.2 %shard_map.90 = bf16[16,32,256]{2,1,0:T(8,128)(2,1)} custom-call(s32[2]{0:T(128)S(1)} %pad_add_fusion.place, bf16[16,32,256]{2,1,0:T(8,128)(2,1)S(1)} %copy-done.4, bf16[16,32,256]{2,1,0:T(8,128)(2,1)S(1)} %collective-permute-done.fx, bf16[2,16,2,256]{3,2,1,0:T(2,128)(2,1)S(1)} %collective-permute-done.3.ro, ...), custom_call_target="tpu_custom_call" | custom-call | flops 1207959552 | bytes 8388608 | tf_op jit(solution)/shard_map/pallas_call | solution.py:56
  50.5 5.0 %all-to-all-done.parts = bf16[64,40,128]{2,1,0:T(8,128)(2,1)S(1)} async-done(((bf16[64,40,128]{2,1,0:T(8,128)(2,1)}), bf16[64,40,128]{2,1,0:T(8,128)(2,1)S(1)}, u32[]{:S(2)}, u32[]{:S(2)}) %all-to-all-start) | async-done | bytes 655392 | tf_op jit(solution)/shard_map/all_to_all | solution.py:415
  55.5 1.0 %shard_map.91 = bf16[64,40,128]{2,1,0:T(8,128)(2,1)} custom-call(bf16[64,40,128]{2,1,0:T(8,128)(2,1)S(1)} %all-to-all-done.parts), custom_call_target="tpu_custom_call" | custom-call | bytes 1048576 | tf_op jit(solution)/shard_map/pallas_call | solution.py:56
  56.5 5.6 %all-to-all-start.1 = ((bf16[64,40,128]{2,1,0:T(8,128)(2,1)}), bf16[64,40,128]{2,1,0:T(8,128)(2,1)S(1)}, u32[]{:S(2)}, u32[]{:S(2)}) async-start(bf16[64,40,128]{2,1,0:T(8,128)(2,1)} %shard_map.91), calls=%async_computation.1 | async-start | bytes 1310720 | tf_op jit(solution)/shard_map/all_to_all | solution.py:437
  62.1 8.1 %shard_map.92 = bf16[16,32,256]{2,1,0:T(8,128)(2,1)} custom-call(s32[2]{0:T(128)S(1)} %pad_add_fusion.place, bf16[16,32,256]{2,1,0:T(8,128)(2,1)S(1)} %copy-done.8, bf16[16,32,256]{2,1,0:T(8,128)(2,1)S(1)} %collective-permute-done.1.cx, bf16[2,16,2,256]{3,2,1,0:T(2,128)(2,1)S(1)} %collective-permute-done.3.ro, ...), custom_call_target="tpu_custom_call" | custom-call | flops 1971322880 | bytes 8388608 | tf_op jit(solution)/shard_map/pallas_call | solution.py:56
  70.2 3.3 %all-to-all-done.1.mine = bf16[64,40,128]{2,1,0:T(8,128)(2,1)S(1)} async-done(((bf16[64,40,128]{2,1,0:T(8,128)(2,1)}), bf16[64,40,128]{2,1,0:T(8,128)(2,1)S(1)}, u32[]{:S(2)}, u32[]{:S(2)}) %all-to-all-start.1) | async-done | bytes 655392 | tf_op jit(solution)/shard_map/all_to_all | solution.py:437
  73.5 3.7 %collective-permute-start.8 = (bf16[64,40,128]{2,1,0:T(8,128)(2,1)S(1)}, bf16[64,40,128]{2,1,0:T(8,128)(2,1)S(1)}, u32[]{:S(2)}, u32[]{:S(2)}) collective-permute-start(bf16[64,40,128]{2,1,0:T(8,128)(2,1)S(1)} %all-to-all-done.1.mine), channel_id=1, source_target_pairs={{0,32},{1,33},{2,34},{3,35},{4,36},{5,37},{6,38},{7,39},{8,40},{9,... | collective-permute-start | bytes 1966088 | tf_op jit(solution)/shard_map/ppermute | solution.py:39
  77.3 1.7 %collective-permute-done.8.theirs = bf16[64,40,128]{2,1,0:T(8,128)(2,1)S(1)} collective-permute-done((bf16[64,40,128]{2,1,0:T(8,128)(2,1)S(1)}, bf16[64,40,128]{2,1,0:T(8,128)(2,1)S(1)}, u32[]{:S(2)}, u32[]{:S(2)}) %collective-permute-start.8) | collective-permute-done | bytes 655392 | tf_op jit(solution)/shard_map/ppermute | solution.py:39
  79.0 2.1 %shard_map.93 = f32[9,256,256]{2,1,0:T(8,128)} custom-call(s32[2]{0:T(128)S(1)} %pad_add_fusion.place, bf16[64,40,128]{2,1,0:T(8,128)(2,1)S(1)} %all-to-all-done.1.mine, bf16[64,40,128]{2,1,0:T(8,128)(2,1)S(1)} %collective-permute-done.8.theirs), custom_call_target="tpu_custom_call" | custom-call | bytes 4194304 | tf_op jit(solution)/shard_map/pallas_call | solution.py:56
  (11 shorter events, 0.0 us)
Async XLA Ops:
  0.6 20.8 %collective-permute-start = (bf16[16,32,256]{2,1,0:T(8,128)(2,1)}, bf16[16,32,256]{2,1,0:T(8,128)(2,1)S(1)}, u32[]{:S(2)}, u32[]{:S(2)}) collective-permute-start(bf16[16,32,256]{2,1,0:T(8,128)(2,1)} %fo.9), channel_id=1, source_target_pairs={{0,32},{1,33},{2,34},{3,35},{4,36},{5,37},{6,38},{7,39},{8,40},{9,... | collective-permute-start | bytes 786440 | tf_op jit(solution)/shard_map/ppermute | solution.py:39
  2.1 13.8 %collective-permute-start.1 = (bf16[16,32,256]{2,1,0:T(8,128)(2,1)}, bf16[16,32,256]{2,1,0:T(8,128)(2,1)S(1)}, u32[]{:S(2)}, u32[]{:S(2)}) collective-permute-start(bf16[16,32,256]{2,1,0:T(8,128)(2,1)} %co.9), channel_id=1, source_target_pairs={{0,32},{1,33},{2,34},{3,35},{4,36},{5,37},{6,38},{7,39},{8,40},{9,... | collective-permute-start | bytes 786440 | tf_op jit(solution)/shard_map/ppermute | solution.py:39
  4.6 11.4 %collective-permute-start.4 = (bf16[16,256]{1,0:T(8,128)(2,1)S(1)}, bf16[16,256]{1,0:T(8,128)(2,1)S(1)}, u32[]{:S(2)}, u32[]{:S(2)}) collective-permute-start(bf16[16,256]{1,0:T(8,128)(2,1)S(1)} %pad.4.to), channel_id=1, source_target_pairs={{0,32},{1,33},{2,34},{3,35},{4,36},{5,37},{6,38},{7,39},{8,40},{9,... | collective-permute-start | bytes 24584 | tf_op jit(solution)/shard_map/ppermute | solution.py:39
  5.1 0.9 %copy-start.2 = (bf16[16,32,256]{2,1,0:T(8,128)(2,1)S(1)}, bf16[16,32,256]{2,1,0:T(8,128)(2,1)}, u32[]{:S(2)}) copy-start(bf16[16,32,256]{2,1,0:T(8,128)(2,1)} %fo.9) | copy-start | bytes 786436
  6.0 0.9 %copy-start.5 = (bf16[16,32,256]{2,1,0:T(8,128)(2,1)S(1)}, bf16[16,32,256]{2,1,0:T(8,128)(2,1)}, u32[]{:S(2)}) copy-start(bf16[16,32,256]{2,1,0:T(8,128)(2,1)} %co.9) | copy-start | bytes 786436
  7.0 13.7 %collective-permute-start.2 = (bf16[2,16,2,256]{3,2,1,0:T(2,128)(2,1)S(1)}, bf16[2,16,2,256]{3,2,1,0:T(2,128)(2,1)S(1)}, u32[]{:S(2)}, u32[]{:S(2)}) collective-permute-start(bf16[2,16,2,256]{3,2,1,0:T(2,128)(2,1)S(1)} %get-tuple-element.18), channel_id=1, source_target_pairs={{0,1},{1,2},{2,3},{3,4},{4,5},{5,6},{6,7},{7,8},{8,9},{9,10},{10,1... | collective-permute-start | bytes 98312 | tf_op jit(solution)/shard_map/ppermute | solution.py:39
  8.8 11.9 %collective-permute-start.3 = (bf16[2,16,2,256]{3,2,1,0:T(2,128)(2,1)S(1)}, bf16[2,16,2,256]{3,2,1,0:T(2,128)(2,1)S(1)}, u32[]{:S(2)}, u32[]{:S(2)}) collective-permute-start(bf16[2,16,2,256]{3,2,1,0:T(2,128)(2,1)S(1)} %get-tuple-element.19), channel_id=1, source_target_pairs={{0,31},{1,0},{2,1},{3,2},{4,3},{5,4},{6,5},{7,6},{8,7},{9,8},{10,9... | collective-permute-start | bytes 98312 | tf_op jit(solution)/shard_map/ppermute | solution.py:39
  15.9 1.0 %copy-start.6 = (bf16[16,32,256]{2,1,0:T(8,128)(2,1)S(1)}, bf16[16,32,256]{2,1,0:T(8,128)(2,1)}, u32[]{:S(2)}) copy-start(bf16[16,32,256]{2,1,0:T(8,128)(2,1)} %co.9) | copy-start | bytes 786436
  20.7 12.8 %copy-start = (bf16[32,288,256]{2,1,0:T(8,128)(2,1)}, bf16[32,288,256]{2,1,0:T(8,128)(2,1)S(1)}, u32[]{:S(2)}) copy-start(bf16[32,288,256]{2,1,0:T(8,128)(2,1)S(1)} %get-tuple-element.23.bands) | copy-start | bytes 14155780
  20.8 1.3 %collective-permute-start.5 = (bf16[2,16,2,256]{3,2,1,0:T(2,128)(2,1)S(1)}, bf16[2,16,2,256]{3,2,1,0:T(2,128)(2,1)S(1)}, u32[]{:S(2)}, u32[]{:S(2)}) collective-permute-start(bf16[2,16,2,256]{3,2,1,0:T(2,128)(2,1)S(1)} %collective-permute-done.3.ro), channel_id=1, source_target_pairs={{0,32},{1,33},{2,34},{3,35},{4,36},{5,37},{6,38},{7,39},{8,40},{9,... | collective-permute-start | bytes 98312 | tf_op jit(solution)/shard_map/ppermute | solution.py:39
  21.2 1.2 %collective-permute-start.6 = (bf16[2,16,2,256]{3,2,1,0:T(2,128)(2,1)S(1)}, bf16[2,16,2,256]{3,2,1,0:T(2,128)(2,1)S(1)}, u32[]{:S(2)}, u32[]{:S(2)}) collective-permute-start(bf16[2,16,2,256]{3,2,1,0:T(2,128)(2,1)S(1)} %collective-permute-done.2.lo), channel_id=1, source_target_pairs={{0,32},{1,33},{2,34},{3,35},{4,36},{5,37},{6,38},{7,39},{8,40},{9,... | collective-permute-start | bytes 98312 | tf_op jit(solution)/shard_map/ppermute | solution.py:39
  22.4 1.0 %copy-start.3 = (bf16[16,32,256]{2,1,0:T(8,128)(2,1)S(1)}, bf16[16,32,256]{2,1,0:T(8,128)(2,1)}, u32[]{:S(2)}) copy-start(bf16[16,32,256]{2,1,0:T(8,128)(2,1)} %fo.9) | copy-start | bytes 786436
  23.4 0.9 %copy-start.7 = (bf16[16,32,256]{2,1,0:T(8,128)(2,1)S(1)}, bf16[16,32,256]{2,1,0:T(8,128)(2,1)}, u32[]{:S(2)}) copy-start(bf16[16,32,256]{2,1,0:T(8,128)(2,1)} %co.9) | copy-start | bytes 786436
  24.9 8.7 %collective-permute-start.7 = (bf16[2,2,48,256]{3,2,1,0:T(8,128)(2,1)S(1)}, bf16[2,2,48,256]{3,2,1,0:T(8,128)(2,1)S(1)}, u32[]{:S(2)}, u32[]{:S(2)}) collective-permute-start(bf16[2,2,48,256]{3,2,1,0:T(8,128)(2,1)S(1)} %shard_map.87), channel_id=1, source_target_pairs={{0,64},{1,65},{2,66},{3,67},{4,68},{5,69},{6,70},{7,71},{8,72},{9,... | collective-permute-start | bytes 294920 | tf_op jit(solution)/shard_map/ppermute | solution.py:39
  25.3 8.3 %copy-start.8 = (bf16[16,32,256]{2,1,0:T(8,128)(2,1)S(1)}, bf16[16,32,256]{2,1,0:T(8,128)(2,1)}, u32[]{:S(2)}) copy-start(bf16[16,32,256]{2,1,0:T(8,128)(2,1)} %co.9) | copy-start | bytes 786436
  33.5 9.4 %copy-start.4 = (bf16[16,32,256]{2,1,0:T(8,128)(2,1)S(1)}, bf16[16,32,256]{2,1,0:T(8,128)(2,1)}, u32[]{:S(2)}) copy-start(bf16[16,32,256]{2,1,0:T(8,128)(2,1)} %fo.9) | copy-start | bytes 786436
  33.5 9.4 %copy-start.9 = (bf16[9,256,256]{2,1,0:T(8,128)(2,1)S(1)}, bf16[9,256,256]{2,1,0:T(8,128)(2,1)}, u32[]{:S(2)}) copy-start(bf16[9,256,256]{2,1,0:T(8,128)(2,1)} %param.10) | copy-start | bytes 3538948
  35.6 19.9 %all-to-all-start = ((bf16[64,40,128]{2,1,0:T(8,128)(2,1)}), bf16[64,40,128]{2,1,0:T(8,128)(2,1)S(1)}, u32[]{:S(2)}, u32[]{:S(2)}) async-start(bf16[64,40,128]{2,1,0:T(8,128)(2,1)} %shard_map.89), calls=%async_computation | async-start | bytes 1310720 | tf_op jit(solution)/shard_map/all_to_all | solution.py:415
  43.0 2.3 %copy-start.1 = (bf16[32,288,256]{2,1,0:T(8,128)(2,1)S(1)}, bf16[32,288,256]{2,1,0:T(8,128)(2,1)}, u32[]{:S(2)}) copy-start(bf16[32,288,256]{2,1,0:T(8,128)(2,1)} %copy-done) | copy-start | bytes 14155780
  56.5 17.0 %all-to-all-start.1 = ((bf16[64,40,128]{2,1,0:T(8,128)(2,1)}), bf16[64,40,128]{2,1,0:T(8,128)(2,1)S(1)}, u32[]{:S(2)}, u32[]{:S(2)}) async-start(bf16[64,40,128]{2,1,0:T(8,128)(2,1)} %shard_map.91), calls=%async_computation.1 | async-start | bytes 1310720 | tf_op jit(solution)/shard_map/all_to_all | solution.py:437
  73.5 5.5 %collective-permute-start.8 = (bf16[64,40,128]{2,1,0:T(8,128)(2,1)S(1)}, bf16[64,40,128]{2,1,0:T(8,128)(2,1)S(1)}, u32[]{:S(2)}, u32[]{:S(2)}) collective-permute-start(bf16[64,40,128]{2,1,0:T(8,128)(2,1)S(1)} %all-to-all-done.1.mine), channel_id=1, source_target_pairs={{0,32},{1,33},{2,34},{3,35},{4,36},{5,37},{6,38},{7,39},{8,40},{9,... | collective-permute-start | bytes 1966088 | tf_op jit(solution)/shard_map/ppermute | solution.py:39

commit v3 on v2

v3 whole, which is shorter than its diff:
```python
import functools
import math

import jax
import jax.numpy as jnp
from jax import lax
from jax.experimental import pallas as pl
from jax.experimental.pallas import tpu as pltpu
from jax.sharding import Mesh, PartitionSpec as P

AXES = ("xl", "core", "y", "xh", "z")
SIZES = (2, 2, 4, 2, 4)
RING = ("xl", "y", "xh", "z")

ROWS = 16
CELLS = 32
SLOTS = 48
BASIS = 9
CHAN = 256
HALF = 128
BAND = 5
KEEP = 40
bf16 = jnp.bfloat16
f32 = jnp.float32


def moves(lat=False, core=False, lon=(0, 0)):
    pairs = []
    for xl in range(2):
        for c in range(2):
            for cell in range(32):
                source = (xl * 2 + c) * 32 + cell
                row = (xl ^ int(lat)) * 2 + (c ^ int(core))
                pairs.append((source, row * 32 + (cell + lon[c]) % 32))
    return pairs


def send(x, **way):
    return lax.ppermute(x, AXES, moves(**way))


def vmem(count):
    return [pl.BlockSpec(memory_space=pltpu.VMEM)] * count


HBM = pl.BlockSpec(memory_space=pltpu.HBM)


def mark(token):
    token[...] = jnp.zeros(token.shape, f32)


TOKEN = ((8, 128), jnp.float32)


def here():
    return lax.axis_index("xl"), lax.axis_index("core")


def call(kernel, outs, operands, scratch=(), flops=0, traffic=0, limit=24, hbm=(), to=(), alias=None):
    return pl.pallas_call(
        kernel,
        out_shape=[jax.ShapeDtypeStruct(*o) for o in outs],
        in_specs=[HBM if i in hbm else vmem(1)[0] for i in range(len(operands))],
        out_specs=[HBM if i in to else vmem(1)[0] for i in range(len(outs))],
        scratch_shapes=list(scratch),
        input_output_aliases=alias or {},
        compiler_params=pltpu.CompilerParams(vmem_limit_bytes=limit * 1024 * 1024),
        cost_estimate=pl.CostEstimate(flops=flops, bytes_accessed=traffic, transcendentals=0),
    )(*operands)


def column_kernel(f_in, fx, c_in, cx, fo, co, edge):
    _, core = here()
    fo[...] = f_in[...]
    co[...] = c_in[...]
    for side in range(2):

        @pl.when(core == side)
        def _():
            cells = slice(CELLS - 2, CELLS) if side == 0 else slice(0, 2)
            for f, pair in enumerate(((f_in, fx), (c_in, cx))):
                for part, ref in enumerate(pair):
                    edge[f, part * ROWS : (part + 1) * ROWS] = ref[:, cells, :]


def boundary(xl, core):
    return [
        ((xl == side) & (core == (1 - side if part == 0 else side)), part, 14 * (1 - side))
        for side in range(2)
        for part in range(2)
    ]


def rows_of(part, first, count):
    return [slice(p * ROWS + first, p * ROWS + first + count) for p in (part, 1 - part)]


def row_kernel(fo, fx, co, cx, near, far, to, tx, after, rows):
    xl, core = here()
    rows[:, :, 36:SLOTS, :] = jnp.zeros((2, 2, SLOTS - 36, CHAN), bf16)
    for chosen, part, first in boundary(xl, core):

        @pl.when(chosen)
        def _():
            span = slice(first, first + 2)
            side, cross = rows_of(part, first, 2)
            for f, pair in enumerate(((fo, fx), (co, cx))):
                rows[f, :, 0:CELLS, :] = pair[part][span]
                rows[f, :, CELLS : CELLS + 2, :] = near[f, side]
                rows[f, :, CELLS + 2 : CELLS + 4, :] = far[f, cross]
            rows[1, 0, SLOTS - 2 : SLOTS, :] = (to, tx)[part][span]


def padded(dst, f, xl, core, own, other, near, far, rows, lanes):
    width = dst.shape[-1]
    dst[:, 36:SLOTS, :] = jnp.zeros((36, SLOTS - 36, width), bf16)
    for part, ref in enumerate((own, other)):
        at = pl.ds(2 + ROWS * (core if part == 0 else 1 - core), ROWS)
        side, cross = rows_of(part, 0, ROWS)
        dst[at, 0:CELLS, :] = ref[:, :, lanes]
        dst[at, CELLS : CELLS + 2, :] = near[f, side, :, lanes]
        dst[at, CELLS + 2 : CELLS + 4, :] = far[f, cross, :, lanes]
    if rows is None:
        dst[0:2] = jnp.zeros((2, SLOTS, width), bf16)
        dst[34:36] = jnp.zeros((2, SLOTS, width), bf16)
    else:
        dst[pl.ds(34 * (1 - xl), 2), 0:36, :] = rows[f, :, 0:36, lanes]
        dst[pl.ds(34 * xl, 2)] = jnp.zeros((2, SLOTS, width), bf16)


def over(index, divisor):
    return ((index.astype(f32) + 0.5) * (1.0 / divisor)).astype(jnp.int32)


def split_taps(index):
    k = over(index, 25)
    tap = index - 25 * k
    b = over(tap, 5)
    return k, b, tap - 5 * b


def iota(shape, axis):
    return lax.broadcasted_iota(jnp.int32, shape, axis)


def band_masks(lanes):
    _, core = here()
    cell = iota((CELLS, lanes), 0)
    lane = iota((CELLS, lanes), 1)
    slot = lane - SLOTS * over(lane, SLOTS)
    side = jnp.where(slot < CELLS + 2, slot - 34 * (1 - core), slot - 2 - 34 * core)
    place = jnp.where(slot < CELLS, slot, jnp.where(slot < CELLS + 4, side, 1000))
    return [(place - cell + 2) == s for s in range(BAND)]


def band(block, masks, lanes, row):
    total = jnp.zeros((CELLS, lanes), f32)
    for s in range(BAND):
        line = block[pl.ds(row, 1), s * lanes : (s + 1) * lanes]
        total = jnp.where(masks[s], jnp.broadcast_to(line, (CELLS, lanes)), total)
    return total.astype(bf16)


def one_hot(row, group, offset, count, total):
    column = iota((total, count), 1)
    return (over(row, group) == column + offset).astype(f32).astype(bf16)


def spread(rep, keep, row_key, lanes, inner):
    lane = iota((1, BAND * lanes), 1)
    s = over(lane, lanes)
    o = over(lane - lanes * s, SLOTS)
    lane_key = jnp.where(o < inner, o * BAND + s, -2)
    table = jnp.where(row_key == lane_key, 1.0, 0.0).astype(bf16)
    kept = jnp.where(keep, rep, 0.0).astype(bf16)
    return jnp.dot(kept, table, preferred_element_type=f32)


def band_table():
    lane = iota((1, BAND * CHAN), 1)
    s = over(lane, CHAN)
    b = over(lane - CHAN * s, SLOTS)
    key = jnp.where(b < BAND, b * BAND + s, -1)
    return jnp.where(iota((25, 1), 0) == key, 1.0, 0.0).astype(bf16)


def tap_lines(taps, lines):
    lines[...] = jnp.dot(
        taps[...].reshape(BASIS * ROWS, 25), band_table(), preferred_element_type=f32
    )


def all_bands(taps, bands, lines):
    tap_lines(taps, lines)
    masks = band_masks(CHAN)

    def step(n, carry):
        for k in range(BASIS):
            line = band(lines, masks, CHAN, k * ROWS + n)
            bands[n, k * CELLS : (k + 1) * CELLS, :] = line
        return carry

    lax.fori_loop(0, ROWS, step, 0, unroll=4)


def own_kernel(start, length, taps, after, masked, flat, bands, lines):
    xl, core = here()
    square = iota((ROWS, ROWS), 0) == iota((ROWS, ROWS), 1)

    def upright(line):
        spread = jnp.where(square, jnp.broadcast_to(line.astype(f32), (ROWS, ROWS)), 0.0)
        return jnp.sum(spread, axis=1, keepdims=True)

    low = upright(start[...])
    high = low + upright(length[...])
    source = (xl * 2 + core) * ROWS + iota((ROWS, 25), 0) - 2 + over(iota((ROWS, 25), 1), BAND)
    source = source.astype(f32)
    inside = (source >= low) & (source < high)
    total = jnp.zeros((ROWS, CHAN), f32)
    for k in range(BASIS):
        part = jnp.where(inside, taps[k].astype(f32), 0.0).astype(bf16)
        masked[k] = part
        at = iota((25, CHAN), 1) == iota((25, CHAN), 0) + 25 * k
        total += jnp.dot(part, at.astype(f32).astype(bf16), preferred_element_type=f32)
    flat[...] = total.astype(bf16)
    all_bands(masked, bands, lines)


def other_kernel(mx, co, cx, after, bands, cot_t, token, lines):
    mark(token)
    all_bands(mx, bands, lines)
    cot_t[:, 0:512] = co[...].reshape(512, CHAN).T
    cot_t[:, 512:1024] = cx[...].reshape(512, CHAN).T


def weight_kernel(fo, fx, near, far, bo, bx, cot_t, grad, field, basis):
    xl, core = here()
    lanes = pl.ds(pl.multiple_of(core * HALF, HALF), HALF)
    padded(field, 0, xl, core, fo, fx, near, far, None, lanes)

    for part, bands in enumerate((bo, bx)):
        begin = ROWS * (core if part == 0 else 1 - core)

        def step(n, carry):
            window = field[pl.ds(begin + n, BAND)].reshape(BAND * SLOTS, HALF)
            out = jnp.dot(
                bands[n, :, 0 : BAND * SLOTS], window, preferred_element_type=f32
            ).astype(bf16)
            at = pl.ds(pl.multiple_of((part * ROWS + n) * CELLS, CELLS), CELLS)
            for k in range(BASIS):
                basis[at, k * HALF : (k + 1) * HALF] = out[k * CELLS : (k + 1) * CELLS]
            return carry

        lax.fori_loop(0, ROWS, step, 0, unroll=16)
    for chosen, part, first in boundary(xl, core):

        @pl.when(chosen)
        def _():
            at = (part * ROWS + first) * CELLS
            basis[at : at + 2 * CELLS, :] = jnp.zeros((2 * CELLS, BASIS * HALF), bf16)

    total = jnp.dot(cot_t[...], basis[...], preferred_element_type=f32)
    for k in range(BASIS):
        grad[k] = total[:, k * HALF : (k + 1) * HALF]


def runs(k, side):
    begin, at = side * 144 + k * 16, 0
    while at < 16:
        s, j = divmod(begin + at, 64)
        count = min(16 - at, 64 - j)
        yield at, s * 8, j, count
        at += count


def weight_end_kernel(
    fo, fx, co, cx, near, far, rows, bo, bx, grad, parts, token, field, cot, tile
):
    mark(token)
    xl, core = here()
    lanes = pl.ds(pl.multiple_of(core * HALF, HALF), HALF)
    field[:, 36:SLOTS, :] = jnp.zeros((6, SLOTS - 36, HALF), bf16)
    field[pl.ds(4 * (1 - xl), 2), 0:36, :] = rows[0, :, 0:36, lanes]
    for chosen, part, first in boundary(xl, core):

        @pl.when(chosen)
        def _():
            ref = (fo, fx)[part]
            at = 2 if first == 0 else 0
            begin = 0 if first == 0 else 12
            side, cross = rows_of(part, begin, 4)
            field[at : at + 4, 0:CELLS, :] = ref[begin : begin + 4, :, lanes]
            field[at : at + 4, CELLS : CELLS + 2, :] = near[0, side, :, lanes]
            field[at : at + 4, CELLS + 2 : CELLS + 4, :] = far[0, cross, :, lanes]
            cot[...] = (co, cx)[part][first : first + 2].reshape(2 * CELLS, CHAN).T
            tile[...] = (bo, bx)[part][first : first + 2]

    basis = []
    for r in range(2):
        window = field[r : r + BAND].reshape(BAND * SLOTS, HALF)
        basis.append(
            jnp.dot(tile[r, :, 0 : BAND * SLOTS], window, preferred_element_type=f32).astype(bf16)
        )
    parts[:, 32:KEEP, :] = jnp.zeros((64, 8, HALF), bf16)
    for k in range(BASIS):
        cells = jnp.concatenate([x[k * CELLS : (k + 1) * CELLS] for x in basis], 0)
        total = (grad[k] + jnp.dot(cot[...], cells, preferred_element_type=f32)).T
        for side in range(2):
            tiles = total[:, side * HALF : (side + 1) * HALF].reshape(16, 8, HALF).astype(bf16)
            for at, s, j, count in runs(k, side):
                parts[j : j + count, s : s + 8, :] = tiles[at : at + count]


def sum_kernel(scale, parts, after, out, token):
    mark(token)
    total = jnp.sum(parts[...].astype(f32), axis=0) * scale
    out[...] = jnp.broadcast_to(total.astype(bf16)[None], out.shape)


def half_kernel(half_of, tiles_ref, out, stage, sems):
    first = pl.multiple_of(half_of() * HALF, HALF)
    copies = []
    for k in range(BASIS):
        for side in range(2):
            for at, s, j, count in runs(k, side):
                tiles = tiles_ref[j : j + count, s : s + 8, :].astype(f32)
                stage[k, at * 8 : (at + count) * 8, side * HALF : (side + 1) * HALF] = (
                    tiles.reshape(count * 8, HALF)
                )
        copies.append(
            pltpu.make_async_copy(stage.at[k], out.at[k, pl.ds(first, HALF), :], sems.at[k])
        )
        copies[-1].start()
    for copy in copies:
        copy.wait()


def own_half_kernel(mine, out, stage, sems):
    half_kernel(lambda: here()[1], mine, out, stage, sems)


def other_half_kernel(theirs, before, out, stage, sems):
    half_kernel(lambda: 1 - here()[1], theirs, out, stage, sems)


def mixed_kernel(
    fo, fx, near, far, rows, mo, w_hbm, after, out, token, field, basis, weight, bands, lines, sems
):
    mark(token)
    xl, core = here()
    copy = pltpu.make_async_copy(w_hbm, weight, sems)
    copy.start()
    padded(field, 0, xl, core, fo, fx, near, far, rows, slice(None))
    tap_lines(mo, lines)
    masks = band_masks(CHAN)
    for n in range(ROWS):
        for k in range(BASIS):
            line = band(lines, masks, CHAN, k * ROWS + n)
            bands[n, k * CELLS : (k + 1) * CELLS, :] = line
        window = field[pl.ds(core * ROWS + n, BAND)].reshape(BAND * SLOTS, CHAN)
        part = jnp.dot(
            bands[n, :, 0 : BAND * SLOTS], window, preferred_element_type=f32
        ).astype(bf16)
        for k in range(BASIS):
            basis[n * CELLS : (n + 1) * CELLS, k * CHAN : (k + 1) * CHAN] = part[
                k * CELLS : (k + 1) * CELLS
            ]
    copy.wait()
    out[...] = (
        jnp.dot(basis[...], weight[...], preferred_element_type=f32)
        .astype(bf16)
        .reshape(ROWS, CELLS, CHAN)
    )


def feature_kernel(
    co, cx, near, far, rows, to, tx, w_hbm, after, out, token, field, lines, grads, bands, total,
    weight, sems
):
    mark(token)
    copy = pltpu.make_async_copy(w_hbm, weight, sems)
    copy.start()
    xl, core = here()
    lanes = 512
    around = ROWS + 4
    padded(field, 1, xl, core, co, cx, near, far, rows, slice(None))

    count = around * 8
    row = iota((count, 1), 0)
    beyond = 34 * (1 - xl) - core * ROWS
    other = 2 + (1 - 2 * core) * ROWS
    rep = jnp.dot(one_hot(row, 8, 2, 16, count), to[...], preferred_element_type=f32)
    rep += jnp.dot(one_hot(row, 8, other, 16, count), tx[...], preferred_element_type=f32)
    rep += jnp.dot(
        one_hot(row, 8, beyond, 2, count),
        rows[1, 0, SLOTS - 2 : SLOTS, :],
        preferred_element_type=f32,
    )
    _, b, _ = split_taps(iota((1, CHAN), 1))
    k, _, s = split_taps(iota((CHAN, 1), 0))
    lines[...] = spread(rep, b == row - 8 * over(row, 8), k * BAND + 4 - s, lanes, BASIS)
    masks = band_masks(lanes)
    copy.wait()
    for k in range(BASIS):
        for h in range(2):
            upstream = field[pl.ds(core * ROWS + h * 10, 10)].reshape(10 * SLOTS, CHAN)
            back = lax.dot_general(
                upstream,
                weight[k * CHAN : (k + 1) * CHAN, :],
                (((1,), (1,)), ((), ())),
                preferred_element_type=f32,
            )
            grads[h * 10 : (h + 1) * 10, k * SLOTS : (k + 1) * SLOTS, :] = back.astype(
                bf16
            ).reshape(10, SLOTS, CHAN)
    total[...] = jnp.zeros_like(total)

    def step(i, carry):
        for b in range(BAND):
            bands[b * CELLS : (b + 1) * CELLS, :] = band(lines, masks, lanes, i * 8 + b)
        part = jnp.dot(
            bands[:, 0 : BASIS * SLOTS], grads[i], preferred_element_type=f32
        ).reshape(BAND, CELLS, CHAN)
        total[pl.ds(i, BAND)] += part
        return carry

    lax.fori_loop(0, around, step, 0, unroll=4)
    out[...] = total[4 : 4 + ROWS].astype(bf16)


def shards(feature, filters, start, length, weight, cotangent):
    fx = send(feature, core=True)
    cx = send(cotangent, core=True)
    block = ((ROWS, CELLS, CHAN), bf16)
    taps = ((BASIS, ROWS, 25), bf16)
    tiles = ((ROWS, BASIS * CELLS, CHAN), bf16)
    lines = pltpu.VMEM((BASIS * ROWS, BAND * CHAN), f32)
    fo, co, edge = call(
        column_kernel,
        [block, block, ((2, 2 * ROWS, 2, CHAN), bf16)],
        (feature, fx, cotangent, cx),
        traffic=2**20,
        limit=8,
    )
    near = send(edge, lon=(1, -1))

    mo, to, bo = call(
        own_kernel,
        [taps, ((ROWS, CHAN), bf16), tiles],
        (start.reshape(1, ROWS), length.reshape(1, ROWS), filters.transpose(1, 0, 2), edge),
        scratch=[lines],
        flops=2 * 144 * 256 * 1280,
        traffic=4 * 2**20,
        limit=16,
    )
    mx = send(mo, core=True)
    tx = send(to, core=True)
    bx, cot_t, after = call(
        other_kernel,
        [tiles, ((CHAN, 1024), bf16), TOKEN],
        (mx, co, cx, edge),
        scratch=[lines],
        flops=2 * 144 * 256 * 1280,
        traffic=4 * 2**20,
        limit=16,
    )
    near, bx = lax.optimization_barrier((near, bx))
    far = send(near, core=True)
    halo = (near, far)

    (rows,) = call(
        row_kernel,
        [((2, 2, SLOTS, CHAN), bf16)],
        (fo, fx, co, cx, *halo, to, tx, after),
        traffic=2**20,
    )
    rows = send(rows, lat=True)
    (grad,) = call(
        weight_kernel,
        [((BASIS, CHAN, HALF), f32)],
        (fo, fx, *halo, bo, bx, cot_t),
        scratch=[
            pltpu.VMEM((36, SLOTS, HALF), bf16),
            pltpu.VMEM((1024, BASIS * HALF), bf16),
        ],
        flops=2 * 32 * 288 * 256 * 256 + 2 * 1024 * 1152 * 256,
        traffic=7 * 2**20,
    )
    parts, after = call(
        weight_end_kernel,
        [((64, KEEP, HALF), bf16), TOKEN],
        (fo, fx, co, cx, *halo, rows, bo, bx, grad),
        scratch=[
            pltpu.VMEM((6, SLOTS, HALF), bf16),
            pltpu.VMEM((CHAN, 2 * CELLS), bf16),
            pltpu.VMEM((2, BASIS * CELLS, CHAN), bf16),
        ],
        flops=2 * 64 * 1152 * 256,
        traffic=3 * 2**20,
    )
    mixing = weight.reshape(BASIS * CHAN, CHAN)

    swapped = lax.all_to_all(parts, RING, 0, 0, tiled=True)
    mixed, after = call(
        mixed_kernel,
        [block, TOKEN],
        (feature, fx, *halo, rows, mo, mixing, after),
        scratch=[
            pltpu.VMEM((36, SLOTS, CHAN), bf16),
            pltpu.VMEM((512, BASIS * CHAN), bf16),
            pltpu.VMEM((BASIS * CHAN, CHAN), bf16),
            pltpu.VMEM((ROWS, BASIS * CELLS, CHAN), bf16),
            lines,
            pltpu.SemaphoreType.DMA,
        ],
        hbm=(6,),
        flops=2 * 16 * 288 * 256 * 256 + 2 * 512 * 2304 * 256,
        traffic=8 * 2**20,
    )
    shared, after = call(
        functools.partial(sum_kernel, 1.0 / math.sqrt(64 * 1024)),
        [((64, KEEP, HALF), bf16), TOKEN],
        (swapped, after),
        traffic=2**20,
    )

    mine = lax.all_to_all(shared, RING, 0, 0, tiled=True)
    grad_feature, after = call(
        feature_kernel,
        [block, TOKEN],
        (cotangent, cx, *halo, rows, to, tx, mixing, after),
        scratch=[
            pltpu.VMEM((36, SLOTS, CHAN), bf16),
            pltpu.VMEM(((ROWS + 4) * 8, BAND * 512), f32),
            pltpu.VMEM((ROWS + 4, BASIS * SLOTS, CHAN), bf16),
            pltpu.VMEM((BAND * CELLS, 512), bf16),
            pltpu.VMEM((ROWS + 8, CELLS, CHAN), f32),
            pltpu.VMEM((BASIS * CHAN, CHAN), bf16),
            pltpu.SemaphoreType.DMA,
        ],
        hbm=(7,),
        flops=2 * 960 * 2304 * 256 + 2 * 20 * 160 * 512 * 256,
        traffic=8 * 2**20,
    )
    mine, grad_feature = lax.optimization_barrier((mine, grad_feature))
    theirs = send(mine, core=True)
    whole = ((BASIS, CHAN, CHAN), f32)
    stage = [pltpu.VMEM((BASIS, HALF, CHAN), f32), pltpu.SemaphoreType.DMA((BASIS,))]
    (grad_weight,) = call(
        own_half_kernel, [whole], (mine,), scratch=stage, to=(0,), traffic=2 * 2**20, limit=8
    )
    (grad_weight,) = call(
        other_half_kernel,
        [whole],
        (theirs, grad_weight),
        scratch=stage,
        hbm=(1,),
        to=(0,),
        alias={1: 0},
        traffic=2 * 2**20,
        limit=8,
    )
    return (mixed, grad_feature, grad_weight)


def solution(mesh):
    fine = Mesh(mesh.devices.reshape(SIZES), AXES)
    lat, lon = ("xl", "core"), ("y", "xh", "z")
    return jax.shard_map(
        shards,
        mesh=fine,
        in_specs=(P(lat, lon, None), P(lat, None, None), P(lat), P(lat), P(), P(lat, lon, None)),
        out_specs=(P(lat, lon, None), P(lat, lon, None), P()),
        check_vma=False,
    )
```

time: 81.7 us -> 71.1 us (0.87)
  Pallas kernels: 31.2 us -> 20.1 us
  waiting for transfers between devices: 11 us -> 19.3 us
  local copies, waits for them, and re-layouts: 8 us -> 3.99 us
  starting transfers between devices: 28.6 us -> 26.3 us
  other arithmetic: 1.5 us -> 0 us
    pallas_call x9 -> x11, Pallas kernels: 31.2 us -> 20.1 us  [call(): pl.pallas_call(kernel, out_shape=[jax.ShapeDtypeStruct(*o) for o in outs]...]
    unnamed x21 -> x16, local copies, waits for them, and re-layouts: 7.88 us -> 3.99 us
    all_to_all x1, waiting for transfers between devices: 5.01 us -> 8.29 us  [shards(): swapped = lax.all_to_all(parts, RING, 0, 0, tiled=True)]
    ppermute x9 -> x8, waiting for transfers between devices: 2.72 us -> 5.72 us  [send(): return lax.ppermute(x, AXES, moves(**way))]
    all_to_all x1, starting transfers between devices: 7.34 us -> 4.64 us  [shards(): swapped = lax.all_to_all(parts, RING, 0, 0, tiled=True)]
    all_to_all x1, waiting for transfers between devices: 3.29 us -> 5.33 us  [shards(): mine = lax.all_to_all(shared, RING, 0, 0, tiled=True)]
    ppermute x9 -> x8, starting transfers between devices: 15.7 us -> 15.3 us  [send(): return lax.ppermute(x, AXES, moves(**way))]
  transfers between devices with their start and end apart: 11 -> 10, of which waited for: 5 -> 8; matrix products, arithmetic and copies ran while one was open for 3% -> 0% of each run, Pallas kernels for 31% -> 23%
where the time goes in v3:
time: 71.1 us; the launch traced here: 70.7 us
  starting transfers between devices  26.3 us (37%)
  Pallas kernels  20.1 us (28%)
  waiting for transfers between devices  19.3 us (27%)
  local copies, waits for them, and re-layouts  3.99 us (6%)
  between operations  0.94 us (1%)
    pallas_call x11, Pallas kernels, call(): pl.pallas_call(kernel, out_shape=[jax.ShapeDtypeStruct(*o) for o in outs]...  20.1 us
    ppermute x8, starting transfers between devices, send(): return lax.ppermute(x, AXES, moves(**way))  15.3 us
    all_to_all x1, waiting for transfers between devices, shards(): swapped = lax.all_to_all(parts, RING, 0, 0, tiled=True)  8.29 us
    all_to_all x1, starting transfers between devices, shards(): mine = lax.all_to_all(shared, RING, 0, 0, tiled=True)  6.38 us
    ppermute x8, waiting for transfers between devices, send(): return lax.ppermute(x, AXES, moves(**way))  5.72 us
    all_to_all x1, waiting for transfers between devices, shards(): mine = lax.all_to_all(shared, RING, 0, 0, tiled=True)  5.33 us
    all_to_all x1, starting transfers between devices, shards(): swapped = lax.all_to_all(parts, RING, 0, 0, tiled=True)  4.64 us
    unnamed x16, local copies, waits for them, and re-layouts  3.99 us
  transfers between devices with their start and end apart: 10, of which 8 were waited for; matrix products, arithmetic and copies ran while one was open for 0% of the time, Pallas kernels for 23%

profile of v3, /device:TPU:1, one launch (start us, length us, event | category | flops | bytes accessed | tf_op | source)
XLA Modules:
  0.0 70.7 jit_solution(3572496119604864510)
XLA Ops:
  0.6 1.5 %collective-permute-start = (bf16[16,32,256]{2,1,0:T(8,128)(2,1)}, bf16[16,32,256]{2,1,0:T(8,128)(2,1)S(1)}, u32[]{:S(2)}, u32[]{:S(2)}) collective-permute-start(bf16[16,32,256]{2,1,0:T(8,128)(2,1)} %fo.1), channel_id=1, source_target_pairs={{0,32},{1,33},{2,34},{3,35},{4,36},{5,37},{6,38},{7,39},{8,40},{9,... | collective-permute-start | bytes 786440 | tf_op jit(solution)/shard_map/ppermute | solution.py:39
  2.1 0.1 collective-permute-start.1
  2.2 1.3 %collective-permute-done.fx = bf16[16,32,256]{2,1,0:T(8,128)(2,1)S(1)} collective-permute-done((bf16[16,32,256]{2,1,0:T(8,128)(2,1)}, bf16[16,32,256]{2,1,0:T(8,128)(2,1)S(1)}, u32[]{:S(2)}, u32[]{:S(2)}) %collective-permute-start) | collective-permute-done | bytes 262176 | tf_op jit(solution)/shard_map/ppermute | solution.py:39
  3.5 0.4 collective-permute-done.1.cx
  3.9 0.0 copy-start
  3.9 0.9 %copy-done = bf16[16,32,256]{2,1,0:T(8,128)(2,1)S(1)} copy-done((bf16[16,32,256]{2,1,0:T(8,128)(2,1)S(1)}, bf16[16,32,256]{2,1,0:T(8,128)(2,1)}, u32[]{:S(2)}) %copy-start) | copy-done | bytes 262168
  4.8 0.0 copy-start.2
  4.8 0.9 %copy-done.2 = bf16[16,32,256]{2,1,0:T(8,128)(2,1)S(1)} copy-done((bf16[16,32,256]{2,1,0:T(8,128)(2,1)S(1)}, bf16[16,32,256]{2,1,0:T(8,128)(2,1)}, u32[]{:S(2)}) %copy-start.2) | copy-done | bytes 262168
  5.8 0.1 shard_map.85
  5.9 8.8 %collective-permute-start.2 = (bf16[2,32,2,256]{3,2,1,0:T(2,128)(2,1)S(1)}, bf16[2,32,2,256]{3,2,1,0:T(2,128)(2,1)S(1)}, u32[]{:S(2)}, u32[]{:S(2)}) collective-permute-start(bf16[2,32,2,256]{3,2,1,0:T(2,128)(2,1)S(1)} %get-tuple-element.23.after), channel_id=1, source_target_pairs={{0,1},{1,2},{2,3},{3,4},{4,5},{5,6},{6,7},{7,8},{8,9},{9,10},{10,1... | collective-permute-start | bytes 196616 | tf_op jit(solution)/shard_map/ppermute | solution.py:39
  14.7 0.0 copy-start.5
  14.7 0.8 %copy-done.5 = bf16[16,9,25]{2,0,1:T(8,128)(2,1)S(1)} copy-done((bf16[16,9,25]{2,0,1:T(8,128)(2,1)S(1)}, bf16[16,9,25]{2,0,1:T(8,128)(2,1)}, u32[]{:S(2)}) %copy-start.5) | copy-done | bytes 7224
  15.5 0.0 copy-start.6
  15.5 0.7 copy-done.6
  16.1 0.0 copy-start.7
  16.1 0.7 copy-done.7
  16.8 1.7 %shard_map.86 = (bf16[9,16,25]{2,1,0:T(8,128)(2,1)S(1)}, bf16[16,256]{1,0:T(8,128)(2,1)S(1)}, bf16[16,288,256]{2,1,0:T(8,128)(2,1)S(1)}) custom-call(s32[1,16]{1,0:T(1,128)S(1)} %bitcast.7, s32[1,16]{1,0:T(1,128)S(1)} %bitcast.8, bf16[9,16,25]{2,1,0:T(8,128)(2,1)S(1)} %bitcast.6, bf16[2,32,2,256]{3,2,1,0:T(2,128)(2,1)S(1)} %get-tuple-element.23.after), custom_call_target="tpu_custom_call" | custom-call | flops 94371840 | bytes 4194304 | tf_op jit(solution)/shard_map/pallas_call | solution.py:61
  18.5 0.1 collective-permute-start.3
  18.6 1.2 %collective-permute-done.3.mx = bf16[9,16,25]{2,1,0:T(8,128)(2,1)S(1)} collective-permute-done((bf16[9,16,25]{2,1,0:T(8,128)(2,1)S(1)}, bf16[9,16,25]{2,1,0:T(8,128)(2,1)S(1)}, u32[]{:S(2)}, u32[]{:S(2)}) %collective-permute-start.3) | collective-permute-done | bytes 7232 | tf_op jit(solution)/shard_map/ppermute | solution.py:39
  19.8 1.8 %shard_map.87 = (bf16[16,288,256]{2,1,0:T(8,128)(2,1)S(1)}, bf16[256,1024]{1,0:T(8,128)(2,1)S(1)}, f32[8,128]{1,0:T(8,128)S(1)}) custom-call(bf16[9,16,25]{2,1,0:T(8,128)(2,1)S(1)} %collective-permute-done.3.mx, bf16[16,32,256]{2,1,0:T(8,128)(2,1)S(1)} %get-tuple-element.25.co, bf16[16,32,256]{2,1,0:T(8,128)(2,1)S(1)} %collective-permute-done.1.cx, ...), custom_call_target="tpu_custom_call" | custom-call | flops 94371840 | bytes 4194304 | tf_op jit(solution)/shard_map/pallas_call | solution.py:61
  21.7 0.0 collective-permute-done.2.near
  21.7 0.2 collective-permute-start.4
  21.9 0.3 collective-permute-start.5
  22.3 0.8 %collective-permute-done.5.tx = bf16[16,256]{1,0:T(8,128)(2,1)S(1)} collective-permute-done((bf16[16,256]{1,0:T(8,128)(2,1)S(1)}, bf16[16,256]{1,0:T(8,128)(2,1)S(1)}, u32[]{:S(2)}, u32[]{:S(2)}) %collective-permute-start.5) | collective-permute-done | bytes 8224 | tf_op jit(solution)/shard_map/ppermute | solution.py:39
  23.1 0.0 collective-permute-done.4.far
  23.1 0.4 collective-permute-start.6
  23.5 2.3 %shard_map.89.grad = f32[9,256,128]{2,1,0:T(8,128)S(1)} custom-call(bf16[16,32,256]{2,1,0:T(8,128)(2,1)S(1)} %get-tuple-element.28.fo, bf16[16,32,256]{2,1,0:T(8,128)(2,1)S(1)} %collective-permute-done.fx, bf16[2,32,2,256]{3,2,1,0:T(2,128)(2,1)S(1)} %collective-permute-done.2.near, bf16[2,32,2,256]{3,2,1,0:T(2,128)(2,1)S(1)} %collective-permute-done.4.far, ...), custom_call_target="tpu_custom_call" | custom-call | flops 1811939328 | bytes 7340032 | tf_op jit(solution)/shard_map/pallas_call | solution.py:61
  25.8 0.0 copy-start.1
  25.8 0.0 copy-start.4
  25.8 1.4 %collective-permute-done.6.rows = bf16[2,2,48,256]{3,2,1,0:T(8,128)(2,1)S(1)} collective-permute-done((bf16[2,2,48,256]{3,2,1,0:T(8,128)(2,1)S(1)}, bf16[2,2,48,256]{3,2,1,0:T(8,128)(2,1)S(1)}, u32[]{:S(2)}, u32[]{:S(2)}) %collective-permute-start.6) | collective-permute-done | bytes 98336 | tf_op jit(solution)/shard_map/ppermute | solution.py:39
  27.2 1.5 %shard_map.90 = (bf16[64,40,128]{2,1,0:T(8,128)(2,1)}, f32[8,128]{1,0:T(8,128)S(1)}) custom-call(bf16[16,32,256]{2,1,0:T(8,128)(2,1)S(1)} %get-tuple-element.28.fo, bf16[16,32,256]{2,1,0:T(8,128)(2,1)S(1)} %collective-permute-done.fx, bf16[16,32,256]{2,1,0:T(8,128)(2,1)S(1)} %get-tuple-element.25.co, bf16[16,32,256]{2,1,0:T(8,128)(2,1)S(1)} %collective-permute-done.1.cx, ...), custom_call_target="tpu_custom_call" | custom-call | flops 37748736 | bytes 3145728 | tf_op jit(solution)/shard_map/pallas_call | solution.py:61
  28.7 4.6 %all-to-all-start = ((bf16[64,40,128]{2,1,0:T(8,128)(2,1)}), bf16[64,40,128]{2,1,0:T(8,128)(2,1)S(1)}, u32[]{:S(2)}, u32[]{:S(2)}) async-start(bf16[64,40,128]{2,1,0:T(8,128)(2,1)} %get-tuple-element.36), calls=%async_computation | async-start | bytes 1310720 | tf_op jit(solution)/shard_map/all_to_all | solution.py:504
  33.4 0.0 copy-done.1
  33.4 0.0 copy-done.4
  33.4 0.0 copy-start.3
  33.4 3.7 %shard_map.91 = (bf16[16,32,256]{2,1,0:T(8,128)(2,1)}, f32[8,128]{1,0:T(8,128)S(1)}) custom-call(bf16[16,32,256]{2,1,0:T(8,128)(2,1)S(1)} %copy-done.1, bf16[16,32,256]{2,1,0:T(8,128)(2,1)S(1)} %collective-permute-done.fx, bf16[2,32,2,256]{3,2,1,0:T(2,128)(2,1)S(1)} %collective-permute-done.2.near, bf16[2,32,2,256]{3,2,1,0:T(2,128)(2,1)S(1)} %collective-permute-done.4.far, ...), custom_call_target="tpu_custom_call" | custom-call | flops 1207959552 | bytes 8388608 | tf_op jit(solution)/shard_map/pallas_call | solution.py:61
  37.1 8.3 %all-to-all-done.parts = bf16[64,40,128]{2,1,0:T(8,128)(2,1)S(1)} async-done(((bf16[64,40,128]{2,1,0:T(8,128)(2,1)}), bf16[64,40,128]{2,1,0:T(8,128)(2,1)S(1)}, u32[]{:S(2)}, u32[]{:S(2)}) %all-to-all-start) | async-done | bytes 655392 | tf_op jit(solution)/shard_map/all_to_all | solution.py:504
  45.4 1.0 %shard_map.92 = (bf16[64,40,128]{2,1,0:T(8,128)(2,1)}, f32[8,128]{1,0:T(8,128)S(1)}) custom-call(bf16[64,40,128]{2,1,0:T(8,128)(2,1)S(1)} %all-to-all-done.parts, f32[8,128]{1,0:T(8,128)S(1)} %get-tuple-element.37.after), custom_call_target="tpu_custom_call" | custom-call | bytes 1048576 | tf_op jit(solution)/shard_map/pallas_call | solution.py:61
  46.3 6.4 %all-to-all-start.1 = ((bf16[64,40,128]{2,1,0:T(8,128)(2,1)}), bf16[64,40,128]{2,1,0:T(8,128)(2,1)S(1)}, u32[]{:S(2)}, u32[]{:S(2)}) async-start(bf16[64,40,128]{2,1,0:T(8,128)(2,1)} %get-tuple-element.38), calls=%async_computation.1 | async-start | bytes 1310720 | tf_op jit(solution)/shard_map/all_to_all | solution.py:528
  52.7 0.0 copy-done.3
  52.7 5.8 %shard_map.93 = (bf16[16,32,256]{2,1,0:T(8,128)(2,1)}, f32[8,128]{1,0:T(8,128)}) custom-call(bf16[16,32,256]{2,1,0:T(8,128)(2,1)S(1)} %copy-done.3, bf16[16,32,256]{2,1,0:T(8,128)(2,1)S(1)} %collective-permute-done.1.cx, bf16[2,32,2,256]{3,2,1,0:T(2,128)(2,1)S(1)} %collective-permute-done.2.near, bf16[2,32,2,256]{3,2,1,0:T(2,128)(2,1)S(1)} %collective-permute-done.4.far, ...), custom_call_target="tpu_custom_call" | custom-call | flops 1971322880 | bytes 8388608 | tf_op jit(solution)/shard_map/pallas_call | solution.py:61
  58.6 5.3 %all-to-all-done.1.mine = bf16[64,40,128]{2,1,0:T(8,128)(2,1)S(1)} async-done(((bf16[64,40,128]{2,1,0:T(8,128)(2,1)}), bf16[64,40,128]{2,1,0:T(8,128)(2,1)S(1)}, u32[]{:S(2)}, u32[]{:S(2)}) %all-to-all-start.1) | async-done | bytes 655392 | tf_op jit(solution)/shard_map/all_to_all | solution.py:528
  63.9 3.8 %collective-permute-start.7 = (bf16[64,40,128]{2,1,0:T(8,128)(2,1)S(1)}, bf16[64,40,128]{2,1,0:T(8,128)(2,1)S(1)}, u32[]{:S(2)}, u32[]{:S(2)}) collective-permute-start(bf16[64,40,128]{2,1,0:T(8,128)(2,1)S(1)} %all-to-all-done.1.mine), channel_id=1, source_target_pairs={{0,32},{1,33},{2,34},{3,35},{4,36},{5,37},{6,38},{7,39},{8,40},{9,... | collective-permute-start | bytes 1966088 | tf_op jit(solution)/shard_map/ppermute | solution.py:39
  67.7 1.1 %shard_map.94.before = f32[9,256,256]{2,1,0:T(8,128)} custom-call(bf16[64,40,128]{2,1,0:T(8,128)(2,1)S(1)} %all-to-all-done.1.mine), custom_call_target="tpu_custom_call" | custom-call | bytes 2097152 | tf_op jit(solution)/shard_map/pallas_call | solution.py:61
  68.8 0.6 collective-permute-done.7.theirs
  69.5 1.1 %shard_map.95 = f32[9,256,256]{2,1,0:T(8,128)} custom-call(bf16[64,40,128]{2,1,0:T(8,128)(2,1)S(1)} %collective-permute-done.7.theirs, f32[9,256,256]{2,1,0:T(8,128)} %shard_map.94.before), custom_call_target="tpu_custom_call", output_to_operand_aliasing={{}: (1, {})} | custom-call | bytes 2097152 | tf_op jit(solution)/shard_map/pallas_call | solution.py:61
  (1 shorter events, 0.0 us)
Async XLA Ops:
  0.6 2.9 %collective-permute-start = (bf16[16,32,256]{2,1,0:T(8,128)(2,1)}, bf16[16,32,256]{2,1,0:T(8,128)(2,1)S(1)}, u32[]{:S(2)}, u32[]{:S(2)}) collective-permute-start(bf16[16,32,256]{2,1,0:T(8,128)(2,1)} %fo.1), channel_id=1, source_target_pairs={{0,32},{1,33},{2,34},{3,35},{4,36},{5,37},{6,38},{7,39},{8,40},{9,... | collective-permute-start | bytes 786440 | tf_op jit(solution)/shard_map/ppermute | solution.py:39
  2.1 1.7 %collective-permute-start.1 = (bf16[16,32,256]{2,1,0:T(8,128)(2,1)}, bf16[16,32,256]{2,1,0:T(8,128)(2,1)S(1)}, u32[]{:S(2)}, u32[]{:S(2)}) collective-permute-start(bf16[16,32,256]{2,1,0:T(8,128)(2,1)} %co.1), channel_id=1, source_target_pairs={{0,32},{1,33},{2,34},{3,35},{4,36},{5,37},{6,38},{7,39},{8,40},{9,... | collective-permute-start | bytes 786440 | tf_op jit(solution)/shard_map/ppermute | solution.py:39
  3.9 0.9 %copy-start = (bf16[16,32,256]{2,1,0:T(8,128)(2,1)S(1)}, bf16[16,32,256]{2,1,0:T(8,128)(2,1)}, u32[]{:S(2)}) copy-start(bf16[16,32,256]{2,1,0:T(8,128)(2,1)} %fo.1) | copy-start | bytes 786436
  4.8 0.9 %copy-start.2 = (bf16[16,32,256]{2,1,0:T(8,128)(2,1)S(1)}, bf16[16,32,256]{2,1,0:T(8,128)(2,1)}, u32[]{:S(2)}) copy-start(bf16[16,32,256]{2,1,0:T(8,128)(2,1)} %co.1) | copy-start | bytes 786436
  5.9 15.8 %collective-permute-start.2 = (bf16[2,32,2,256]{3,2,1,0:T(2,128)(2,1)S(1)}, bf16[2,32,2,256]{3,2,1,0:T(2,128)(2,1)S(1)}, u32[]{:S(2)}, u32[]{:S(2)}) collective-permute-start(bf16[2,32,2,256]{3,2,1,0:T(2,128)(2,1)S(1)} %get-tuple-element.23.after), channel_id=1, source_target_pairs={{0,1},{1,2},{2,3},{3,4},{4,5},{5,6},{6,7},{7,8},{8,9},{9,10},{10,1... | collective-permute-start | bytes 196616 | tf_op jit(solution)/shard_map/ppermute | solution.py:39
  14.7 0.8 %copy-start.5 = (bf16[16,9,25]{2,0,1:T(8,128)(2,1)S(1)}, bf16[16,9,25]{2,0,1:T(8,128)(2,1)}, u32[]{:S(2)}) copy-start(bf16[16,9,25]{2,0,1:T(8,128)(2,1)} %param.7) | copy-start | bytes 21604
  15.5 0.7 copy-start.6
  16.1 0.7 copy-start.7
  18.5 1.3 %collective-permute-start.3 = (bf16[9,16,25]{2,1,0:T(8,128)(2,1)S(1)}, bf16[9,16,25]{2,1,0:T(8,128)(2,1)S(1)}, u32[]{:S(2)}, u32[]{:S(2)}) collective-permute-start(bf16[9,16,25]{2,1,0:T(8,128)(2,1)S(1)} %get-tuple-element.24.mo), channel_id=1, source_target_pairs={{0,32},{1,33},{2,34},{3,35},{4,36},{5,37},{6,38},{7,39},{8,40},{9,... | collective-permute-start | bytes 21608 | tf_op jit(solution)/shard_map/ppermute | solution.py:39
  21.7 1.4 %collective-permute-start.4 = (bf16[2,32,2,256]{3,2,1,0:T(2,128)(2,1)S(1)}, bf16[2,32,2,256]{3,2,1,0:T(2,128)(2,1)S(1)}, u32[]{:S(2)}, u32[]{:S(2)}) collective-permute-start(bf16[2,32,2,256]{3,2,1,0:T(2,128)(2,1)S(1)} %collective-permute-done.2.near), channel_id=1, source_target_pairs={{0,32},{1,33},{2,34},{3,35},{4,36},{5,37},{6,38},{7,39},{8,40},{9,... | collective-permute-start | bytes 196616 | tf_op jit(solution)/shard_map/ppermute | solution.py:39
  21.9 1.2 %collective-permute-start.5 = (bf16[16,256]{1,0:T(8,128)(2,1)S(1)}, bf16[16,256]{1,0:T(8,128)(2,1)S(1)}, u32[]{:S(2)}, u32[]{:S(2)}) collective-permute-start(bf16[16,256]{1,0:T(8,128)(2,1)S(1)} %get-tuple-element.29.to), channel_id=1, source_target_pairs={{0,32},{1,33},{2,34},{3,35},{4,36},{5,37},{6,38},{7,39},{8,40},{9,... | collective-permute-start | bytes 24584 | tf_op jit(solution)/shard_map/ppermute | solution.py:39
  23.1 4.1 %collective-permute-start.6 = (bf16[2,2,48,256]{3,2,1,0:T(8,128)(2,1)S(1)}, bf16[2,2,48,256]{3,2,1,0:T(8,128)(2,1)S(1)}, u32[]{:S(2)}, u32[]{:S(2)}) collective-permute-start(bf16[2,2,48,256]{3,2,1,0:T(8,128)(2,1)S(1)} %shard_map.88), channel_id=1, source_target_pairs={{0,64},{1,65},{2,66},{3,67},{4,68},{5,69},{6,70},{7,71},{8,72},{9,... | collective-permute-start | bytes 294920 | tf_op jit(solution)/shard_map/ppermute | solution.py:39
  25.8 7.6 %copy-start.1 = (bf16[16,32,256]{2,1,0:T(8,128)(2,1)S(1)}, bf16[16,32,256]{2,1,0:T(8,128)(2,1)}, u32[]{:S(2)}) copy-start(bf16[16,32,256]{2,1,0:T(8,128)(2,1)} %fo.1) | copy-start | bytes 786436
  25.8 7.6 %copy-start.4 = (bf16[9,256,256]{2,1,0:T(8,128)(2,1)S(1)}, bf16[9,256,256]{2,1,0:T(8,128)(2,1)}, u32[]{:S(2)}) copy-start(bf16[9,256,256]{2,1,0:T(8,128)(2,1)} %param.10) | copy-start | bytes 3538948
  28.7 16.6 %all-to-all-start = ((bf16[64,40,128]{2,1,0:T(8,128)(2,1)}), bf16[64,40,128]{2,1,0:T(8,128)(2,1)S(1)}, u32[]{:S(2)}, u32[]{:S(2)}) async-start(bf16[64,40,128]{2,1,0:T(8,128)(2,1)} %get-tuple-element.36), calls=%async_computation | async-start | bytes 1310720 | tf_op jit(solution)/shard_map/all_to_all | solution.py:504
  33.4 19.3 %copy-start.3 = (bf16[16,32,256]{2,1,0:T(8,128)(2,1)S(1)}, bf16[16,32,256]{2,1,0:T(8,128)(2,1)}, u32[]{:S(2)}) copy-start(bf16[16,32,256]{2,1,0:T(8,128)(2,1)} %co.1) | copy-start | bytes 786436
  46.3 17.6 %all-to-all-start.1 = ((bf16[64,40,128]{2,1,0:T(8,128)(2,1)}), bf16[64,40,128]{2,1,0:T(8,128)(2,1)S(1)}, u32[]{:S(2)}, u32[]{:S(2)}) async-start(bf16[64,40,128]{2,1,0:T(8,128)(2,1)} %get-tuple-element.38), calls=%async_computation.1 | async-start | bytes 1310720 | tf_op jit(solution)/shard_map/all_to_all | solution.py:528
  63.9 5.5 %collective-permute-start.7 = (bf16[64,40,128]{2,1,0:T(8,128)(2,1)S(1)}, bf16[64,40,128]{2,1,0:T(8,128)(2,1)S(1)}, u32[]{:S(2)}, u32[]{:S(2)}) collective-permute-start(bf16[64,40,128]{2,1,0:T(8,128)(2,1)S(1)} %all-to-all-done.1.mine), channel_id=1, source_target_pairs={{0,32},{1,33},{2,34},{3,35},{4,36},{5,37},{6,38},{7,39},{8,40},{9,... | collective-permute-start | bytes 1966088 | tf_op jit(solution)/shard_map/ppermute | solution.py:39

commit v4 on v3

--- a/solution.py
+++ b/solution.py
@@ -70,18 +70,16 @@
     )(*operands)
 
 
-def column_kernel(f_in, fx, c_in, cx, fo, co, edge):
+def column_kernel(own, fx, cx, edge):
     _, core = here()
-    fo[...] = f_in[...]
-    co[...] = c_in[...]
     for side in range(2):
 
         @pl.when(core == side)
         def _():
             cells = slice(CELLS - 2, CELLS) if side == 0 else slice(0, 2)
-            for f, pair in enumerate(((f_in, fx), (c_in, cx))):
-                for part, ref in enumerate(pair):
-                    edge[f, part * ROWS : (part + 1) * ROWS] = ref[:, cells, :]
+            for f, other in enumerate((fx, cx)):
+                edge[f, 0:ROWS] = own[f, :, cells, :]
+                edge[f, ROWS : 2 * ROWS] = other[:, cells, :]
 
 
 def boundary(xl, core):
@@ -96,20 +94,20 @@
     return [slice(p * ROWS + first, p * ROWS + first + count) for p in (part, 1 - part)]
 
 
-def row_kernel(fo, fx, co, cx, near, far, to, tx, after, rows):
+def row_kernel(own, fx, cx, near, far, to, tx, rows):
     xl, core = here()
-    rows[:, :, 36:SLOTS, :] = jnp.zeros((2, 2, SLOTS - 36, CHAN), bf16)
+    rows[:, :, 36:40, :] = jnp.zeros((2, 2, 4, CHAN), bf16)
     for chosen, part, first in boundary(xl, core):
 
         @pl.when(chosen)
         def _():
             span = slice(first, first + 2)
             side, cross = rows_of(part, first, 2)
-            for f, pair in enumerate(((fo, fx), (co, cx))):
+            for f, pair in enumerate(((own.at[0], fx), (own.at[1], cx))):
                 rows[f, :, 0:CELLS, :] = pair[part][span]
                 rows[f, :, CELLS : CELLS + 2, :] = near[f, side]
                 rows[f, :, CELLS + 2 : CELLS + 4, :] = far[f, cross]
-            rows[1, 0, SLOTS - 2 : SLOTS, :] = (to, tx)[part][span]
+            rows[1, 0, 38:40, :] = (to, tx)[part][span]
 
 
 def padded(dst, f, xl, core, own, other, near, far, rows, lanes):
@@ -204,40 +202,27 @@
     lax.fori_loop(0, ROWS, step, 0, unroll=4)
 
 
-def own_kernel(start, length, taps, after, masked, flat, bands, lines):
-    xl, core = here()
-    square = iota((ROWS, ROWS), 0) == iota((ROWS, ROWS), 1)
-
-    def upright(line):
-        spread = jnp.where(square, jnp.broadcast_to(line.astype(f32), (ROWS, ROWS)), 0.0)
-        return jnp.sum(spread, axis=1, keepdims=True)
-
-    low = upright(start[...])
-    high = low + upright(length[...])
-    source = (xl * 2 + core) * ROWS + iota((ROWS, 25), 0) - 2 + over(iota((ROWS, 25), 1), BAND)
-    source = source.astype(f32)
-    inside = (source >= low) & (source < high)
+def band_kernel(mo, mx, own, cx, after, bo, bx, cot_t, to, tx, lines):
+    to[...] = flat_taps(mo)
+    tx[...] = flat_taps(mx)
+    all_bands(mo, bo, lines)
+    all_bands(mx, bx, lines)
+    cot_t[:, 0:512] = own[1].reshape(512, CHAN).T
+    cot_t[:, 512:1024] = cx[...].reshape(512, CHAN).T
+
+
+def flat_taps(taps):
     total = jnp.zeros((ROWS, CHAN), f32)
     for k in range(BASIS):
-        part = jnp.where(inside, taps[k].astype(f32), 0.0).astype(bf16)
-        masked[k] = part
         at = iota((25, CHAN), 1) == iota((25, CHAN), 0) + 25 * k
-        total += jnp.dot(part, at.astype(f32).astype(bf16), preferred_element_type=f32)
-    flat[...] = total.astype(bf16)
-    all_bands(masked, bands, lines)
-
-
-def other_kernel(mx, co, cx, after, bands, cot_t, token, lines):
-    mark(token)
-    all_bands(mx, bands, lines)
-    cot_t[:, 0:512] = co[...].reshape(512, CHAN).T
-    cot_t[:, 512:1024] = cx[...].reshape(512, CHAN).T
-
-
-def weight_kernel(fo, fx, near, far, bo, bx, cot_t, grad, field, basis):
+        total += jnp.dot(taps[k], at.astype(f32).astype(bf16), preferred_element_type=f32)
+    return total.astype(bf16)
+
+
+def weight_kernel(own, fx, near, far, bo, bx, cot_t, grad, field, basis):
     xl, core = here()
     lanes = pl.ds(pl.multiple_of(core * HALF, HALF), HALF)
-    padded(field, 0, xl, core, fo, fx, near, far, None, lanes)
+    padded(field, 0, xl, core, own.at[0], fx, near, far, None, lanes)
 
     for part, bands in enumerate((bo, bx)):
         begin = ROWS * (core if part == 0 else 1 - core)
@@ -275,7 +260,7 @@
 
 
 def weight_end_kernel(
-    fo, fx, co, cx, near, far, rows, bo, bx, grad, parts, token, field, cot, tile
+    own, fx, cx, near, far, rows, bo, bx, grad, parts, token, field, cot, tile
 ):
     mark(token)
     xl, core = here()
@@ -286,14 +271,14 @@
 
         @pl.when(chosen)
         def _():
-            ref = (fo, fx)[part]
+            ref = (own.at[0], fx)[part]
             at = 2 if first == 0 else 0
             begin = 0 if first == 0 else 12
             side, cross = rows_of(part, begin, 4)
             field[at : at + 4, 0:CELLS, :] = ref[begin : begin + 4, :, lanes]
             field[at : at + 4, CELLS : CELLS + 2, :] = near[0, side, :, lanes]
             field[at : at + 4, CELLS + 2 : CELLS + 4, :] = far[0, cross, :, lanes]
-            cot[...] = (co, cx)[part][first : first + 2].reshape(2 * CELLS, CHAN).T
+            cot[...] = (own.at[1], cx)[part][first : first + 2].reshape(2 * CELLS, CHAN).T
             tile[...] = (bo, bx)[part][first : first + 2]
 
     basis = []
@@ -345,7 +330,8 @@
 
 
 def mixed_kernel(
-    fo, fx, near, far, rows, mo, w_hbm, after, out, token, field, basis, weight, bands, lines, sems
+    fo, fx, near, far, rows, mo, w_hbm, after, out, token,
+    field, basis, weight, bands, lines, sems
 ):
     mark(token)
     xl, core = here()
@@ -393,9 +379,7 @@
     rep = jnp.dot(one_hot(row, 8, 2, 16, count), to[...], preferred_element_type=f32)
     rep += jnp.dot(one_hot(row, 8, other, 16, count), tx[...], preferred_element_type=f32)
     rep += jnp.dot(
-        one_hot(row, 8, beyond, 2, count),
-        rows[1, 0, SLOTS - 2 : SLOTS, :],
-        preferred_element_type=f32,
+        one_hot(row, 8, beyond, 2, count), rows[1, 0, 38:40, :], preferred_element_type=f32
     )
     _, b, _ = split_taps(iota((1, CHAN), 1))
     k, _, s = split_taps(iota((CHAN, 1), 0))
@@ -432,37 +416,34 @@
 def shards(feature, filters, start, length, weight, cotangent):
     fx = send(feature, core=True)
     cx = send(cotangent, core=True)
+    lat = lax.axis_index("xl") * 2 + lax.axis_index("core")
+    source = lat * ROWS + jnp.arange(ROWS, dtype=jnp.int32)[:, None] - 2
+    source = source + jnp.arange(25, dtype=jnp.int32)[None, :] // BAND - start[:, None]
+    inside = (source >= 0) & (source < length[:, None])
+    mo = jnp.where(inside[None], filters.transpose(1, 0, 2), jnp.zeros((), bf16))
+    mx = send(mo, core=True)
+    own = jnp.stack([feature, cotangent])
+
     block = ((ROWS, CELLS, CHAN), bf16)
-    taps = ((BASIS, ROWS, 25), bf16)
     tiles = ((ROWS, BASIS * CELLS, CHAN), bf16)
+    flat = ((ROWS, CHAN), bf16)
     lines = pltpu.VMEM((BASIS * ROWS, BAND * CHAN), f32)
-    fo, co, edge = call(
+    (edge,) = call(
         column_kernel,
-        [block, block, ((2, 2 * ROWS, 2, CHAN), bf16)],
-        (feature, fx, cotangent, cx),
+        [((2, 2 * ROWS, 2, CHAN), bf16)],
+        (own, fx, cx),
         traffic=2**20,
         limit=8,
     )
     near = send(edge, lon=(1, -1))
 
-    mo, to, bo = call(
-        own_kernel,
-        [taps, ((ROWS, CHAN), bf16), tiles],
-        (start.reshape(1, ROWS), length.reshape(1, ROWS), filters.transpose(1, 0, 2), edge),
+    bo, bx, cot_t, to, tx = call(
+        band_kernel,
+        [tiles, tiles, ((CHAN, 1024), bf16), flat, flat],
+        (mo, mx, own, cx, edge),
         scratch=[lines],
-        flops=2 * 144 * 256 * 1280,
-        traffic=4 * 2**20,
-        limit=16,
-    )
-    mx = send(mo, core=True)
-    tx = send(to, core=True)
-    bx, cot_t, after = call(
-        other_kernel,
-        [tiles, ((CHAN, 1024), bf16), TOKEN],
-        (mx, co, cx, edge),
-        scratch=[lines],
-        flops=2 * 144 * 256 * 1280,
-        traffic=4 * 2**20,
+        flops=4 * 144 * 256 * 1280,
+        traffic=8 * 2**20,
         limit=16,
     )
     near, bx = lax.optimization_barrier((near, bx))
@@ -471,15 +452,15 @@
 
     (rows,) = call(
         row_kernel,
-        [((2, 2, SLOTS, CHAN), bf16)],
-        (fo, fx, co, cx, *halo, to, tx, after),
+        [((2, 2, 40, CHAN), bf16)],
+        (own, fx, cx, *halo, to, tx),
         traffic=2**20,
     )
     rows = send(rows, lat=True)
     (grad,) = call(
         weight_kernel,
         [((BASIS, CHAN, HALF), f32)],
-        (fo, fx, *halo, bo, bx, cot_t),
+        (own, fx, *halo, bo, bx, cot_t),
         scratch=[
             pltpu.VMEM((36, SLOTS, HALF), bf16),
             pltpu.VMEM((1024, BASIS * HALF), bf16),
@@ -490,7 +471,7 @@
     parts, after = call(
         weight_end_kernel,
         [((64, KEEP, HALF), bf16), TOKEN],
-        (fo, fx, co, cx, *halo, rows, bo, bx, grad),
+        (own, fx, cx, *halo, rows, bo, bx, grad),
         scratch=[
             pltpu.VMEM((6, SLOTS, HALF), bf16),
             pltpu.VMEM((CHAN, 2 * CELLS), bf16),

time: 71.1 us -> 68.5 us (0.963)
  local copies, waits for them, and re-layouts: 3.99 us -> 0.02 us
  other arithmetic: 0 us -> 2.62 us
  waiting for transfers between devices: 19.3 us -> 17.8 us
    unnamed x16 -> x6, local copies, waits for them, and re-layouts: 3.99 us -> 0.02 us
    ppermute x8 -> x7, waiting for transfers between devices: 5.72 us -> 4.19 us  [send(): return lax.ppermute(x, AXES, moves(**way))]
    another operation x0 -> x1, other arithmetic: none -> 1.08 us  [shards(): own = jnp.stack([feature, cotangent])]
    all_to_all x1, starting transfers between devices: 4.64 us -> 5.54 us  [shards(): swapped = lax.all_to_all(parts, RING, 0, 0, tiled=True)]
    select_n x0 -> x2, other arithmetic: none -> 0.78 us  [the longest x1 0.77 us: shards(): jnp.where(inside[None], filters.transpose(1, 0, 2), jnp.zeros((), bf16))]
    and x0 -> x1, other arithmetic: none -> 0.75 us  [shards(): inside = (source >= 0) & (source < length[:, None])]
    ppermute x8 -> x7, starting transfers between devices: 15.3 us -> 14.8 us  [send(): return lax.ppermute(x, AXES, moves(**way))]
    pallas_call x11 -> x10, Pallas kernels: 20.1 us -> 20 us  [call(): pl.pallas_call(kernel, out_shape=[jax.ShapeDtypeStruct(*o) for o in outs]...]
  transfers between devices with their start and end apart: 10 -> 9, of which waited for: 8 -> 6; matrix products, arithmetic and copies ran while one was open for 0% -> 4% of each run, Pallas kernels for 23% -> 24%
where the time goes in v4:
time: 68.5 us; the launch traced here: 68.1 us
  starting transfers between devices  26.7 us (39%)
  Pallas kernels  20 us (29%)
  waiting for transfers between devices  17.8 us (26%)
  other arithmetic  2.62 us (4%)
  between operations  0.95 us (1%)
    pallas_call x10, Pallas kernels, call(): pl.pallas_call(kernel, out_shape=[jax.ShapeDtypeStruct(*o) for o in outs]...  20 us
    ppermute x7, starting transfers between devices, send(): return lax.ppermute(x, AXES, moves(**way))  14.8 us
    all_to_all x1, waiting for transfers between devices, shards(): swapped = lax.all_to_all(parts, RING, 0, 0, tiled=True)  8.26 us
    all_to_all x1, starting transfers between devices, shards(): mine = lax.all_to_all(shared, RING, 0, 0, tiled=True)  6.31 us
    all_to_all x1, starting transfers between devices, shards(): swapped = lax.all_to_all(parts, RING, 0, 0, tiled=True)  5.54 us
    all_to_all x1, waiting for transfers between devices, shards(): mine = lax.all_to_all(shared, RING, 0, 0, tiled=True)  5.36 us
    ppermute x7, waiting for transfers between devices, send(): return lax.ppermute(x, AXES, moves(**way))  4.19 us
  transfers between devices with their start and end apart: 9, of which 6 were waited for; matrix products, arithmetic and copies ran while one was open for 4% of the time, Pallas kernels for 24%

profile of v4, /device:TPU:1, one launch (start us, length us, event | category | flops | bytes accessed | tf_op | source)
XLA Modules:
  0.0 68.1 jit_solution(9720093009601598460)
XLA Ops:
  0.6 1.5 %collective-permute-start = (bf16[16,32,256]{2,1,0:T(8,128)(2,1)}, bf16[16,32,256]{2,1,0:T(8,128)(2,1)S(1)}, u32[]{:S(2)}, u32[]{:S(2)}) collective-permute-start(bf16[16,32,256]{2,1,0:T(8,128)(2,1)} %fo.1), channel_id=1, source_target_pairs={{0,32},{1,33},{2,34},{3,35},{4,36},{5,37},{6,38},{7,39},{8,40},{9,... | collective-permute-start | bytes 786440 | tf_op jit(solution)/shard_map/ppermute | solution.py:39
  2.1 0.1 collective-permute-start.1
  2.2 1.1 %pad_maximum_fusion.own = bf16[2,16,32,256]{3,2,1,0:T(8,128)(2,1)S(1)} fusion(bf16[1,16,32,256]{3,2,1,0:T(8,128)(2,1)} %bitcast.6, bf16[1,16,32,256]{3,2,1,0:T(8,128)(2,1)} %bitcast.5), kind=kLoop, calls=%fused_computation | loop fusion | flops 262144 | bytes 1048576 | tf_op jit(solution)/shard_map/stack | solution.py:425
  3.3 0.7 %fusion.2 = pred[16,25]{1,0:T(8,128)(4,1)S(1)} fusion(s32[16]{0:T(128)} %param.9, s32[16]{0:T(128)} %param.8, s32[25]{0:T(128)S(1)} %and_select_fusion, s32[16]{0:T(128)S(1)} %add_add_fusion), kind=kLoop, calls=%fused_computation.5 | loop fusion | flops 2000 | bytes 692 | tf_op jit(solution)/shard_map/and | solution.py:422
  4.1 0.0 collective-permute-done.fx
  4.1 0.0 collective-permute-done.1.cx
  4.1 0.1 shard_map.85.after
  4.2 8.8 %collective-permute-start.2 = (bf16[2,32,2,256]{3,2,1,0:T(2,128)(2,1)S(1)}, bf16[2,32,2,256]{3,2,1,0:T(2,128)(2,1)S(1)}, u32[]{:S(2)}, u32[]{:S(2)}) collective-permute-start(bf16[2,32,2,256]{3,2,1,0:T(2,128)(2,1)S(1)} %shard_map.85.after), channel_id=1, source_target_pairs={{0,1},{1,2},{2,3},{3,4},{4,5},{5,6},{6,7},{7,8},{8,9},{9,10},{10,1... | collective-permute-start | bytes 196616 | tf_op jit(solution)/shard_map/ppermute | solution.py:39
  13.0 0.8 %select_bitcast_fusion.mo = bf16[9,16,25]{2,1,0:T(8,128)(2,1)S(1)} fusion(bf16[16,9,25]{2,0,1:T(8,128)(2,1)} %param.7, pred[16,25]{1,0:T(8,128)(4,1)S(1)} %fusion.2), kind=kLoop, calls=%fused_computation.1 | loop fusion | flops 3600 | bytes 14800 | tf_op jit(solution)/shard_map/jit(_where)/select_n | solution.py:423
  13.8 0.0 collective-permute-start.3
  13.8 1.2 %collective-permute-done.3.mx = bf16[9,16,25]{2,1,0:T(8,128)(2,1)S(1)} collective-permute-done((bf16[9,16,25]{2,1,0:T(8,128)(2,1)S(1)}, bf16[9,16,25]{2,1,0:T(8,128)(2,1)S(1)}, u32[]{:S(2)}, u32[]{:S(2)}) %collective-permute-start.3) | collective-permute-done | bytes 7232 | tf_op jit(solution)/shard_map/ppermute | solution.py:39
  15.0 3.5 %shard_map.86 = (bf16[16,288,256]{2,1,0:T(8,128)(2,1)S(1)}, bf16[16,288,256]{2,1,0:T(8,128)(2,1)S(1)}, bf16[256,1024]{1,0:T(8,128)(2,1)S(1)}, bf16[16,256]{1,0:T(8,128)(2,1)S(1)}, bf16[16,256]{1,0:T(8,128)(2,1)S(1)}) custom-call(bf16[9,16,25]{2,1,0:T(8,128)(2,1)S(1)} %select_bitcast_fusion.mo, bf16[9,16,25]{2,1,0:T(8,128)(2,1)S(1)} %collective-permute-done.3.mx, ...), custom_call_target="tpu_custom_call" | custom-call | flops 188743680 | bytes 8388608 | tf_op jit(solution)/shard_map/pallas_call | solution.py:61
  18.5 0.0 collective-permute-done.2.near
  18.5 0.2 collective-permute-start.4
  18.8 1.1 %collective-permute-done.4.far = bf16[2,32,2,256]{3,2,1,0:T(2,128)(2,1)S(1)} collective-permute-done((bf16[2,32,2,256]{3,2,1,0:T(2,128)(2,1)S(1)}, bf16[2,32,2,256]{3,2,1,0:T(2,128)(2,1)S(1)}, u32[]{:S(2)}, u32[]{:S(2)}) %collective-permute-start.4) | collective-permute-done | bytes 65568 | tf_op jit(solution)/shard_map/ppermute | solution.py:39
  19.9 0.4 collective-permute-start.5
  20.3 2.3 %shard_map.88.grad = f32[9,256,128]{2,1,0:T(8,128)S(1)} custom-call(bf16[2,16,32,256]{3,2,1,0:T(8,128)(2,1)S(1)} %pad_maximum_fusion.own, bf16[16,32,256]{2,1,0:T(8,128)(2,1)S(1)} %collective-permute-done.fx, bf16[2,32,2,256]{3,2,1,0:T(2,128)(2,1)S(1)} %collective-permute-done.2.near, bf16[2,32,2,256]{3,2,1,0:T(2,128)(2,1)S(1)} %collective-permute-done.4.far, ...), custom_call_target="tpu_custom_call" | custom-call | flops 1811939328 | bytes 7340032 | tf_op jit(solution)/shard_map/pallas_call | solution.py:61
  22.6 0.0 copy-start
  22.6 0.0 copy-start.2
  22.6 1.3 %collective-permute-done.5.rows = bf16[2,2,40,256]{3,2,1,0:T(8,128)(2,1)S(1)} collective-permute-done((bf16[2,2,40,256]{3,2,1,0:T(8,128)(2,1)S(1)}, bf16[2,2,40,256]{3,2,1,0:T(8,128)(2,1)S(1)}, u32[]{:S(2)}, u32[]{:S(2)}) %collective-permute-start.5) | collective-permute-done | bytes 81952 | tf_op jit(solution)/shard_map/ppermute | solution.py:39
  23.9 1.5 %shard_map.89 = (bf16[64,40,128]{2,1,0:T(8,128)(2,1)}, f32[8,128]{1,0:T(8,128)S(1)}) custom-call(bf16[2,16,32,256]{3,2,1,0:T(8,128)(2,1)S(1)} %pad_maximum_fusion.own, bf16[16,32,256]{2,1,0:T(8,128)(2,1)S(1)} %collective-permute-done.fx, bf16[16,32,256]{2,1,0:T(8,128)(2,1)S(1)} %collective-permute-done.1.cx, ...), custom_call_target="tpu_custom_call" | custom-call | flops 37748736 | bytes 3145728 | tf_op jit(solution)/shard_map/pallas_call | solution.py:61
  25.3 5.5 %all-to-all-start = ((bf16[64,40,128]{2,1,0:T(8,128)(2,1)}), bf16[64,40,128]{2,1,0:T(8,128)(2,1)S(1)}, u32[]{:S(2)}, u32[]{:S(2)}) async-start(bf16[64,40,128]{2,1,0:T(8,128)(2,1)} %get-tuple-element.28), calls=%async_computation | async-start | bytes 1310720 | tf_op jit(solution)/shard_map/all_to_all | solution.py:485
  30.9 0.0 copy-done
  30.9 0.0 copy-done.2
  30.9 0.0 copy-start.1
  30.9 3.7 %shard_map.90 = (bf16[16,32,256]{2,1,0:T(8,128)(2,1)}, f32[8,128]{1,0:T(8,128)S(1)}) custom-call(bf16[16,32,256]{2,1,0:T(8,128)(2,1)S(1)} %copy-done, bf16[16,32,256]{2,1,0:T(8,128)(2,1)S(1)} %collective-permute-done.fx, bf16[2,32,2,256]{3,2,1,0:T(2,128)(2,1)S(1)} %collective-permute-done.2.near, bf16[2,32,2,256]{3,2,1,0:T(2,128)(2,1)S(1)} %collective-permute-done.4.far, ...), custom_call_target="tpu_custom_call" | custom-call | flops 1207959552 | bytes 8388608 | tf_op jit(solution)/shard_map/pallas_call | solution.py:61
  34.6 8.3 %all-to-all-done.parts = bf16[64,40,128]{2,1,0:T(8,128)(2,1)S(1)} async-done(((bf16[64,40,128]{2,1,0:T(8,128)(2,1)}), bf16[64,40,128]{2,1,0:T(8,128)(2,1)S(1)}, u32[]{:S(2)}, u32[]{:S(2)}) %all-to-all-start) | async-done | bytes 655392 | tf_op jit(solution)/shard_map/all_to_all | solution.py:485
  42.8 1.0 %shard_map.91 = (bf16[64,40,128]{2,1,0:T(8,128)(2,1)}, f32[8,128]{1,0:T(8,128)S(1)}) custom-call(bf16[64,40,128]{2,1,0:T(8,128)(2,1)S(1)} %all-to-all-done.parts, f32[8,128]{1,0:T(8,128)S(1)} %get-tuple-element.29.after), custom_call_target="tpu_custom_call" | custom-call | bytes 1048576 | tf_op jit(solution)/shard_map/pallas_call | solution.py:61
  43.8 6.3 %all-to-all-start.1 = ((bf16[64,40,128]{2,1,0:T(8,128)(2,1)}), bf16[64,40,128]{2,1,0:T(8,128)(2,1)S(1)}, u32[]{:S(2)}, u32[]{:S(2)}) async-start(bf16[64,40,128]{2,1,0:T(8,128)(2,1)} %get-tuple-element.30), calls=%async_computation.1 | async-start | bytes 1310720 | tf_op jit(solution)/shard_map/all_to_all | solution.py:509
  50.1 0.0 copy-done.1
  50.1 5.8 %shard_map.92 = (bf16[16,32,256]{2,1,0:T(8,128)(2,1)}, f32[8,128]{1,0:T(8,128)}) custom-call(bf16[16,32,256]{2,1,0:T(8,128)(2,1)S(1)} %copy-done.1, bf16[16,32,256]{2,1,0:T(8,128)(2,1)S(1)} %collective-permute-done.1.cx, bf16[2,32,2,256]{3,2,1,0:T(2,128)(2,1)S(1)} %collective-permute-done.2.near, bf16[2,32,2,256]{3,2,1,0:T(2,128)(2,1)S(1)} %collective-permute-done.4.far, ...), custom_call_target="tpu_custom_call" | custom-call | flops 1971322880 | bytes 8388608 | tf_op jit(solution)/shard_map/pallas_call | solution.py:61
  56.0 5.4 %all-to-all-done.1.mine = bf16[64,40,128]{2,1,0:T(8,128)(2,1)S(1)} async-done(((bf16[64,40,128]{2,1,0:T(8,128)(2,1)}), bf16[64,40,128]{2,1,0:T(8,128)(2,1)S(1)}, u32[]{:S(2)}, u32[]{:S(2)}) %all-to-all-start.1) | async-done | bytes 655392 | tf_op jit(solution)/shard_map/all_to_all | solution.py:509
  61.4 3.8 %collective-permute-start.6 = (bf16[64,40,128]{2,1,0:T(8,128)(2,1)S(1)}, bf16[64,40,128]{2,1,0:T(8,128)(2,1)S(1)}, u32[]{:S(2)}, u32[]{:S(2)}) collective-permute-start(bf16[64,40,128]{2,1,0:T(8,128)(2,1)S(1)} %all-to-all-done.1.mine), channel_id=1, source_target_pairs={{0,32},{1,33},{2,34},{3,35},{4,36},{5,37},{6,38},{7,39},{8,40},{9,... | collective-permute-start | bytes 1966088 | tf_op jit(solution)/shard_map/ppermute | solution.py:39
  65.1 1.1 %shard_map.93.before = f32[9,256,256]{2,1,0:T(8,128)} custom-call(bf16[64,40,128]{2,1,0:T(8,128)(2,1)S(1)} %all-to-all-done.1.mine), custom_call_target="tpu_custom_call" | custom-call | bytes 2097152 | tf_op jit(solution)/shard_map/pallas_call | solution.py:61
  66.2 0.6 collective-permute-done.6.theirs
  66.9 1.1 %shard_map.94 = f32[9,256,256]{2,1,0:T(8,128)} custom-call(bf16[64,40,128]{2,1,0:T(8,128)(2,1)S(1)} %collective-permute-done.6.theirs, f32[9,256,256]{2,1,0:T(8,128)} %shard_map.93.before), custom_call_target="tpu_custom_call", output_to_operand_aliasing={{}: (1, {})} | custom-call | bytes 2097152 | tf_op jit(solution)/shard_map/pallas_call | solution.py:61
  (3 shorter events, 0.0 us)
Async XLA Ops:
  0.6 3.5 %collective-permute-start = (bf16[16,32,256]{2,1,0:T(8,128)(2,1)}, bf16[16,32,256]{2,1,0:T(8,128)(2,1)S(1)}, u32[]{:S(2)}, u32[]{:S(2)}) collective-permute-start(bf16[16,32,256]{2,1,0:T(8,128)(2,1)} %fo.1), channel_id=1, source_target_pairs={{0,32},{1,33},{2,34},{3,35},{4,36},{5,37},{6,38},{7,39},{8,40},{9,... | collective-permute-start | bytes 786440 | tf_op jit(solution)/shard_map/ppermute | solution.py:39
  2.1 2.0 %collective-permute-start.1 = (bf16[16,32,256]{2,1,0:T(8,128)(2,1)}, bf16[16,32,256]{2,1,0:T(8,128)(2,1)S(1)}, u32[]{:S(2)}, u32[]{:S(2)}) collective-permute-start(bf16[16,32,256]{2,1,0:T(8,128)(2,1)} %co.1), channel_id=1, source_target_pairs={{0,32},{1,33},{2,34},{3,35},{4,36},{5,37},{6,38},{7,39},{8,40},{9,... | collective-permute-start | bytes 786440 | tf_op jit(solution)/shard_map/ppermute | solution.py:39
  4.2 14.3 %collective-permute-start.2 = (bf16[2,32,2,256]{3,2,1,0:T(2,128)(2,1)S(1)}, bf16[2,32,2,256]{3,2,1,0:T(2,128)(2,1)S(1)}, u32[]{:S(2)}, u32[]{:S(2)}) collective-permute-start(bf16[2,32,2,256]{3,2,1,0:T(2,128)(2,1)S(1)} %shard_map.85.after), channel_id=1, source_target_pairs={{0,1},{1,2},{2,3},{3,4},{4,5},{5,6},{6,7},{7,8},{8,9},{9,10},{10,1... | collective-permute-start | bytes 196616 | tf_op jit(solution)/shard_map/ppermute | solution.py:39
  13.8 1.2 %collective-permute-start.3 = (bf16[9,16,25]{2,1,0:T(8,128)(2,1)S(1)}, bf16[9,16,25]{2,1,0:T(8,128)(2,1)S(1)}, u32[]{:S(2)}, u32[]{:S(2)}) collective-permute-start(bf16[9,16,25]{2,1,0:T(8,128)(2,1)S(1)} %select_bitcast_fusion.mo), channel_id=1, source_target_pairs={{0,32},{1,33},{2,34},{3,35},{4,36},{5,37},{6,38},{7,39},{8,40},{9,... | collective-permute-start | bytes 21608 | tf_op jit(solution)/shard_map/ppermute | solution.py:39
  18.5 1.3 %collective-permute-start.4 = (bf16[2,32,2,256]{3,2,1,0:T(2,128)(2,1)S(1)}, bf16[2,32,2,256]{3,2,1,0:T(2,128)(2,1)S(1)}, u32[]{:S(2)}, u32[]{:S(2)}) collective-permute-start(bf16[2,32,2,256]{3,2,1,0:T(2,128)(2,1)S(1)} %collective-permute-done.2.near), channel_id=1, source_target_pairs={{0,32},{1,33},{2,34},{3,35},{4,36},{5,37},{6,38},{7,39},{8,40},{9,... | collective-permute-start | bytes 196616 | tf_op jit(solution)/shard_map/ppermute | solution.py:39
  19.9 4.0 %collective-permute-start.5 = (bf16[2,2,40,256]{3,2,1,0:T(8,128)(2,1)S(1)}, bf16[2,2,40,256]{3,2,1,0:T(8,128)(2,1)S(1)}, u32[]{:S(2)}, u32[]{:S(2)}) collective-permute-start(bf16[2,2,40,256]{3,2,1,0:T(8,128)(2,1)S(1)} %shard_map.87), channel_id=1, source_target_pairs={{0,64},{1,65},{2,66},{3,67},{4,68},{5,69},{6,70},{7,71},{8,72},{9,... | collective-permute-start | bytes 245768 | tf_op jit(solution)/shard_map/ppermute | solution.py:39
  22.6 8.3 %copy-start = (bf16[16,32,256]{2,1,0:T(8,128)(2,1)S(1)}, bf16[16,32,256]{2,1,0:T(8,128)(2,1)}, u32[]{:S(2)}) copy-start(bf16[16,32,256]{2,1,0:T(8,128)(2,1)} %fo.1) | copy-start | bytes 786436
  22.6 8.3 %copy-start.2 = (bf16[9,256,256]{2,1,0:T(8,128)(2,1)S(1)}, bf16[9,256,256]{2,1,0:T(8,128)(2,1)}, u32[]{:S(2)}) copy-start(bf16[9,256,256]{2,1,0:T(8,128)(2,1)} %param.10) | copy-start | bytes 3538948
  25.3 17.5 %all-to-all-start = ((bf16[64,40,128]{2,1,0:T(8,128)(2,1)}), bf16[64,40,128]{2,1,0:T(8,128)(2,1)S(1)}, u32[]{:S(2)}, u32[]{:S(2)}) async-start(bf16[64,40,128]{2,1,0:T(8,128)(2,1)} %get-tuple-element.28), calls=%async_computation | async-start | bytes 1310720 | tf_op jit(solution)/shard_map/all_to_all | solution.py:485
  30.9 19.2 %copy-start.1 = (bf16[16,32,256]{2,1,0:T(8,128)(2,1)S(1)}, bf16[16,32,256]{2,1,0:T(8,128)(2,1)}, u32[]{:S(2)}) copy-start(bf16[16,32,256]{2,1,0:T(8,128)(2,1)} %co.1) | copy-start | bytes 786436
  43.8 17.5 %all-to-all-start.1 = ((bf16[64,40,128]{2,1,0:T(8,128)(2,1)}), bf16[64,40,128]{2,1,0:T(8,128)(2,1)S(1)}, u32[]{:S(2)}, u32[]{:S(2)}) async-start(bf16[64,40,128]{2,1,0:T(8,128)(2,1)} %get-tuple-element.30), calls=%async_computation.1 | async-start | bytes 1310720 | tf_op jit(solution)/shard_map/all_to_all | solution.py:509
  61.4 5.5 %collective-permute-start.6 = (bf16[64,40,128]{2,1,0:T(8,128)(2,1)S(1)}, bf16[64,40,128]{2,1,0:T(8,128)(2,1)S(1)}, u32[]{:S(2)}, u32[]{:S(2)}) collective-permute-start(bf16[64,40,128]{2,1,0:T(8,128)(2,1)S(1)} %all-to-all-done.1.mine), channel_id=1, source_target_pairs={{0,32},{1,33},{2,34},{3,35},{4,36},{5,37},{6,38},{7,39},{8,40},{9,... | collective-permute-start | bytes 1966088 | tf_op jit(solution)/shard_map/ppermute | solution.py:39

commit v5 on v4

--- a/solution.py
+++ b/solution.py
@@ -19,7 +19,7 @@
 CHAN = 256
 HALF = 128
 BAND = 5
-KEEP = 40
+CHUNK = (9, 4, 128)
 bf16 = jnp.bfloat16
 f32 = jnp.float32
 
@@ -202,13 +202,16 @@
     lax.fori_loop(0, ROWS, step, 0, unroll=4)
 
 
-def band_kernel(mo, mx, own, cx, after, bo, bx, cot_t, to, tx, lines):
+def own_band_kernel(mo, own, after, bo, cot_t, to, lines):
     to[...] = flat_taps(mo)
+    all_bands(mo, bo, lines)
+    cot_t[...] = own[1].reshape(512, CHAN).T
+
+
+def other_band_kernel(mx, cx, after, bx, cot_t, tx, lines):
     tx[...] = flat_taps(mx)
-    all_bands(mo, bo, lines)
     all_bands(mx, bx, lines)
-    cot_t[:, 0:512] = own[1].reshape(512, CHAN).T
-    cot_t[:, 512:1024] = cx[...].reshape(512, CHAN).T
+    cot_t[...] = cx[...].reshape(512, CHAN).T
 
 
 def flat_taps(taps):
@@ -219,7 +222,7 @@
     return total.astype(bf16)
 
 
-def weight_kernel(own, fx, near, far, bo, bx, cot_t, grad, field, basis):
+def weight_kernel(own, fx, near, far, bo, bx, ct_o, ct_x, grad, field, basis):
     xl, core = here()
     lanes = pl.ds(pl.multiple_of(core * HALF, HALF), HALF)
     padded(field, 0, xl, core, own.at[0], fx, near, far, None, lanes)
@@ -245,17 +248,18 @@
             at = (part * ROWS + first) * CELLS
             basis[at : at + 2 * CELLS, :] = jnp.zeros((2 * CELLS, BASIS * HALF), bf16)
 
-    total = jnp.dot(cot_t[...], basis[...], preferred_element_type=f32)
+    total = jnp.dot(ct_o[...], basis[0:512, :], preferred_element_type=f32)
+    total += jnp.dot(ct_x[...], basis[512:1024, :], preferred_element_type=f32)
     for k in range(BASIS):
-        grad[k] = total[:, k * HALF : (k + 1) * HALF]
-
-
-def runs(k, side):
-    begin, at = side * 144 + k * 16, 0
+        grad[k] = total[:, k * HALF : (k + 1) * HALF].T
+
+
+def runs(k, side, half):
+    begin, at = half * 288 + side * 144 + k * 16, 0
     while at < 16:
-        s, j = divmod(begin + at, 64)
+        slot, j = divmod(begin + at, 64)
         count = min(16 - at, 64 - j)
-        yield at, s * 8, j, count
+        yield at, slot, j, count
         at += count
 
 
@@ -278,43 +282,54 @@
             field[at : at + 4, 0:CELLS, :] = ref[begin : begin + 4, :, lanes]
             field[at : at + 4, CELLS : CELLS + 2, :] = near[0, side, :, lanes]
             field[at : at + 4, CELLS + 2 : CELLS + 4, :] = far[0, cross, :, lanes]
-            cot[...] = (own.at[1], cx)[part][first : first + 2].reshape(2 * CELLS, CHAN).T
+            cot[...] = (own.at[1], cx)[part][first : first + 2].reshape(2 * CELLS, CHAN)
             tile[...] = (bo, bx)[part][first : first + 2]
 
     basis = []
     for r in range(2):
         window = field[r : r + BAND].reshape(BAND * SLOTS, HALF)
         basis.append(
-            jnp.dot(tile[r, :, 0 : BAND * SLOTS], window, preferred_element_type=f32).astype(bf16)
+            jnp.dot(tile[r, :, 0 : BAND * SLOTS], window, preferred_element_type=f32)
         )
-    parts[:, 32:KEEP, :] = jnp.zeros((64, 8, HALF), bf16)
     for k in range(BASIS):
         cells = jnp.concatenate([x[k * CELLS : (k + 1) * CELLS] for x in basis], 0)
-        total = (grad[k] + jnp.dot(cot[...], cells, preferred_element_type=f32)).T
+        total = grad[k] + jnp.dot(cells.T.astype(bf16), cot[...], preferred_element_type=f32)
         for side in range(2):
-            tiles = total[:, side * HALF : (side + 1) * HALF].reshape(16, 8, HALF).astype(bf16)
-            for at, s, j, count in runs(k, side):
-                parts[j : j + count, s : s + 8, :] = tiles[at : at + count]
-
-
-def sum_kernel(scale, parts, after, out, token):
+            tiles = total[:, side * HALF : (side + 1) * HALF].reshape(16, 8, HALF)
+            for half in range(2):
+                piece = tiles[:, half * 4 : (half + 1) * 4, :].astype(bf16)
+                for at, slot, j, count in runs(k, side, half):
+                    parts[j : j + count, slot] = piece[at : at + count]
+
+
+def sum_kernel(scale, parts, after, out, token, copies, sems):
     mark(token)
     total = jnp.sum(parts[...].astype(f32), axis=0) * scale
-    out[...] = jnp.broadcast_to(total.astype(bf16)[None], out.shape)
+    copies[...] = jnp.broadcast_to(total.astype(bf16)[None], copies.shape)
+    sends = [
+        pltpu.make_async_copy(copies, out.at[i * 8 : (i + 1) * 8], sems.at[i]) for i in range(8)
+    ]
+    for x in sends:
+        x.start()
+    for x in sends:
+        x.wait()
 
 
 def half_kernel(half_of, tiles_ref, out, stage, sems):
-    first = pl.multiple_of(half_of() * HALF, HALF)
+    first = half_of() * 16
     copies = []
     for k in range(BASIS):
         for side in range(2):
-            for at, s, j, count in runs(k, side):
-                tiles = tiles_ref[j : j + count, s : s + 8, :].astype(f32)
-                stage[k, at * 8 : (at + count) * 8, side * HALF : (side + 1) * HALF] = (
-                    tiles.reshape(count * 8, HALF)
-                )
+            for half in range(2):
+                for at, slot, j, count in runs(k, side, half):
+                    stage[
+                        k,
+                        at : at + count,
+                        half * 4 : (half + 1) * 4,
+                        side * HALF : (side + 1) * HALF,
+                    ] = tiles_ref[j : j + count, slot].astype(f32)
         copies.append(
-            pltpu.make_async_copy(stage.at[k], out.at[k, pl.ds(first, HALF), :], sems.at[k])
+            pltpu.make_async_copy(stage.at[k], out.at[k, pl.ds(first, 16)], sems.at[k])
         )
         copies[-1].start()
     for copy in copies:
@@ -416,12 +431,6 @@
 def shards(feature, filters, start, length, weight, cotangent):
     fx = send(feature, core=True)
     cx = send(cotangent, core=True)
-    lat = lax.axis_index("xl") * 2 + lax.axis_index("core")
-    source = lat * ROWS + jnp.arange(ROWS, dtype=jnp.int32)[:, None] - 2
-    source = source + jnp.arange(25, dtype=jnp.int32)[None, :] // BAND - start[:, None]
-    inside = (source >= 0) & (source < length[:, None])
-    mo = jnp.where(inside[None], filters.transpose(1, 0, 2), jnp.zeros((), bf16))
-    mx = send(mo, core=True)
     own = jnp.stack([feature, cotangent])
 
     block = ((ROWS, CELLS, CHAN), bf16)
@@ -435,15 +444,32 @@
         traffic=2**20,
         limit=8,
     )
+    edge, start = lax.optimization_barrier((edge, start))
     near = send(edge, lon=(1, -1))
-
-    bo, bx, cot_t, to, tx = call(
-        band_kernel,
-        [tiles, tiles, ((CHAN, 1024), bf16), flat, flat],
-        (mo, mx, own, cx, edge),
+    lat = lax.axis_index("xl") * 2 + lax.axis_index("core")
+    source = lat * ROWS + jnp.arange(ROWS, dtype=jnp.int32)[:, None] - 2
+    source = source + jnp.arange(25, dtype=jnp.int32)[None, :] // BAND - start[:, None]
+    inside = (source >= 0) & (source < length[:, None])
+    mo = jnp.where(inside[None], filters.transpose(1, 0, 2), jnp.zeros((), bf16))
+    mx = send(mo, core=True)
+
+    turned = ((CHAN, 512), bf16)
+    bo, ct_o, to = call(
+        own_band_kernel,
+        [tiles, turned, flat],
+        (mo, own, edge),
         scratch=[lines],
-        flops=4 * 144 * 256 * 1280,
-        traffic=8 * 2**20,
+        flops=2 * 144 * 256 * 1280,
+        traffic=4 * 2**20,
+        limit=16,
+    )
+    bx, ct_x, tx = call(
+        other_band_kernel,
+        [tiles, turned, flat],
+        (mx, cx, to),
+        scratch=[lines],
+        flops=2 * 144 * 256 * 1280,
+        traffic=4 * 2**20,
         limit=16,
     )
     near, bx = lax.optimization_barrier((near, bx))
@@ -459,8 +485,8 @@
     rows = send(rows, lat=True)
     (grad,) = call(
         weight_kernel,
-        [((BASIS, CHAN, HALF), f32)],
-        (own, fx, *halo, bo, bx, cot_t),
+        [((BASIS, HALF, CHAN), f32)],
+        (own, fx, *halo, bo, bx, ct_o, ct_x),
         scratch=[
             pltpu.VMEM((36, SLOTS, HALF), bf16),
             pltpu.VMEM((1024, BASIS * HALF), bf16),
@@ -470,11 +496,11 @@
     )
     parts, after = call(
         weight_end_kernel,
-        [((64, KEEP, HALF), bf16), TOKEN],
+        [((64, *CHUNK), bf16), TOKEN],
         (own, fx, cx, *halo, rows, bo, bx, grad),
         scratch=[
             pltpu.VMEM((6, SLOTS, HALF), bf16),
-            pltpu.VMEM((CHAN, 2 * CELLS), bf16),
+            pltpu.VMEM((2 * CELLS, CHAN), bf16),
             pltpu.VMEM((2, BASIS * CELLS, CHAN), bf16),
         ],
         flops=2 * 64 * 1152 * 256,
@@ -501,8 +527,10 @@
     )
     shared, after = call(
         functools.partial(sum_kernel, 1.0 / math.sqrt(64 * 1024)),
-        [((64, KEEP, HALF), bf16), TOKEN],
+        [((64, *CHUNK), bf16), TOKEN],
         (swapped, after),
+        scratch=[pltpu.VMEM((8, *CHUNK), bf16), pltpu.SemaphoreType.DMA((8,))],
+        to=(0,),
         traffic=2**20,
     )
 
@@ -526,8 +554,8 @@
     )
     mine, grad_feature = lax.optimization_barrier((mine, grad_feature))
     theirs = send(mine, core=True)
-    whole = ((BASIS, CHAN, CHAN), f32)
-    stage = [pltpu.VMEM((BASIS, HALF, CHAN), f32), pltpu.SemaphoreType.DMA((BASIS,))]
+    whole = ((BASIS, 32, 8, CHAN), f32)
+    stage = [pltpu.VMEM((BASIS, 16, 8, CHAN), f32), pltpu.SemaphoreType.DMA((BASIS,))]
     (grad_weight,) = call(
         own_half_kernel, [whole], (mine,), scratch=stage, to=(0,), traffic=2 * 2**20, limit=8
     )
@@ -542,7 +570,7 @@
         traffic=2 * 2**20,
         limit=8,
     )
-    return (mixed, grad_feature, grad_weight)
+    return (mixed, grad_feature, grad_weight.reshape(BASIS, CHAN, CHAN))
 
 
 def solution(mesh):

time: 68.5 us -> 67 us (0.978)
  waiting for transfers between devices: 17.8 us -> 15.6 us
    ppermute x7, waiting for transfers between devices: 4.19 us -> 2.89 us  [send(): return lax.ppermute(x, AXES, moves(**way))]
    pallas_call x10 -> x11, Pallas kernels: 20 us -> 20.4 us  [call(): pl.pallas_call(kernel, out_shape=[jax.ShapeDtypeStruct(*o) for o in outs]...]
  transfers between devices with their start and end apart: 9 -> 9, of which waited for: 6 -> 7; matrix products, arithmetic and copies ran while one was open for 4% -> 4% of each run, Pallas kernels for 24% -> 25%
where the time goes in v5:
time: 67 us; the launch traced here: 66.7 us
  starting transfers between devices  27.1 us (40%)
  Pallas kernels  20.4 us (30%)
  waiting for transfers between devices  15.6 us (23%)
  other arithmetic  2.61 us (4%)
  between operations  0.94 us (1%)
    pallas_call x11, Pallas kernels, call(): pl.pallas_call(kernel, out_shape=[jax.ShapeDtypeStruct(*o) for o in outs]...  20.4 us
    ppermute x7, starting transfers between devices, send(): return lax.ppermute(x, AXES, moves(**way))  14.9 us
    all_to_all x1, waiting for transfers between devices, shards(): swapped = lax.all_to_all(parts, RING, 0, 0, tiled=True)  7.76 us
    all_to_all x1, starting transfers between devices, shards(): mine = lax.all_to_all(shared, RING, 0, 0, tiled=True)  6.21 us
    all_to_all x1, starting transfers between devices, shards(): swapped = lax.all_to_all(parts, RING, 0, 0, tiled=True)  5.98 us
    all_to_all x1, waiting for transfers between devices, shards(): mine = lax.all_to_all(shared, RING, 0, 0, tiled=True)  4.99 us
    ppermute x7, waiting for transfers between devices, send(): return lax.ppermute(x, AXES, moves(**way))  2.89 us
  transfers between devices with their start and end apart: 9, of which 7 were waited for; matrix products, arithmetic and copies ran while one was open for 4% of the time, Pallas kernels for 25%

profile of v5, /device:TPU:1, one launch (start us, length us, event | category | flops | bytes accessed | tf_op | source)
XLA Modules:
  0.0 66.7 jit_solution(3106493448238625710)
XLA Ops:
  0.6 1.5 %collective-permute-start = (bf16[16,32,256]{2,1,0:T(8,128)(2,1)}, bf16[16,32,256]{2,1,0:T(8,128)(2,1)S(1)}, u32[]{:S(2)}, u32[]{:S(2)}) collective-permute-start(bf16[16,32,256]{2,1,0:T(8,128)(2,1)} %fo.1), channel_id=1, source_target_pairs={{0,32},{1,33},{2,34},{3,35},{4,36},{5,37},{6,38},{7,39},{8,40},{9,... | collective-permute-start | bytes 786440 | tf_op jit(solution)/shard_map/ppermute | solution.py:39
  2.1 0.1 collective-permute-start.1
  2.2 1.1 %pad_maximum_fusion.own = bf16[2,16,32,256]{3,2,1,0:T(8,128)(2,1)S(1)} fusion(bf16[1,16,32,256]{3,2,1,0:T(8,128)(2,1)} %bitcast.7, bf16[1,16,32,256]{3,2,1,0:T(8,128)(2,1)} %bitcast.6), kind=kLoop, calls=%fused_computation | loop fusion | flops 262144 | bytes 1048576 | tf_op jit(solution)/shard_map/stack | solution.py:434
  3.3 0.2 collective-permute-done.fx
  3.5 0.4 collective-permute-done.1.cx
  3.9 0.1 shard_map.85.after
  4.0 8.8 %collective-permute-start.2 = (bf16[2,32,2,256]{3,2,1,0:T(2,128)(2,1)S(1)}, bf16[2,32,2,256]{3,2,1,0:T(2,128)(2,1)S(1)}, u32[]{:S(2)}, u32[]{:S(2)}) collective-permute-start(bf16[2,32,2,256]{3,2,1,0:T(2,128)(2,1)S(1)} %shard_map.85.after), channel_id=1, source_target_pairs={{0,1},{1,2},{2,3},{3,4},{4,5},{5,6},{6,7},{7,8},{8,9},{9,10},{10,1... | collective-permute-start | bytes 196616 | tf_op jit(solution)/shard_map/ppermute | solution.py:39
  12.8 0.7 %fusion.2 = pred[16,25]{1,0:T(8,128)(4,1)S(1)} fusion(s32[16]{0:T(128)} %param.9, s32[16]{0:T(128)} %param.8, s32[25]{0:T(128)S(1)} %and_select_fusion, s32[16]{0:T(128)S(1)} %add_add_fusion), kind=kLoop, calls=%fused_computation.5 | loop fusion | flops 2000 | bytes 692 | tf_op jit(solution)/shard_map/and | solution.py:452
  13.5 0.8 %select_bitcast_fusion.mo = bf16[9,16,25]{2,1,0:T(8,128)(2,1)S(1)} fusion(bf16[16,9,25]{2,0,1:T(8,128)(2,1)} %param.7, pred[16,25]{1,0:T(8,128)(4,1)S(1)} %fusion.2), kind=kLoop, calls=%fused_computation.1 | loop fusion | flops 3600 | bytes 14800 | tf_op jit(solution)/shard_map/jit(_where)/select_n | solution.py:453
  14.3 0.0 collective-permute-start.3
  14.3 1.8 %shard_map.86 = (bf16[16,288,256]{2,1,0:T(8,128)(2,1)S(1)}, bf16[256,512]{1,0:T(8,128)(2,1)S(1)}, bf16[16,256]{1,0:T(8,128)(2,1)S(1)}) custom-call(bf16[9,16,25]{2,1,0:T(8,128)(2,1)S(1)} %select_bitcast_fusion.mo, bf16[2,16,32,256]{3,2,1,0:T(8,128)(2,1)S(1)} %pad_maximum_fusion.own, bf16[2,32,2,256]{3,2,1,0:T(2,128)(2,1)S(1)} %shard_map.85.after), custom_call_target="tpu_custom_call" | custom-call | flops 94371840 | bytes 4194304 | tf_op jit(solution)/shard_map/pallas_call | solution.py:61
  16.1 0.0 collective-permute-done.3.mx
  16.1 1.8 %shard_map.87 = (bf16[16,288,256]{2,1,0:T(8,128)(2,1)S(1)}, bf16[256,512]{1,0:T(8,128)(2,1)S(1)}, bf16[16,256]{1,0:T(8,128)(2,1)S(1)}) custom-call(bf16[9,16,25]{2,1,0:T(8,128)(2,1)S(1)} %collective-permute-done.3.mx, bf16[16,32,256]{2,1,0:T(8,128)(2,1)S(1)} %collective-permute-done.1.cx, bf16[16,256]{1,0:T(8,128)(2,1)S(1)} %get-tuple-element.24.after.to), custom_call_target="tpu_custom_call" | custom-call | flops 94371840 | bytes 4194304 | tf_op jit(solution)/shard_map/pallas_call | solution.py:61
  17.9 0.0 collective-permute-done.2.near
  17.9 0.6 collective-permute-start.4
  18.5 0.9 %collective-permute-done.4.far = bf16[2,32,2,256]{3,2,1,0:T(2,128)(2,1)S(1)} collective-permute-done((bf16[2,32,2,256]{3,2,1,0:T(2,128)(2,1)S(1)}, bf16[2,32,2,256]{3,2,1,0:T(2,128)(2,1)S(1)}, u32[]{:S(2)}, u32[]{:S(2)}) %collective-permute-start.4) | collective-permute-done | bytes 65568 | tf_op jit(solution)/shard_map/ppermute | solution.py:39
  19.4 0.4 collective-permute-start.5
  19.8 2.5 %shard_map.89.grad = f32[9,128,256]{2,1,0:T(8,128)S(1)} custom-call(bf16[2,16,32,256]{3,2,1,0:T(8,128)(2,1)S(1)} %pad_maximum_fusion.own, bf16[16,32,256]{2,1,0:T(8,128)(2,1)S(1)} %collective-permute-done.fx, bf16[2,32,2,256]{3,2,1,0:T(2,128)(2,1)S(1)} %collective-permute-done.2.near, bf16[2,32,2,256]{3,2,1,0:T(2,128)(2,1)S(1)} %collective-permute-done.4.far, ...), custom_call_target="tpu_custom_call" | custom-call | flops 1811939328 | bytes 7340032 | tf_op jit(solution)/shard_map/pallas_call | solution.py:61
  22.2 0.0 copy-start
  22.3 0.0 copy-start.2
  22.3 0.9 %collective-permute-done.5.rows = bf16[2,2,40,256]{3,2,1,0:T(8,128)(2,1)S(1)} collective-permute-done((bf16[2,2,40,256]{3,2,1,0:T(8,128)(2,1)S(1)}, bf16[2,2,40,256]{3,2,1,0:T(8,128)(2,1)S(1)}, u32[]{:S(2)}, u32[]{:S(2)}) %collective-permute-start.5) | collective-permute-done | bytes 81952 | tf_op jit(solution)/shard_map/ppermute | solution.py:39
  23.2 1.4 %shard_map.90 = (bf16[64,9,4,128]{3,2,1,0:T(4,128)(2,1)}, f32[8,128]{1,0:T(8,128)S(1)}) custom-call(bf16[2,16,32,256]{3,2,1,0:T(8,128)(2,1)S(1)} %pad_maximum_fusion.own, bf16[16,32,256]{2,1,0:T(8,128)(2,1)S(1)} %collective-permute-done.fx, bf16[16,32,256]{2,1,0:T(8,128)(2,1)S(1)} %collective-permute-done.1.cx, ...), custom_call_target="tpu_custom_call" | custom-call | flops 37748736 | bytes 3145728 | tf_op jit(solution)/shard_map/pallas_call | solution.py:61
  24.6 6.0 %all-to-all-start = ((bf16[64,9,4,128]{3,2,1,0:T(4,128)(2,1)}), bf16[64,9,4,128]{3,2,1,0:T(4,128)(2,1)S(1)}, u32[]{:S(2)}, u32[]{:S(2)}) async-start(bf16[64,9,4,128]{3,2,1,0:T(4,128)(2,1)} %get-tuple-element.34), calls=%async_computation | async-start | bytes 1179648 | tf_op jit(solution)/shard_map/all_to_all | solution.py:511
  30.6 0.0 copy-done
  30.6 0.0 copy-done.2
  30.6 0.0 copy-start.1
  30.6 3.7 %shard_map.91 = (bf16[16,32,256]{2,1,0:T(8,128)(2,1)}, f32[8,128]{1,0:T(8,128)S(1)}) custom-call(bf16[16,32,256]{2,1,0:T(8,128)(2,1)S(1)} %copy-done, bf16[16,32,256]{2,1,0:T(8,128)(2,1)S(1)} %collective-permute-done.fx, bf16[2,32,2,256]{3,2,1,0:T(2,128)(2,1)S(1)} %collective-permute-done.2.near, bf16[2,32,2,256]{3,2,1,0:T(2,128)(2,1)S(1)} %collective-permute-done.4.far, ...), custom_call_target="tpu_custom_call" | custom-call | flops 1207959552 | bytes 8388608 | tf_op jit(solution)/shard_map/pallas_call | solution.py:61
  34.3 7.8 %all-to-all-done.parts = bf16[64,9,4,128]{3,2,1,0:T(4,128)(2,1)S(1)} async-done(((bf16[64,9,4,128]{3,2,1,0:T(4,128)(2,1)}), bf16[64,9,4,128]{3,2,1,0:T(4,128)(2,1)S(1)}, u32[]{:S(2)}, u32[]{:S(2)}) %all-to-all-start) | async-done | bytes 589856 | tf_op jit(solution)/shard_map/all_to_all | solution.py:511
  42.1 1.1 %shard_map.92 = (bf16[64,9,4,128]{3,2,1,0:T(4,128)(2,1)}, f32[8,128]{1,0:T(8,128)S(1)}) custom-call(bf16[64,9,4,128]{3,2,1,0:T(4,128)(2,1)S(1)} %all-to-all-done.parts, f32[8,128]{1,0:T(8,128)S(1)} %get-tuple-element.35.after), custom_call_target="tpu_custom_call" | custom-call | bytes 1048576 | tf_op jit(solution)/shard_map/pallas_call | solution.py:61
  43.2 6.2 %all-to-all-start.1 = ((bf16[64,9,4,128]{3,2,1,0:T(4,128)(2,1)}), bf16[64,9,4,128]{3,2,1,0:T(4,128)(2,1)S(1)}, u32[]{:S(2)}, u32[]{:S(2)}) async-start(bf16[64,9,4,128]{3,2,1,0:T(4,128)(2,1)} %get-tuple-element.36), calls=%async_computation.1 | async-start | bytes 1179648 | tf_op jit(solution)/shard_map/all_to_all | solution.py:537
  49.4 0.0 copy-done.1
  49.4 5.8 %shard_map.93 = (bf16[16,32,256]{2,1,0:T(8,128)(2,1)}, f32[8,128]{1,0:T(8,128)}) custom-call(bf16[16,32,256]{2,1,0:T(8,128)(2,1)S(1)} %copy-done.1, bf16[16,32,256]{2,1,0:T(8,128)(2,1)S(1)} %collective-permute-done.1.cx, bf16[2,32,2,256]{3,2,1,0:T(2,128)(2,1)S(1)} %collective-permute-done.2.near, bf16[2,32,2,256]{3,2,1,0:T(2,128)(2,1)S(1)} %collective-permute-done.4.far, ...), custom_call_target="tpu_custom_call" | custom-call | flops 1971322880 | bytes 8388608 | tf_op jit(solution)/shard_map/pallas_call | solution.py:61
  55.3 5.0 %all-to-all-done.1.mine = bf16[64,9,4,128]{3,2,1,0:T(4,128)(2,1)S(1)} async-done(((bf16[64,9,4,128]{3,2,1,0:T(4,128)(2,1)}), bf16[64,9,4,128]{3,2,1,0:T(4,128)(2,1)S(1)}, u32[]{:S(2)}, u32[]{:S(2)}) %all-to-all-start.1) | async-done | bytes 589856 | tf_op jit(solution)/shard_map/all_to_all | solution.py:537
  60.3 3.5 %collective-permute-start.6 = (bf16[64,9,4,128]{3,2,1,0:T(4,128)(2,1)S(1)}, bf16[64,9,4,128]{3,2,1,0:T(4,128)(2,1)S(1)}, u32[]{:S(2)}, u32[]{:S(2)}) collective-permute-start(bf16[64,9,4,128]{3,2,1,0:T(4,128)(2,1)S(1)} %all-to-all-done.1.mine), channel_id=1, source_target_pairs={{0,32},{1,33},{2,34},{3,35},{4,36},{5,37},{6,38},{7,39},{8,40},{9,... | collective-permute-start | bytes 1769480 | tf_op jit(solution)/shard_map/ppermute | solution.py:39
  63.8 1.1 %shard_map.94.before = f32[9,32,8,256]{3,2,1,0:T(8,128)} custom-call(bf16[64,9,4,128]{3,2,1,0:T(4,128)(2,1)S(1)} %all-to-all-done.1.mine), custom_call_target="tpu_custom_call" | custom-call | bytes 2097152 | tf_op jit(solution)/shard_map/pallas_call | solution.py:61
  64.9 0.5 collective-permute-done.6.theirs
  65.4 1.1 %shard_map.95 = f32[9,32,8,256]{3,2,1,0:T(8,128)} custom-call(bf16[64,9,4,128]{3,2,1,0:T(4,128)(2,1)S(1)} %collective-permute-done.6.theirs, f32[9,32,8,256]{3,2,1,0:T(8,128)} %shard_map.94.before), custom_call_target="tpu_custom_call", output_to_operand_aliasing={{}: (1, {})} | custom-call | bytes 2097152 | tf_op jit(solution)/shard_map/pallas_call | solution.py:61
  (3 shorter events, 0.0 us)
Async XLA Ops:
  0.6 2.9 %collective-permute-start = (bf16[16,32,256]{2,1,0:T(8,128)(2,1)}, bf16[16,32,256]{2,1,0:T(8,128)(2,1)S(1)}, u32[]{:S(2)}, u32[]{:S(2)}) collective-permute-start(bf16[16,32,256]{2,1,0:T(8,128)(2,1)} %fo.1), channel_id=1, source_target_pairs={{0,32},{1,33},{2,34},{3,35},{4,36},{5,37},{6,38},{7,39},{8,40},{9,... | collective-permute-start | bytes 786440 | tf_op jit(solution)/shard_map/ppermute | solution.py:39
  2.1 1.7 %collective-permute-start.1 = (bf16[16,32,256]{2,1,0:T(8,128)(2,1)}, bf16[16,32,256]{2,1,0:T(8,128)(2,1)S(1)}, u32[]{:S(2)}, u32[]{:S(2)}) collective-permute-start(bf16[16,32,256]{2,1,0:T(8,128)(2,1)} %co.1), channel_id=1, source_target_pairs={{0,32},{1,33},{2,34},{3,35},{4,36},{5,37},{6,38},{7,39},{8,40},{9,... | collective-permute-start | bytes 786440 | tf_op jit(solution)/shard_map/ppermute | solution.py:39
  4.0 13.9 %collective-permute-start.2 = (bf16[2,32,2,256]{3,2,1,0:T(2,128)(2,1)S(1)}, bf16[2,32,2,256]{3,2,1,0:T(2,128)(2,1)S(1)}, u32[]{:S(2)}, u32[]{:S(2)}) collective-permute-start(bf16[2,32,2,256]{3,2,1,0:T(2,128)(2,1)S(1)} %shard_map.85.after), channel_id=1, source_target_pairs={{0,1},{1,2},{2,3},{3,4},{4,5},{5,6},{6,7},{7,8},{8,9},{9,10},{10,1... | collective-permute-start | bytes 196616 | tf_op jit(solution)/shard_map/ppermute | solution.py:39
  14.3 1.8 %collective-permute-start.3 = (bf16[9,16,25]{2,1,0:T(8,128)(2,1)S(1)}, bf16[9,16,25]{2,1,0:T(8,128)(2,1)S(1)}, u32[]{:S(2)}, u32[]{:S(2)}) collective-permute-start(bf16[9,16,25]{2,1,0:T(8,128)(2,1)S(1)} %select_bitcast_fusion.mo), channel_id=1, source_target_pairs={{0,32},{1,33},{2,34},{3,35},{4,36},{5,37},{6,38},{7,39},{8,40},{9,... | collective-permute-start | bytes 21608 | tf_op jit(solution)/shard_map/ppermute | solution.py:39
  17.9 1.5 %collective-permute-start.4 = (bf16[2,32,2,256]{3,2,1,0:T(2,128)(2,1)S(1)}, bf16[2,32,2,256]{3,2,1,0:T(2,128)(2,1)S(1)}, u32[]{:S(2)}, u32[]{:S(2)}) collective-permute-start(bf16[2,32,2,256]{3,2,1,0:T(2,128)(2,1)S(1)} %collective-permute-done.2.near), channel_id=1, source_target_pairs={{0,32},{1,33},{2,34},{3,35},{4,36},{5,37},{6,38},{7,39},{8,40},{9,... | collective-permute-start | bytes 196616 | tf_op jit(solution)/shard_map/ppermute | solution.py:39
  19.4 3.8 %collective-permute-start.5 = (bf16[2,2,40,256]{3,2,1,0:T(8,128)(2,1)S(1)}, bf16[2,2,40,256]{3,2,1,0:T(8,128)(2,1)S(1)}, u32[]{:S(2)}, u32[]{:S(2)}) collective-permute-start(bf16[2,2,40,256]{3,2,1,0:T(8,128)(2,1)S(1)} %shard_map.88), channel_id=1, source_target_pairs={{0,64},{1,65},{2,66},{3,67},{4,68},{5,69},{6,70},{7,71},{8,72},{9,... | collective-permute-start | bytes 245768 | tf_op jit(solution)/shard_map/ppermute | solution.py:39
  22.2 8.4 %copy-start = (bf16[16,32,256]{2,1,0:T(8,128)(2,1)S(1)}, bf16[16,32,256]{2,1,0:T(8,128)(2,1)}, u32[]{:S(2)}) copy-start(bf16[16,32,256]{2,1,0:T(8,128)(2,1)} %fo.1) | copy-start | bytes 786436
  22.3 8.4 %copy-start.2 = (bf16[9,256,256]{2,1,0:T(8,128)(2,1)S(1)}, bf16[9,256,256]{2,1,0:T(8,128)(2,1)}, u32[]{:S(2)}) copy-start(bf16[9,256,256]{2,1,0:T(8,128)(2,1)} %param.10) | copy-start | bytes 3538948
  24.6 17.5 %all-to-all-start = ((bf16[64,9,4,128]{3,2,1,0:T(4,128)(2,1)}), bf16[64,9,4,128]{3,2,1,0:T(4,128)(2,1)S(1)}, u32[]{:S(2)}, u32[]{:S(2)}) async-start(bf16[64,9,4,128]{3,2,1,0:T(4,128)(2,1)} %get-tuple-element.34), calls=%async_computation | async-start | bytes 1179648 | tf_op jit(solution)/shard_map/all_to_all | solution.py:511
  30.6 18.8 %copy-start.1 = (bf16[16,32,256]{2,1,0:T(8,128)(2,1)S(1)}, bf16[16,32,256]{2,1,0:T(8,128)(2,1)}, u32[]{:S(2)}) copy-start(bf16[16,32,256]{2,1,0:T(8,128)(2,1)} %co.1) | copy-start | bytes 786436
  43.2 17.1 %all-to-all-start.1 = ((bf16[64,9,4,128]{3,2,1,0:T(4,128)(2,1)}), bf16[64,9,4,128]{3,2,1,0:T(4,128)(2,1)S(1)}, u32[]{:S(2)}, u32[]{:S(2)}) async-start(bf16[64,9,4,128]{3,2,1,0:T(4,128)(2,1)} %get-tuple-element.36), calls=%async_computation.1 | async-start | bytes 1179648 | tf_op jit(solution)/shard_map/all_to_all | solution.py:537
  60.3 5.1 %collective-permute-start.6 = (bf16[64,9,4,128]{3,2,1,0:T(4,128)(2,1)S(1)}, bf16[64,9,4,128]{3,2,1,0:T(4,128)(2,1)S(1)}, u32[]{:S(2)}, u32[]{:S(2)}) collective-permute-start(bf16[64,9,4,128]{3,2,1,0:T(4,128)(2,1)S(1)} %all-to-all-done.1.mine), channel_id=1, source_target_pairs={{0,32},{1,33},{2,34},{3,35},{4,36},{5,37},{6,38},{7,39},{8,40},{9,... | collective-permute-start | bytes 1769480 | tf_op jit(solution)/shard_map/ppermute | solution.py:39

commit v6 on v5

--- a/solution.py
+++ b/solution.py
@@ -254,17 +254,17 @@
         grad[k] = total[:, k * HALF : (k + 1) * HALF].T
 
 
-def runs(k, side, half):
-    begin, at = half * 288 + side * 144 + k * 16, 0
-    while at < 16:
-        slot, j = divmod(begin + at, 64)
-        count = min(16 - at, 64 - j)
-        yield at, slot, j, count
-        at += count
+def quarters():
+    for side in range(2):
+        for half in range(2):
+            first = (half * 2 + side) * 16
+            lanes = slice(side * HALF, (side + 1) * HALF)
+            yield slice(first, first + 16), slice(half * 4, (half + 1) * 4), lanes
 
 
 def weight_end_kernel(
-    own, fx, cx, near, far, rows, bo, bx, grad, parts, token, field, cot, tile
+    own, fx, cx, near, far, rows, bo, bx, grad, out, token,
+    field, cot, tile, parts, sems
 ):
     mark(token)
     xl, core = here()
@@ -291,15 +291,17 @@
         basis.append(
             jnp.dot(tile[r, :, 0 : BAND * SLOTS], window, preferred_element_type=f32)
         )
+    sends = []
     for k in range(BASIS):
         cells = jnp.concatenate([x[k * CELLS : (k + 1) * CELLS] for x in basis], 0)
         total = grad[k] + jnp.dot(cells.T.astype(bf16), cot[...], preferred_element_type=f32)
-        for side in range(2):
-            tiles = total[:, side * HALF : (side + 1) * HALF].reshape(16, 8, HALF)
-            for half in range(2):
-                piece = tiles[:, half * 4 : (half + 1) * 4, :].astype(bf16)
-                for at, slot, j, count in runs(k, side, half):
-                    parts[j : j + count, slot] = piece[at : at + count]
+        tiles = total.reshape(16, 8, CHAN)
+        for chunks, rows_, columns in quarters():
+            parts[chunks, k] = tiles[:, rows_, columns].astype(bf16)
+        sends.append(pltpu.make_async_copy(parts.at[:, k], out.at[:, k], sems.at[k]))
+        sends[-1].start()
+    for x in sends:
+        x.wait()
 
 
 def sum_kernel(scale, parts, after, out, token, copies, sems):
@@ -319,15 +321,8 @@
     first = half_of() * 16
     copies = []
     for k in range(BASIS):
-        for side in range(2):
-            for half in range(2):
-                for at, slot, j, count in runs(k, side, half):
-                    stage[
-                        k,
-                        at : at + count,
-                        half * 4 : (half + 1) * 4,
-                        side * HALF : (side + 1) * HALF,
-                    ] = tiles_ref[j : j + count, slot].astype(f32)
+        for chunks, rows_, columns in quarters():
+            stage[k, :, rows_, columns] = tiles_ref[chunks, k].astype(f32)
         copies.append(
             pltpu.make_async_copy(stage.at[k], out.at[k, pl.ds(first, 16)], sems.at[k])
         )
@@ -502,7 +497,10 @@
             pltpu.VMEM((6, SLOTS, HALF), bf16),
             pltpu.VMEM((2 * CELLS, CHAN), bf16),
             pltpu.VMEM((2, BASIS * CELLS, CHAN), bf16),
+            pltpu.VMEM((64, *CHUNK), bf16),
+            pltpu.SemaphoreType.DMA((BASIS,)),
         ],
+        to=(0,),
         flops=2 * 64 * 1152 * 256,
         traffic=3 * 2**20,
     )

time: 67 us -> 67 us (level)
  no operation moved by 1% of the time
where the time goes in v6:
time: 67 us; the launch traced here: 66.6 us
  starting transfers between devices  27.1 us (40%)
  Pallas kernels  20.3 us (30%)
  waiting for transfers between devices  15.7 us (23%)
  other arithmetic  2.61 us (4%)
  between operations  0.95 us (1%)
    pallas_call x11, Pallas kernels, call(): pl.pallas_call(kernel, out_shape=[jax.ShapeDtypeStruct(*o) for o in outs]...  20.3 us
    ppermute x7, starting transfers between devices, send(): return lax.ppermute(x, AXES, moves(**way))  14.9 us
    all_to_all x1, waiting for transfers between devices, shards(): swapped = lax.all_to_all(parts, RING, 0, 0, tiled=True)  7.77 us
    all_to_all x1, starting transfers between devices, shards(): mine = lax.all_to_all(shared, RING, 0, 0, tiled=True)  6.21 us
    all_to_all x1, starting transfers between devices, shards(): swapped = lax.all_to_all(parts, RING, 0, 0, tiled=True)  5.99 us
    all_to_all x1, waiting for transfers between devices, shards(): mine = lax.all_to_all(shared, RING, 0, 0, tiled=True)  5 us
    ppermute x7, waiting for transfers between devices, send(): return lax.ppermute(x, AXES, moves(**way))  2.89 us
  transfers between devices with their start and end apart: 9, of which 7 were waited for; matrix products, arithmetic and copies ran while one was open for 4% of the time, Pallas kernels for 25%

profile of v6, /device:TPU:1, one launch (start us, length us, event | category | flops | bytes accessed | tf_op | source)
XLA Modules:
  0.0 66.6 jit_solution(13633916156570474033)
XLA Ops:
  0.6 1.5 %collective-permute-start = (bf16[16,32,256]{2,1,0:T(8,128)(2,1)}, bf16[16,32,256]{2,1,0:T(8,128)(2,1)S(1)}, u32[]{:S(2)}, u32[]{:S(2)}) collective-permute-start(bf16[16,32,256]{2,1,0:T(8,128)(2,1)} %fo.1), channel_id=1, source_target_pairs={{0,32},{1,33},{2,34},{3,35},{4,36},{5,37},{6,38},{7,39},{8,40},{9,... | collective-permute-start | bytes 786440 | tf_op jit(solution)/shard_map/ppermute | solution.py:39
  2.1 0.1 collective-permute-start.1
  2.2 1.1 %pad_maximum_fusion.own = bf16[2,16,32,256]{3,2,1,0:T(8,128)(2,1)S(1)} fusion(bf16[1,16,32,256]{3,2,1,0:T(8,128)(2,1)} %bitcast.7, bf16[1,16,32,256]{3,2,1,0:T(8,128)(2,1)} %bitcast.6), kind=kLoop, calls=%fused_computation | loop fusion | flops 262144 | bytes 1048576 | tf_op jit(solution)/shard_map/stack | solution.py:429
  3.3 0.2 collective-permute-done.fx
  3.5 0.4 collective-permute-done.1.cx
  3.9 0.1 shard_map.85.after
  4.0 8.8 %collective-permute-start.2 = (bf16[2,32,2,256]{3,2,1,0:T(2,128)(2,1)S(1)}, bf16[2,32,2,256]{3,2,1,0:T(2,128)(2,1)S(1)}, u32[]{:S(2)}, u32[]{:S(2)}) collective-permute-start(bf16[2,32,2,256]{3,2,1,0:T(2,128)(2,1)S(1)} %shard_map.85.after), channel_id=1, source_target_pairs={{0,1},{1,2},{2,3},{3,4},{4,5},{5,6},{6,7},{7,8},{8,9},{9,10},{10,1... | collective-permute-start | bytes 196616 | tf_op jit(solution)/shard_map/ppermute | solution.py:39
  12.8 0.7 %fusion.2 = pred[16,25]{1,0:T(8,128)(4,1)S(1)} fusion(s32[16]{0:T(128)} %param.9, s32[16]{0:T(128)} %param.8, s32[25]{0:T(128)S(1)} %and_select_fusion, s32[16]{0:T(128)S(1)} %add_add_fusion), kind=kLoop, calls=%fused_computation.5 | loop fusion | flops 2000 | bytes 692 | tf_op jit(solution)/shard_map/and | solution.py:447
  13.5 0.8 %select_bitcast_fusion.mo = bf16[9,16,25]{2,1,0:T(8,128)(2,1)S(1)} fusion(bf16[16,9,25]{2,0,1:T(8,128)(2,1)} %param.7, pred[16,25]{1,0:T(8,128)(4,1)S(1)} %fusion.2), kind=kLoop, calls=%fused_computation.1 | loop fusion | flops 3600 | bytes 14800 | tf_op jit(solution)/shard_map/jit(_where)/select_n | solution.py:448
  14.3 0.0 collective-permute-start.3
  14.3 1.8 %shard_map.86 = (bf16[16,288,256]{2,1,0:T(8,128)(2,1)S(1)}, bf16[256,512]{1,0:T(8,128)(2,1)S(1)}, bf16[16,256]{1,0:T(8,128)(2,1)S(1)}) custom-call(bf16[9,16,25]{2,1,0:T(8,128)(2,1)S(1)} %select_bitcast_fusion.mo, bf16[2,16,32,256]{3,2,1,0:T(8,128)(2,1)S(1)} %pad_maximum_fusion.own, bf16[2,32,2,256]{3,2,1,0:T(2,128)(2,1)S(1)} %shard_map.85.after), custom_call_target="tpu_custom_call" | custom-call | flops 94371840 | bytes 4194304 | tf_op jit(solution)/shard_map/pallas_call | solution.py:61
  16.1 0.0 collective-permute-done.3.mx
  16.1 1.8 %shard_map.87 = (bf16[16,288,256]{2,1,0:T(8,128)(2,1)S(1)}, bf16[256,512]{1,0:T(8,128)(2,1)S(1)}, bf16[16,256]{1,0:T(8,128)(2,1)S(1)}) custom-call(bf16[9,16,25]{2,1,0:T(8,128)(2,1)S(1)} %collective-permute-done.3.mx, bf16[16,32,256]{2,1,0:T(8,128)(2,1)S(1)} %collective-permute-done.1.cx, bf16[16,256]{1,0:T(8,128)(2,1)S(1)} %get-tuple-element.24.after.to), custom_call_target="tpu_custom_call" | custom-call | flops 94371840 | bytes 4194304 | tf_op jit(solution)/shard_map/pallas_call | solution.py:61
  17.9 0.0 collective-permute-done.2.near
  17.9 0.6 collective-permute-start.4
  18.5 0.9 %collective-permute-done.4.far = bf16[2,32,2,256]{3,2,1,0:T(2,128)(2,1)S(1)} collective-permute-done((bf16[2,32,2,256]{3,2,1,0:T(2,128)(2,1)S(1)}, bf16[2,32,2,256]{3,2,1,0:T(2,128)(2,1)S(1)}, u32[]{:S(2)}, u32[]{:S(2)}) %collective-permute-start.4) | collective-permute-done | bytes 65568 | tf_op jit(solution)/shard_map/ppermute | solution.py:39
  19.4 0.4 collective-permute-start.5
  19.8 2.5 %shard_map.89.grad = f32[9,128,256]{2,1,0:T(8,128)S(1)} custom-call(bf16[2,16,32,256]{3,2,1,0:T(8,128)(2,1)S(1)} %pad_maximum_fusion.own, bf16[16,32,256]{2,1,0:T(8,128)(2,1)S(1)} %collective-permute-done.fx, bf16[2,32,2,256]{3,2,1,0:T(2,128)(2,1)S(1)} %collective-permute-done.2.near, bf16[2,32,2,256]{3,2,1,0:T(2,128)(2,1)S(1)} %collective-permute-done.4.far, ...), custom_call_target="tpu_custom_call" | custom-call | flops 1811939328 | bytes 7340032 | tf_op jit(solution)/shard_map/pallas_call | solution.py:61
  22.2 0.0 copy-start
  22.3 0.0 copy-start.2
  22.3 0.9 %collective-permute-done.5.rows = bf16[2,2,40,256]{3,2,1,0:T(8,128)(2,1)S(1)} collective-permute-done((bf16[2,2,40,256]{3,2,1,0:T(8,128)(2,1)S(1)}, bf16[2,2,40,256]{3,2,1,0:T(8,128)(2,1)S(1)}, u32[]{:S(2)}, u32[]{:S(2)}) %collective-permute-start.5) | collective-permute-done | bytes 81952 | tf_op jit(solution)/shard_map/ppermute | solution.py:39
  23.2 1.4 %shard_map.90 = (bf16[64,9,4,128]{3,2,1,0:T(4,128)(2,1)}, f32[8,128]{1,0:T(8,128)S(1)}) custom-call(bf16[2,16,32,256]{3,2,1,0:T(8,128)(2,1)S(1)} %pad_maximum_fusion.own, bf16[16,32,256]{2,1,0:T(8,128)(2,1)S(1)} %collective-permute-done.fx, bf16[16,32,256]{2,1,0:T(8,128)(2,1)S(1)} %collective-permute-done.1.cx, ...), custom_call_target="tpu_custom_call" | custom-call | flops 37748736 | bytes 3145728 | tf_op jit(solution)/shard_map/pallas_call | solution.py:61
  24.6 6.0 %all-to-all-start = ((bf16[64,9,4,128]{3,2,1,0:T(4,128)(2,1)}), bf16[64,9,4,128]{3,2,1,0:T(4,128)(2,1)S(1)}, u32[]{:S(2)}, u32[]{:S(2)}) async-start(bf16[64,9,4,128]{3,2,1,0:T(4,128)(2,1)} %get-tuple-element.34), calls=%async_computation | async-start | bytes 1179648 | tf_op jit(solution)/shard_map/all_to_all | solution.py:509
  30.6 0.0 copy-done
  30.6 0.0 copy-done.2
  30.6 0.0 copy-start.1
  30.6 3.7 %shard_map.91 = (bf16[16,32,256]{2,1,0:T(8,128)(2,1)}, f32[8,128]{1,0:T(8,128)S(1)}) custom-call(bf16[16,32,256]{2,1,0:T(8,128)(2,1)S(1)} %copy-done, bf16[16,32,256]{2,1,0:T(8,128)(2,1)S(1)} %collective-permute-done.fx, bf16[2,32,2,256]{3,2,1,0:T(2,128)(2,1)S(1)} %collective-permute-done.2.near, bf16[2,32,2,256]{3,2,1,0:T(2,128)(2,1)S(1)} %collective-permute-done.4.far, ...), custom_call_target="tpu_custom_call" | custom-call | flops 1207959552 | bytes 8388608 | tf_op jit(solution)/shard_map/pallas_call | solution.py:61
  34.3 7.8 %all-to-all-done.parts = bf16[64,9,4,128]{3,2,1,0:T(4,128)(2,1)S(1)} async-done(((bf16[64,9,4,128]{3,2,1,0:T(4,128)(2,1)}), bf16[64,9,4,128]{3,2,1,0:T(4,128)(2,1)S(1)}, u32[]{:S(2)}, u32[]{:S(2)}) %all-to-all-start) | async-done | bytes 589856 | tf_op jit(solution)/shard_map/all_to_all | solution.py:509
  42.0 1.1 %shard_map.92 = (bf16[64,9,4,128]{3,2,1,0:T(4,128)(2,1)}, f32[8,128]{1,0:T(8,128)S(1)}) custom-call(bf16[64,9,4,128]{3,2,1,0:T(4,128)(2,1)S(1)} %all-to-all-done.parts, f32[8,128]{1,0:T(8,128)S(1)} %get-tuple-element.35.after), custom_call_target="tpu_custom_call" | custom-call | bytes 1048576 | tf_op jit(solution)/shard_map/pallas_call | solution.py:61
  43.2 6.2 %all-to-all-start.1 = ((bf16[64,9,4,128]{3,2,1,0:T(4,128)(2,1)}), bf16[64,9,4,128]{3,2,1,0:T(4,128)(2,1)S(1)}, u32[]{:S(2)}, u32[]{:S(2)}) async-start(bf16[64,9,4,128]{3,2,1,0:T(4,128)(2,1)} %get-tuple-element.36), calls=%async_computation.1 | async-start | bytes 1179648 | tf_op jit(solution)/shard_map/all_to_all | solution.py:535
  49.4 0.0 copy-done.1
  49.4 5.8 %shard_map.93 = (bf16[16,32,256]{2,1,0:T(8,128)(2,1)}, f32[8,128]{1,0:T(8,128)}) custom-call(bf16[16,32,256]{2,1,0:T(8,128)(2,1)S(1)} %copy-done.1, bf16[16,32,256]{2,1,0:T(8,128)(2,1)S(1)} %collective-permute-done.1.cx, bf16[2,32,2,256]{3,2,1,0:T(2,128)(2,1)S(1)} %collective-permute-done.2.near, bf16[2,32,2,256]{3,2,1,0:T(2,128)(2,1)S(1)} %collective-permute-done.4.far, ...), custom_call_target="tpu_custom_call" | custom-call | flops 1971322880 | bytes 8388608 | tf_op jit(solution)/shard_map/pallas_call | solution.py:61
  55.2 5.0 %all-to-all-done.1.mine = bf16[64,9,4,128]{3,2,1,0:T(4,128)(2,1)S(1)} async-done(((bf16[64,9,4,128]{3,2,1,0:T(4,128)(2,1)}), bf16[64,9,4,128]{3,2,1,0:T(4,128)(2,1)S(1)}, u32[]{:S(2)}, u32[]{:S(2)}) %all-to-all-start.1) | async-done | bytes 589856 | tf_op jit(solution)/shard_map/all_to_all | solution.py:535
  60.2 3.5 %collective-permute-start.6 = (bf16[64,9,4,128]{3,2,1,0:T(4,128)(2,1)S(1)}, bf16[64,9,4,128]{3,2,1,0:T(4,128)(2,1)S(1)}, u32[]{:S(2)}, u32[]{:S(2)}) collective-permute-start(bf16[64,9,4,128]{3,2,1,0:T(4,128)(2,1)S(1)} %all-to-all-done.1.mine), channel_id=1, source_target_pairs={{0,32},{1,33},{2,34},{3,35},{4,36},{5,37},{6,38},{7,39},{8,40},{9,... | collective-permute-start | bytes 1769480 | tf_op jit(solution)/shard_map/ppermute | solution.py:39
  63.7 1.1 %shard_map.94.before = f32[9,32,8,256]{3,2,1,0:T(8,128)} custom-call(bf16[64,9,4,128]{3,2,1,0:T(4,128)(2,1)S(1)} %all-to-all-done.1.mine), custom_call_target="tpu_custom_call" | custom-call | bytes 2097152 | tf_op jit(solution)/shard_map/pallas_call | solution.py:61
  64.8 0.5 collective-permute-done.6.theirs
  65.4 1.1 %shard_map.95 = f32[9,32,8,256]{3,2,1,0:T(8,128)} custom-call(bf16[64,9,4,128]{3,2,1,0:T(4,128)(2,1)S(1)} %collective-permute-done.6.theirs, f32[9,32,8,256]{3,2,1,0:T(8,128)} %shard_map.94.before), custom_call_target="tpu_custom_call", output_to_operand_aliasing={{}: (1, {})} | custom-call | bytes 2097152 | tf_op jit(solution)/shard_map/pallas_call | solution.py:61
  (3 shorter events, 0.0 us)
Async XLA Ops:
  0.6 2.9 %collective-permute-start = (bf16[16,32,256]{2,1,0:T(8,128)(2,1)}, bf16[16,32,256]{2,1,0:T(8,128)(2,1)S(1)}, u32[]{:S(2)}, u32[]{:S(2)}) collective-permute-start(bf16[16,32,256]{2,1,0:T(8,128)(2,1)} %fo.1), channel_id=1, source_target_pairs={{0,32},{1,33},{2,34},{3,35},{4,36},{5,37},{6,38},{7,39},{8,40},{9,... | collective-permute-start | bytes 786440 | tf_op jit(solution)/shard_map/ppermute | solution.py:39
  2.1 1.7 %collective-permute-start.1 = (bf16[16,32,256]{2,1,0:T(8,128)(2,1)}, bf16[16,32,256]{2,1,0:T(8,128)(2,1)S(1)}, u32[]{:S(2)}, u32[]{:S(2)}) collective-permute-start(bf16[16,32,256]{2,1,0:T(8,128)(2,1)} %co.1), channel_id=1, source_target_pairs={{0,32},{1,33},{2,34},{3,35},{4,36},{5,37},{6,38},{7,39},{8,40},{9,... | collective-permute-start | bytes 786440 | tf_op jit(solution)/shard_map/ppermute | solution.py:39
  4.0 13.9 %collective-permute-start.2 = (bf16[2,32,2,256]{3,2,1,0:T(2,128)(2,1)S(1)}, bf16[2,32,2,256]{3,2,1,0:T(2,128)(2,1)S(1)}, u32[]{:S(2)}, u32[]{:S(2)}) collective-permute-start(bf16[2,32,2,256]{3,2,1,0:T(2,128)(2,1)S(1)} %shard_map.85.after), channel_id=1, source_target_pairs={{0,1},{1,2},{2,3},{3,4},{4,5},{5,6},{6,7},{7,8},{8,9},{9,10},{10,1... | collective-permute-start | bytes 196616 | tf_op jit(solution)/shard_map/ppermute | solution.py:39
  14.3 1.8 %collective-permute-start.3 = (bf16[9,16,25]{2,1,0:T(8,128)(2,1)S(1)}, bf16[9,16,25]{2,1,0:T(8,128)(2,1)S(1)}, u32[]{:S(2)}, u32[]{:S(2)}) collective-permute-start(bf16[9,16,25]{2,1,0:T(8,128)(2,1)S(1)} %select_bitcast_fusion.mo), channel_id=1, source_target_pairs={{0,32},{1,33},{2,34},{3,35},{4,36},{5,37},{6,38},{7,39},{8,40},{9,... | collective-permute-start | bytes 21608 | tf_op jit(solution)/shard_map/ppermute | solution.py:39
  17.9 1.5 %collective-permute-start.4 = (bf16[2,32,2,256]{3,2,1,0:T(2,128)(2,1)S(1)}, bf16[2,32,2,256]{3,2,1,0:T(2,128)(2,1)S(1)}, u32[]{:S(2)}, u32[]{:S(2)}) collective-permute-start(bf16[2,32,2,256]{3,2,1,0:T(2,128)(2,1)S(1)} %collective-permute-done.2.near), channel_id=1, source_target_pairs={{0,32},{1,33},{2,34},{3,35},{4,36},{5,37},{6,38},{7,39},{8,40},{9,... | collective-permute-start | bytes 196616 | tf_op jit(solution)/shard_map/ppermute | solution.py:39
  19.4 3.8 %collective-permute-start.5 = (bf16[2,2,40,256]{3,2,1,0:T(8,128)(2,1)S(1)}, bf16[2,2,40,256]{3,2,1,0:T(8,128)(2,1)S(1)}, u32[]{:S(2)}, u32[]{:S(2)}) collective-permute-start(bf16[2,2,40,256]{3,2,1,0:T(8,128)(2,1)S(1)} %shard_map.88), channel_id=1, source_target_pairs={{0,64},{1,65},{2,66},{3,67},{4,68},{5,69},{6,70},{7,71},{8,72},{9,... | collective-permute-start | bytes 245768 | tf_op jit(solution)/shard_map/ppermute | solution.py:39
  22.2 8.3 %copy-start = (bf16[16,32,256]{2,1,0:T(8,128)(2,1)S(1)}, bf16[16,32,256]{2,1,0:T(8,128)(2,1)}, u32[]{:S(2)}) copy-start(bf16[16,32,256]{2,1,0:T(8,128)(2,1)} %fo.1) | copy-start | bytes 786436
  22.3 8.3 %copy-start.2 = (bf16[9,256,256]{2,1,0:T(8,128)(2,1)S(1)}, bf16[9,256,256]{2,1,0:T(8,128)(2,1)}, u32[]{:S(2)}) copy-start(bf16[9,256,256]{2,1,0:T(8,128)(2,1)} %param.10) | copy-start | bytes 3538948
  24.6 17.5 %all-to-all-start = ((bf16[64,9,4,128]{3,2,1,0:T(4,128)(2,1)}), bf16[64,9,4,128]{3,2,1,0:T(4,128)(2,1)S(1)}, u32[]{:S(2)}, u32[]{:S(2)}) async-start(bf16[64,9,4,128]{3,2,1,0:T(4,128)(2,1)} %get-tuple-element.34), calls=%async_computation | async-start | bytes 1179648 | tf_op jit(solution)/shard_map/all_to_all | solution.py:509
  30.6 18.8 %copy-start.1 = (bf16[16,32,256]{2,1,0:T(8,128)(2,1)S(1)}, bf16[16,32,256]{2,1,0:T(8,128)(2,1)}, u32[]{:S(2)}) copy-start(bf16[16,32,256]{2,1,0:T(8,128)(2,1)} %co.1) | copy-start | bytes 786436
  43.2 17.1 %all-to-all-start.1 = ((bf16[64,9,4,128]{3,2,1,0:T(4,128)(2,1)}), bf16[64,9,4,128]{3,2,1,0:T(4,128)(2,1)S(1)}, u32[]{:S(2)}, u32[]{:S(2)}) async-start(bf16[64,9,4,128]{3,2,1,0:T(4,128)(2,1)} %get-tuple-element.36), calls=%async_computation.1 | async-start | bytes 1179648 | tf_op jit(solution)/shard_map/all_to_all | solution.py:535
  60.2 5.1 %collective-permute-start.6 = (bf16[64,9,4,128]{3,2,1,0:T(4,128)(2,1)S(1)}, bf16[64,9,4,128]{3,2,1,0:T(4,128)(2,1)S(1)}, u32[]{:S(2)}, u32[]{:S(2)}) collective-permute-start(bf16[64,9,4,128]{3,2,1,0:T(4,128)(2,1)S(1)} %all-to-all-done.1.mine), channel_id=1, source_target_pairs={{0,32},{1,33},{2,34},{3,35},{4,36},{5,37},{6,38},{7,39},{8,40},{9,... | collective-permute-start | bytes 1769480 | tf_op jit(solution)/shard_map/ppermute | solution.py:39

commit v7 on v6

--- a/solution.py
+++ b/solution.py
@@ -70,16 +70,15 @@
     )(*operands)
 
 
-def column_kernel(own, fx, cx, edge):
+def column_kernel(f, own, other, edge):
     _, core = here()
     for side in range(2):
 
         @pl.when(core == side)
         def _():
             cells = slice(CELLS - 2, CELLS) if side == 0 else slice(0, 2)
-            for f, other in enumerate((fx, cx)):
-                edge[f, 0:ROWS] = own[f, :, cells, :]
-                edge[f, ROWS : 2 * ROWS] = other[:, cells, :]
+            edge[0:ROWS] = own[f, :, cells, :]
+            edge[ROWS : 2 * ROWS] = other[:, cells, :]
 
 
 def boundary(xl, core):
@@ -94,36 +93,35 @@
     return [slice(p * ROWS + first, p * ROWS + first + count) for p in (part, 1 - part)]
 
 
-def row_kernel(own, fx, cx, near, far, to, tx, rows):
+def row_kernel(f, own, other, near, far, to, tx, rows):
     xl, core = here()
-    rows[:, :, 36:40, :] = jnp.zeros((2, 2, 4, CHAN), bf16)
+    rows[:, 36:40, :] = jnp.zeros((2, 4, CHAN), bf16)
     for chosen, part, first in boundary(xl, core):
 
         @pl.when(chosen)
         def _():
             span = slice(first, first + 2)
             side, cross = rows_of(part, first, 2)
-            for f, pair in enumerate(((own.at[0], fx), (own.at[1], cx))):
-                rows[f, :, 0:CELLS, :] = pair[part][span]
-                rows[f, :, CELLS : CELLS + 2, :] = near[f, side]
-                rows[f, :, CELLS + 2 : CELLS + 4, :] = far[f, cross]
-            rows[1, 0, 38:40, :] = (to, tx)[part][span]
-
-
-def padded(dst, f, xl, core, own, other, near, far, rows, lanes):
+            rows[:, 0:CELLS, :] = (own.at[f], other)[part][span]
+            rows[:, CELLS : CELLS + 2, :] = near[side]
+            rows[:, CELLS + 2 : CELLS + 4, :] = far[cross]
+            rows[0, 38:40, :] = (to, tx)[part][span]
+
+
+def padded(dst, xl, core, own, other, near, far, rows, lanes):
     width = dst.shape[-1]
     dst[:, 36:SLOTS, :] = jnp.zeros((36, SLOTS - 36, width), bf16)
     for part, ref in enumerate((own, other)):
         at = pl.ds(2 + ROWS * (core if part == 0 else 1 - core), ROWS)
         side, cross = rows_of(part, 0, ROWS)
         dst[at, 0:CELLS, :] = ref[:, :, lanes]
-        dst[at, CELLS : CELLS + 2, :] = near[f, side, :, lanes]
-        dst[at, CELLS + 2 : CELLS + 4, :] = far[f, cross, :, lanes]
+        dst[at, CELLS : CELLS + 2, :] = near[side, :, lanes]
+        dst[at, CELLS + 2 : CELLS + 4, :] = far[cross, :, lanes]
     if rows is None:
         dst[0:2] = jnp.zeros((2, SLOTS, width), bf16)
         dst[34:36] = jnp.zeros((2, SLOTS, width), bf16)
     else:
-        dst[pl.ds(34 * (1 - xl), 2), 0:36, :] = rows[f, :, 0:36, lanes]
+        dst[pl.ds(34 * (1 - xl), 2), 0:36, :] = rows[:, 0:36, lanes]
         dst[pl.ds(34 * xl, 2)] = jnp.zeros((2, SLOTS, width), bf16)
 
 
@@ -225,7 +223,7 @@
 def weight_kernel(own, fx, near, far, bo, bx, ct_o, ct_x, grad, field, basis):
     xl, core = here()
     lanes = pl.ds(pl.multiple_of(core * HALF, HALF), HALF)
-    padded(field, 0, xl, core, own.at[0], fx, near, far, None, lanes)
+    padded(field, xl, core, own.at[0], fx, near, far, None, lanes)
 
     for part, bands in enumerate((bo, bx)):
         begin = ROWS * (core if part == 0 else 1 - core)
@@ -263,14 +261,14 @@
 
 
 def weight_end_kernel(
-    own, fx, cx, near, far, rows, bo, bx, grad, out, token,
+    own, fx, cx, near, far, rows, after, bo, bx, grad, out, token,
     field, cot, tile, parts, sems
 ):
     mark(token)
     xl, core = here()
     lanes = pl.ds(pl.multiple_of(core * HALF, HALF), HALF)
     field[:, 36:SLOTS, :] = jnp.zeros((6, SLOTS - 36, HALF), bf16)
-    field[pl.ds(4 * (1 - xl), 2), 0:36, :] = rows[0, :, 0:36, lanes]
+    field[pl.ds(4 * (1 - xl), 2), 0:36, :] = rows[:, 0:36, lanes]
     for chosen, part, first in boundary(xl, core):
 
         @pl.when(chosen)
@@ -280,8 +278,8 @@
             begin = 0 if first == 0 else 12
             side, cross = rows_of(part, begin, 4)
             field[at : at + 4, 0:CELLS, :] = ref[begin : begin + 4, :, lanes]
-            field[at : at + 4, CELLS : CELLS + 2, :] = near[0, side, :, lanes]
-            field[at : at + 4, CELLS + 2 : CELLS + 4, :] = far[0, cross, :, lanes]
+            field[at : at + 4, CELLS : CELLS + 2, :] = near[side, :, lanes]
+            field[at : at + 4, CELLS + 2 : CELLS + 4, :] = far[cross, :, lanes]
             cot[...] = (own.at[1], cx)[part][first : first + 2].reshape(2 * CELLS, CHAN)
             tile[...] = (bo, bx)[part][first : first + 2]
 
@@ -347,7 +345,7 @@
     xl, core = here()
     copy = pltpu.make_async_copy(w_hbm, weight, sems)
     copy.start()
-    padded(field, 0, xl, core, fo, fx, near, far, rows, slice(None))
+    padded(field, xl, core, fo, fx, near, far, rows, slice(None))
     tap_lines(mo, lines)
     masks = band_masks(CHAN)
     for n in range(ROWS):
@@ -380,7 +378,7 @@
     xl, core = here()
     lanes = 512
     around = ROWS + 4
-    padded(field, 1, xl, core, co, cx, near, far, rows, slice(None))
+    padded(field, xl, core, co, cx, near, far, rows, slice(None))
 
     count = around * 8
     row = iota((count, 1), 0)
@@ -389,7 +387,7 @@
     rep = jnp.dot(one_hot(row, 8, 2, 16, count), to[...], preferred_element_type=f32)
     rep += jnp.dot(one_hot(row, 8, other, 16, count), tx[...], preferred_element_type=f32)
     rep += jnp.dot(
-        one_hot(row, 8, beyond, 2, count), rows[1, 0, 38:40, :], preferred_element_type=f32
+        one_hot(row, 8, beyond, 2, count), rows[0, 38:40, :], preferred_element_type=f32
     )
     _, b, _ = split_taps(iota((1, CHAN), 1))
     k, _, s = split_taps(iota((CHAN, 1), 0))
@@ -432,15 +430,14 @@
     tiles = ((ROWS, BASIS * CELLS, CHAN), bf16)
     flat = ((ROWS, CHAN), bf16)
     lines = pltpu.VMEM((BASIS * ROWS, BAND * CHAN), f32)
-    (edge,) = call(
-        column_kernel,
-        [((2, 2 * ROWS, 2, CHAN), bf16)],
-        (own, fx, cx),
-        traffic=2**20,
-        limit=8,
-    )
-    edge, start = lax.optimization_barrier((edge, start))
-    near = send(edge, lon=(1, -1))
+    column = ((2 * ROWS, 2, CHAN), bf16)
+    edges = [
+        call(functools.partial(column_kernel, f), [column], (own, other), traffic=2**20, limit=8)[0]
+        for f, other in enumerate((fx, cx))
+    ]
+    near_f = send(edges[0], lon=(1, -1))
+    near_c = send(edges[1], lon=(1, -1))
+    edge, start = lax.optimization_barrier((edges[0], start))
     lat = lax.axis_index("xl") * 2 + lax.axis_index("core")
     source = lat * ROWS + jnp.arange(ROWS, dtype=jnp.int32)[:, None] - 2
     source = source + jnp.arange(25, dtype=jnp.int32)[None, :] // BAND - start[:, None]
@@ -467,21 +464,27 @@
         traffic=4 * 2**20,
         limit=16,
     )
-    near, bx = lax.optimization_barrier((near, bx))
-    far = send(near, core=True)
-    halo = (near, far)
-
-    (rows,) = call(
-        row_kernel,
-        [((2, 2, 40, CHAN), bf16)],
-        (own, fx, cx, *halo, to, tx),
-        traffic=2**20,
-    )
-    rows = send(rows, lat=True)
+    near_f, bx = lax.optimization_barrier((near_f, bx))
+    far_f = send(near_f, core=True)
+    far_c = send(near_c, core=True)
+
+    sides = ((near_f, far_f), (near_c, far_c))
+    rows_f, rows_c = [
+        send(
+            call(
+                functools.partial(row_kernel, f),
+                [((2, 40, CHAN), bf16)],
+                (own, other, *sides[f], to, tx),
+                traffic=2**20,
+            )[0],
+            lat=True,
+        )
+        for f, other in enumerate((fx, cx))
+    ]
     (grad,) = call(
         weight_kernel,
         [((BASIS, HALF, CHAN), f32)],
-        (own, fx, *halo, bo, bx, ct_o, ct_x),
+        (own, fx, *sides[0], bo, bx, ct_o, ct_x),
         scratch=[
             pltpu.VMEM((36, SLOTS, HALF), bf16),
             pltpu.VMEM((1024, BASIS * HALF), bf16),
@@ -492,7 +495,7 @@
     parts, after = call(
         weight_end_kernel,
         [((64, *CHUNK), bf16), TOKEN],
-        (own, fx, cx, *halo, rows, bo, bx, grad),
+        (own, fx, cx, *sides[0], rows_f, rows_c, bo, bx, grad),
         scratch=[
             pltpu.VMEM((6, SLOTS, HALF), bf16),
             pltpu.VMEM((2 * CELLS, CHAN), bf16),
@@ -510,7 +513,7 @@
     mixed, after = call(
         mixed_kernel,
         [block, TOKEN],
-        (feature, fx, *halo, rows, mo, mixing, after),
+        (feature, fx, *sides[0], rows_f, mo, mixing, after),
         scratch=[
             pltpu.VMEM((36, SLOTS, CHAN), bf16),
             pltpu.VMEM((512, BASIS * CHAN), bf16),
@@ -536,7 +539,7 @@
     grad_feature, after = call(
         feature_kernel,
         [block, TOKEN],
-        (cotangent, cx, *halo, rows, to, tx, mixing, after),
+        (cotangent, cx, *sides[1], rows_c, to, tx, mixing, after),
         scratch=[
             pltpu.VMEM((36, SLOTS, CHAN), bf16),
             pltpu.VMEM(((ROWS + 4) * 8, BAND * 512), f32),

time: 67 us -> 66.3 us (0.990)
  starting transfers between devices: 27.1 us -> 29.5 us
  waiting for transfers between devices: 15.7 us -> 13.9 us
  other arithmetic: 2.61 us -> 1.18 us
    ppermute x7 -> x10, starting transfers between devices: 14.9 us -> 16.6 us  [send(): return lax.ppermute(x, AXES, moves(**way))]
    ppermute x7 -> x10, waiting for transfers between devices: 2.89 us -> 1.48 us  [send(): return lax.ppermute(x, AXES, moves(**way))]
    select_n x1, other arithmetic: 0.78 us -> 0.01 us  [shards(): jnp.where(inside[None], filters.transpose(1, 0, 2), jnp.zeros((), bf16))]
    pallas_call x11 -> x13, Pallas kernels: 20.3 us -> 20.3 us  [call(): pl.pallas_call(kernel, out_shape=[jax.ShapeDtypeStruct(*o) for o in outs]...]
  transfers between devices with their start and end apart: 9 -> 12, of which waited for: 7 -> 5; matrix products, arithmetic and copies ran while one was open for 4% -> 2% of each run, Pallas kernels for 25% -> 25%
where the time goes in v7:
time: 66.3 us; the launch traced here: 66 us
  starting transfers between devices  29.5 us (44%)
  Pallas kernels  20.3 us (31%)
  waiting for transfers between devices  13.9 us (21%)
  other arithmetic  1.18 us (2%)
  between operations  1.02 us (2%)
    pallas_call x13, Pallas kernels, call(): pl.pallas_call(kernel, out_shape=[jax.ShapeDtypeStruct(*o) for o in outs]...  20.3 us
    ppermute x10, starting transfers between devices, send(): return lax.ppermute(x, AXES, moves(**way))  16.6 us
    all_to_all x1, waiting for transfers between devices, shards(): swapped = lax.all_to_all(parts, RING, 0, 0, tiled=True)  7.3 us
    all_to_all x1, starting transfers between devices, shards(): mine = lax.all_to_all(shared, RING, 0, 0, tiled=True)  6.48 us
    all_to_all x1, starting transfers between devices, shards(): swapped = lax.all_to_all(parts, RING, 0, 0, tiled=True)  6.4 us
    all_to_all x1, waiting for transfers between devices, shards(): mine = lax.all_to_all(shared, RING, 0, 0, tiled=True)  5.17 us
    ppermute x10, waiting for transfers between devices, send(): return lax.ppermute(x, AXES, moves(**way))  1.48 us
  transfers between devices with their start and end apart: 12, of which 5 were waited for; matrix products, arithmetic and copies ran while one was open for 2% of the time, Pallas kernels for 25%

profile of v7, /device:TPU:1, one launch (start us, length us, event | category | flops | bytes accessed | tf_op | source)
XLA Modules:
  0.0 66.0 jit_solution(2332319456367256701)
XLA Ops:
  0.6 0.0 copy-start.5
  0.6 0.0 copy-start.4
  0.7 0.0 copy-start.3
  0.7 1.5 %collective-permute-start = (bf16[16,32,256]{2,1,0:T(8,128)(2,1)}, bf16[16,32,256]{2,1,0:T(8,128)(2,1)S(1)}, u32[]{:S(2)}, u32[]{:S(2)}) collective-permute-start(bf16[16,32,256]{2,1,0:T(8,128)(2,1)} %fo.1), channel_id=1, source_target_pairs={{0,32},{1,33},{2,34},{3,35},{4,36},{5,37},{6,38},{7,39},{8,40},{9,... | collective-permute-start | bytes 786440 | tf_op jit(solution)/shard_map/ppermute | solution.py:39
  2.2 0.1 collective-permute-start.3
  2.3 1.1 %pad_maximum_fusion.own = bf16[2,16,32,256]{3,2,1,0:T(8,128)(2,1)S(1)} fusion(bf16[1,16,32,256]{3,2,1,0:T(8,128)(2,1)} %bitcast.7, bf16[1,16,32,256]{3,2,1,0:T(8,128)(2,1)} %bitcast.6), kind=kLoop, calls=%fused_computation | loop fusion | flops 262144 | bytes 1048576 | tf_op jit(solution)/shard_map/stack | solution.py:427
  3.4 0.2 collective-permute-done.other.fx
  3.6 8.8 %collective-permute-start.1 = (bf16[32,2,256]{2,1,0:T(2,128)(2,1)S(1)}, bf16[32,2,256]{2,1,0:T(2,128)(2,1)S(1)}, u32[]{:S(2)}, u32[]{:S(2)}) collective-permute-start(bf16[32,2,256]{2,1,0:T(2,128)(2,1)S(1)} %shard_map.85.after), channel_id=1, source_target_pairs={{0,1},{1,2},{2,3},{3,4},{4,5},{5,6},{6,7},{7,8},{8,9},{9,10},{10,1... | collective-permute-start | bytes 98312 | tf_op jit(solution)/shard_map/ppermute | solution.py:39
  12.4 0.0 collective-permute-done.3.cx.other
  12.4 0.3 collective-permute-start.6
  12.8 0.0 copy-done.5
  12.8 0.0 copy-done.4
  12.8 0.1 fusion.2
  12.8 0.0 copy-done.3
  12.9 0.1 collective-permute-start.2
  13.0 1.8 %shard_map.86 = (bf16[16,288,256]{2,1,0:T(8,128)(2,1)S(1)}, bf16[256,512]{1,0:T(8,128)(2,1)S(1)}, bf16[16,256]{1,0:T(8,128)(2,1)S(1)}) custom-call(bf16[9,16,25]{2,1,0:T(8,128)(2,1)S(1)} %select_bitcast_fusion.mo, bf16[2,16,32,256]{3,2,1,0:T(8,128)(2,1)S(1)} %pad_maximum_fusion.own, bf16[32,2,256]{2,1,0:T(2,128)(2,1)S(1)} %shard_map.85.after), custom_call_target="tpu_custom_call" | custom-call | flops 94371840 | bytes 4194304 | tf_op jit(solution)/shard_map/pallas_call | solution.py:61
  14.8 0.0 collective-permute-done.2.mx
  14.8 1.8 %shard_map.87 = (bf16[16,288,256]{2,1,0:T(8,128)(2,1)S(1)}, bf16[256,512]{1,0:T(8,128)(2,1)S(1)}, bf16[16,256]{1,0:T(8,128)(2,1)S(1)}) custom-call(bf16[9,16,25]{2,1,0:T(8,128)(2,1)S(1)} %collective-permute-done.2.mx, bf16[16,32,256]{2,1,0:T(8,128)(2,1)S(1)} %collective-permute-done.3.cx.other, bf16[16,256]{1,0:T(8,128)(2,1)S(1)} %get-tuple-element.24.after.to), custom_call_target="tpu_custom_call" | custom-call | flops 94371840 | bytes 4194304 | tf_op jit(solution)/shard_map/pallas_call | solution.py:61
  16.6 0.0 collective-permute-done.1.near
  16.6 0.6 collective-permute-start.4
  17.1 0.0 collective-permute-done.6.near
  17.1 0.1 collective-permute-start.7
  17.2 0.8 %collective-permute-done.4.far = bf16[32,2,256]{2,1,0:T(2,128)(2,1)S(1)} collective-permute-done((bf16[32,2,256]{2,1,0:T(2,128)(2,1)S(1)}, bf16[32,2,256]{2,1,0:T(2,128)(2,1)S(1)}, u32[]{:S(2)}, u32[]{:S(2)}) %collective-permute-start.4) | collective-permute-done | bytes 32800 | tf_op jit(solution)/shard_map/ppermute | solution.py:39
  18.0 0.4 collective-permute-start.5
  18.4 0.0 collective-permute-done.7.far
  18.4 1.2 %collective-permute-start.8 = (bf16[2,40,256]{2,1,0:T(8,128)(2,1)S(1)}, bf16[2,40,256]{2,1,0:T(8,128)(2,1)S(1)}, u32[]{:S(2)}, u32[]{:S(2)}) collective-permute-start(bf16[2,40,256]{2,1,0:T(8,128)(2,1)S(1)} %shard_map.90), channel_id=1, source_target_pairs={{0,64},{1,65},{2,66},{3,67},{4,68},{5,69},{6,70},{7,71},{8,72},{9,... | collective-permute-start | bytes 122888 | tf_op jit(solution)/shard_map/ppermute | solution.py:39
  19.7 2.5 %shard_map.91.grad = f32[9,128,256]{2,1,0:T(8,128)S(1)} custom-call(bf16[2,16,32,256]{3,2,1,0:T(8,128)(2,1)S(1)} %pad_maximum_fusion.own, bf16[16,32,256]{2,1,0:T(8,128)(2,1)S(1)} %collective-permute-done.other.fx, bf16[32,2,256]{2,1,0:T(2,128)(2,1)S(1)} %collective-permute-done.1.near, bf16[32,2,256]{2,1,0:T(2,128)(2,1)S(1)} %collective-permute-done.4.far, ...), custom_call_target="tpu_custom_call" | custom-call | flops 1811939328 | bytes 7340032 | tf_op jit(solution)/shard_map/pallas_call | solution.py:61
  22.1 0.0 copy-start
  22.1 0.0 copy-start.2
  22.1 0.0 collective-permute-done.5.rows
  22.1 0.0 collective-permute-done.8.after.rows
  22.2 1.4 %shard_map.92 = (bf16[64,9,4,128]{3,2,1,0:T(4,128)(2,1)}, f32[8,128]{1,0:T(8,128)S(1)}) custom-call(bf16[2,16,32,256]{3,2,1,0:T(8,128)(2,1)S(1)} %pad_maximum_fusion.own, bf16[16,32,256]{2,1,0:T(8,128)(2,1)S(1)} %collective-permute-done.other.fx, bf16[16,32,256]{2,1,0:T(8,128)(2,1)S(1)} %collective-permute-done.3.cx.other, ...), custom_call_target="tpu_custom_call" | custom-call | flops 37748736 | bytes 3145728 | tf_op jit(solution)/shard_map/pallas_call | solution.py:61
  23.5 6.4 %all-to-all-start = ((bf16[64,9,4,128]{3,2,1,0:T(4,128)(2,1)}), bf16[64,9,4,128]{3,2,1,0:T(4,128)(2,1)S(1)}, u32[]{:S(2)}, u32[]{:S(2)}) async-start(bf16[64,9,4,128]{3,2,1,0:T(4,128)(2,1)} %get-tuple-element.34), calls=%async_computation | async-start | bytes 1179648 | tf_op jit(solution)/shard_map/all_to_all | solution.py:512
  30.0 0.0 copy-done
  30.0 0.0 copy-done.2
  30.0 0.0 copy-start.1
  30.0 3.7 %shard_map.93 = (bf16[16,32,256]{2,1,0:T(8,128)(2,1)}, f32[8,128]{1,0:T(8,128)S(1)}) custom-call(bf16[16,32,256]{2,1,0:T(8,128)(2,1)S(1)} %copy-done, bf16[16,32,256]{2,1,0:T(8,128)(2,1)S(1)} %collective-permute-done.other.fx, bf16[32,2,256]{2,1,0:T(2,128)(2,1)S(1)} %collective-permute-done.1.near, bf16[32,2,256]{2,1,0:T(2,128)(2,1)S(1)} %collective-permute-done.4.far, ...), custom_call_target="tpu_custom_call" | custom-call | flops 1207959552 | bytes 8388608 | tf_op jit(solution)/shard_map/pallas_call | solution.py:61
  33.7 7.3 %all-to-all-done.parts = bf16[64,9,4,128]{3,2,1,0:T(4,128)(2,1)S(1)} async-done(((bf16[64,9,4,128]{3,2,1,0:T(4,128)(2,1)}), bf16[64,9,4,128]{3,2,1,0:T(4,128)(2,1)S(1)}, u32[]{:S(2)}, u32[]{:S(2)}) %all-to-all-start) | async-done | bytes 589856 | tf_op jit(solution)/shard_map/all_to_all | solution.py:512
  41.0 1.1 %shard_map.94 = (bf16[64,9,4,128]{3,2,1,0:T(4,128)(2,1)}, f32[8,128]{1,0:T(8,128)S(1)}) custom-call(bf16[64,9,4,128]{3,2,1,0:T(4,128)(2,1)S(1)} %all-to-all-done.parts, f32[8,128]{1,0:T(8,128)S(1)} %get-tuple-element.35.after), custom_call_target="tpu_custom_call" | custom-call | bytes 1048576 | tf_op jit(solution)/shard_map/pallas_call | solution.py:61
  42.1 6.5 %all-to-all-start.1 = ((bf16[64,9,4,128]{3,2,1,0:T(4,128)(2,1)}), bf16[64,9,4,128]{3,2,1,0:T(4,128)(2,1)S(1)}, u32[]{:S(2)}, u32[]{:S(2)}) async-start(bf16[64,9,4,128]{3,2,1,0:T(4,128)(2,1)} %get-tuple-element.36), calls=%async_computation.1 | async-start | bytes 1179648 | tf_op jit(solution)/shard_map/all_to_all | solution.py:538
  48.6 0.0 copy-done.1
  48.6 5.8 %shard_map.95 = (bf16[16,32,256]{2,1,0:T(8,128)(2,1)}, f32[8,128]{1,0:T(8,128)}) custom-call(bf16[16,32,256]{2,1,0:T(8,128)(2,1)S(1)} %copy-done.1, bf16[16,32,256]{2,1,0:T(8,128)(2,1)S(1)} %collective-permute-done.3.cx.other, bf16[32,2,256]{2,1,0:T(2,128)(2,1)S(1)} %collective-permute-done.6.near, bf16[32,2,256]{2,1,0:T(2,128)(2,1)S(1)} %collective-permute-done.7.far, ...), custom_call_target="tpu_custom_call" | custom-call | flops 1971322880 | bytes 8388608 | tf_op jit(solution)/shard_map/pallas_call | solution.py:61
  54.5 5.2 %all-to-all-done.1.mine = bf16[64,9,4,128]{3,2,1,0:T(4,128)(2,1)S(1)} async-done(((bf16[64,9,4,128]{3,2,1,0:T(4,128)(2,1)}), bf16[64,9,4,128]{3,2,1,0:T(4,128)(2,1)S(1)}, u32[]{:S(2)}, u32[]{:S(2)}) %all-to-all-start.1) | async-done | bytes 589856 | tf_op jit(solution)/shard_map/all_to_all | solution.py:538
  59.6 3.5 %collective-permute-start.9 = (bf16[64,9,4,128]{3,2,1,0:T(4,128)(2,1)S(1)}, bf16[64,9,4,128]{3,2,1,0:T(4,128)(2,1)S(1)}, u32[]{:S(2)}, u32[]{:S(2)}) collective-permute-start(bf16[64,9,4,128]{3,2,1,0:T(4,128)(2,1)S(1)} %all-to-all-done.1.mine), channel_id=1, source_target_pairs={{0,32},{1,33},{2,34},{3,35},{4,36},{5,37},{6,38},{7,39},{8,40},{9,... | collective-permute-start | bytes 1769480 | tf_op jit(solution)/shard_map/ppermute | solution.py:39
  63.1 1.1 %shard_map.96.before = f32[9,32,8,256]{3,2,1,0:T(8,128)} custom-call(bf16[64,9,4,128]{3,2,1,0:T(4,128)(2,1)S(1)} %all-to-all-done.1.mine), custom_call_target="tpu_custom_call" | custom-call | bytes 2097152 | tf_op jit(solution)/shard_map/pallas_call | solution.py:61
  64.2 0.5 collective-permute-done.9.theirs
  64.7 1.1 %shard_map.97 = f32[9,32,8,256]{3,2,1,0:T(8,128)} custom-call(bf16[64,9,4,128]{3,2,1,0:T(4,128)(2,1)S(1)} %collective-permute-done.9.theirs, f32[9,32,8,256]{3,2,1,0:T(8,128)} %shard_map.96.before), custom_call_target="tpu_custom_call", output_to_operand_aliasing={{}: (1, {})} | custom-call | bytes 2097152 | tf_op jit(solution)/shard_map/pallas_call | solution.py:61
  (7 shorter events, 0.1 us)
Async XLA Ops:
  0.6 12.1 %copy-start.5 = (s32[16]{0:T(128)S(1)}, s32[16]{0:T(128)}, u32[]{:S(2)}) copy-start(s32[16]{0:T(128)} %param.8) | copy-start | bytes 196
  0.6 12.1 %copy-start.4 = (s32[16]{0:T(128)S(1)}, s32[16]{0:T(128)}, u32[]{:S(2)}) copy-start(s32[16]{0:T(128)} %param.9) | copy-start | bytes 196
  0.7 12.2 %copy-start.3 = (bf16[16,9,25]{2,0,1:T(8,128)(2,1)S(1)}, bf16[16,9,25]{2,0,1:T(8,128)(2,1)}, u32[]{:S(2)}) copy-start(bf16[16,9,25]{2,0,1:T(8,128)(2,1)} %param.7) | copy-start | bytes 21604
  0.7 2.9 %collective-permute-start = (bf16[16,32,256]{2,1,0:T(8,128)(2,1)}, bf16[16,32,256]{2,1,0:T(8,128)(2,1)S(1)}, u32[]{:S(2)}, u32[]{:S(2)}) collective-permute-start(bf16[16,32,256]{2,1,0:T(8,128)(2,1)} %fo.1), channel_id=1, source_target_pairs={{0,32},{1,33},{2,34},{3,35},{4,36},{5,37},{6,38},{7,39},{8,40},{9,... | collective-permute-start | bytes 786440 | tf_op jit(solution)/shard_map/ppermute | solution.py:39
  2.2 10.2 %collective-permute-start.3 = (bf16[16,32,256]{2,1,0:T(8,128)(2,1)}, bf16[16,32,256]{2,1,0:T(8,128)(2,1)S(1)}, u32[]{:S(2)}, u32[]{:S(2)}) collective-permute-start(bf16[16,32,256]{2,1,0:T(8,128)(2,1)} %co.1), channel_id=1, source_target_pairs={{0,32},{1,33},{2,34},{3,35},{4,36},{5,37},{6,38},{7,39},{8,40},{9,... | collective-permute-start | bytes 786440 | tf_op jit(solution)/shard_map/ppermute | solution.py:39
  3.6 13.0 %collective-permute-start.1 = (bf16[32,2,256]{2,1,0:T(2,128)(2,1)S(1)}, bf16[32,2,256]{2,1,0:T(2,128)(2,1)S(1)}, u32[]{:S(2)}, u32[]{:S(2)}) collective-permute-start(bf16[32,2,256]{2,1,0:T(2,128)(2,1)S(1)} %shard_map.85.after), channel_id=1, source_target_pairs={{0,1},{1,2},{2,3},{3,4},{4,5},{5,6},{6,7},{7,8},{8,9},{9,10},{10,1... | collective-permute-start | bytes 98312 | tf_op jit(solution)/shard_map/ppermute | solution.py:39
  12.4 4.7 %collective-permute-start.6 = (bf16[32,2,256]{2,1,0:T(2,128)(2,1)S(1)}, bf16[32,2,256]{2,1,0:T(2,128)(2,1)S(1)}, u32[]{:S(2)}, u32[]{:S(2)}) collective-permute-start(bf16[32,2,256]{2,1,0:T(2,128)(2,1)S(1)} %shard_map.89), channel_id=1, source_target_pairs={{0,1},{1,2},{2,3},{3,4},{4,5},{5,6},{6,7},{7,8},{8,9},{9,10},{10,1... | collective-permute-start | bytes 98312 | tf_op jit(solution)/shard_map/ppermute | solution.py:39
  12.9 1.9 %collective-permute-start.2 = (bf16[9,16,25]{2,1,0:T(8,128)(2,1)S(1)}, bf16[9,16,25]{2,1,0:T(8,128)(2,1)S(1)}, u32[]{:S(2)}, u32[]{:S(2)}) collective-permute-start(bf16[9,16,25]{2,1,0:T(8,128)(2,1)S(1)} %select_bitcast_fusion.mo), channel_id=1, source_target_pairs={{0,32},{1,33},{2,34},{3,35},{4,36},{5,37},{6,38},{7,39},{8,40},{9,... | collective-permute-start | bytes 21608 | tf_op jit(solution)/shard_map/ppermute | solution.py:39
  16.6 1.4 %collective-permute-start.4 = (bf16[32,2,256]{2,1,0:T(2,128)(2,1)S(1)}, bf16[32,2,256]{2,1,0:T(2,128)(2,1)S(1)}, u32[]{:S(2)}, u32[]{:S(2)}) collective-permute-start(bf16[32,2,256]{2,1,0:T(2,128)(2,1)S(1)} %collective-permute-done.1.near), channel_id=1, source_target_pairs={{0,32},{1,33},{2,34},{3,35},{4,36},{5,37},{6,38},{7,39},{8,40},{9,... | collective-permute-start | bytes 98312 | tf_op jit(solution)/shard_map/ppermute | solution.py:39
  17.1 1.3 %collective-permute-start.7 = (bf16[32,2,256]{2,1,0:T(2,128)(2,1)S(1)}, bf16[32,2,256]{2,1,0:T(2,128)(2,1)S(1)}, u32[]{:S(2)}, u32[]{:S(2)}) collective-permute-start(bf16[32,2,256]{2,1,0:T(2,128)(2,1)S(1)} %collective-permute-done.6.near), channel_id=1, source_target_pairs={{0,32},{1,33},{2,34},{3,35},{4,36},{5,37},{6,38},{7,39},{8,40},{9,... | collective-permute-start | bytes 98312 | tf_op jit(solution)/shard_map/ppermute | solution.py:39
  18.0 4.1 %collective-permute-start.5 = (bf16[2,40,256]{2,1,0:T(8,128)(2,1)S(1)}, bf16[2,40,256]{2,1,0:T(8,128)(2,1)S(1)}, u32[]{:S(2)}, u32[]{:S(2)}) collective-permute-start(bf16[2,40,256]{2,1,0:T(8,128)(2,1)S(1)} %shard_map.88), channel_id=1, source_target_pairs={{0,64},{1,65},{2,66},{3,67},{4,68},{5,69},{6,70},{7,71},{8,72},{9,... | collective-permute-start | bytes 122888 | tf_op jit(solution)/shard_map/ppermute | solution.py:39
  18.4 3.7 %collective-permute-start.8 = (bf16[2,40,256]{2,1,0:T(8,128)(2,1)S(1)}, bf16[2,40,256]{2,1,0:T(8,128)(2,1)S(1)}, u32[]{:S(2)}, u32[]{:S(2)}) collective-permute-start(bf16[2,40,256]{2,1,0:T(8,128)(2,1)S(1)} %shard_map.90), channel_id=1, source_target_pairs={{0,64},{1,65},{2,66},{3,67},{4,68},{5,69},{6,70},{7,71},{8,72},{9,... | collective-permute-start | bytes 122888 | tf_op jit(solution)/shard_map/ppermute | solution.py:39
  22.1 7.8 %copy-start = (bf16[16,32,256]{2,1,0:T(8,128)(2,1)S(1)}, bf16[16,32,256]{2,1,0:T(8,128)(2,1)}, u32[]{:S(2)}) copy-start(bf16[16,32,256]{2,1,0:T(8,128)(2,1)} %fo.1) | copy-start | bytes 786436
  22.1 7.8 %copy-start.2 = (bf16[9,256,256]{2,1,0:T(8,128)(2,1)S(1)}, bf16[9,256,256]{2,1,0:T(8,128)(2,1)}, u32[]{:S(2)}) copy-start(bf16[9,256,256]{2,1,0:T(8,128)(2,1)} %param.10) | copy-start | bytes 3538948
  23.5 17.4 %all-to-all-start = ((bf16[64,9,4,128]{3,2,1,0:T(4,128)(2,1)}), bf16[64,9,4,128]{3,2,1,0:T(4,128)(2,1)S(1)}, u32[]{:S(2)}, u32[]{:S(2)}) async-start(bf16[64,9,4,128]{3,2,1,0:T(4,128)(2,1)} %get-tuple-element.34), calls=%async_computation | async-start | bytes 1179648 | tf_op jit(solution)/shard_map/all_to_all | solution.py:512
  30.0 18.6 %copy-start.1 = (bf16[16,32,256]{2,1,0:T(8,128)(2,1)S(1)}, bf16[16,32,256]{2,1,0:T(8,128)(2,1)}, u32[]{:S(2)}) copy-start(bf16[16,32,256]{2,1,0:T(8,128)(2,1)} %co.1) | copy-start | bytes 786436
  42.1 17.5 %all-to-all-start.1 = ((bf16[64,9,4,128]{3,2,1,0:T(4,128)(2,1)}), bf16[64,9,4,128]{3,2,1,0:T(4,128)(2,1)S(1)}, u32[]{:S(2)}, u32[]{:S(2)}) async-start(bf16[64,9,4,128]{3,2,1,0:T(4,128)(2,1)} %get-tuple-element.36), calls=%async_computation.1 | async-start | bytes 1179648 | tf_op jit(solution)/shard_map/all_to_all | solution.py:538
  59.6 5.1 %collective-permute-start.9 = (bf16[64,9,4,128]{3,2,1,0:T(4,128)(2,1)S(1)}, bf16[64,9,4,128]{3,2,1,0:T(4,128)(2,1)S(1)}, u32[]{:S(2)}, u32[]{:S(2)}) collective-permute-start(bf16[64,9,4,128]{3,2,1,0:T(4,128)(2,1)S(1)} %all-to-all-done.1.mine), channel_id=1, source_target_pairs={{0,32},{1,33},{2,34},{3,35},{4,36},{5,37},{6,38},{7,39},{8,40},{9,... | collective-permute-start | bytes 1769480 | tf_op jit(solution)/shard_map/ppermute | solution.py:39

commit v8 on v7

--- a/solution.py
+++ b/solution.py
@@ -261,7 +261,7 @@
 
 
 def weight_end_kernel(
-    own, fx, cx, near, far, rows, after, bo, bx, grad, out, token,
+    own, fx, cx, near, far, rows, bo, bx, grad, out, token,
     field, cot, tile, parts, sems
 ):
     mark(token)
@@ -495,7 +495,7 @@
     parts, after = call(
         weight_end_kernel,
         [((64, *CHUNK), bf16), TOKEN],
-        (own, fx, cx, *sides[0], rows_f, rows_c, bo, bx, grad),
+        (own, fx, cx, *sides[0], rows_f, bo, bx, grad),
         scratch=[
             pltpu.VMEM((6, SLOTS, HALF), bf16),
             pltpu.VMEM((2 * CELLS, CHAN), bf16),
@@ -509,6 +509,7 @@
     )
     mixing = weight.reshape(BASIS * CHAN, CHAN)
 
+    parts, rows_c = lax.optimization_barrier((parts, rows_c))
     swapped = lax.all_to_all(parts, RING, 0, 0, tiled=True)
     mixed, after = call(
         mixed_kernel,

time: 66.3 us -> 66.4 us (level)
  transfers between devices with their start and end apart: 12 -> 12, of which waited for: 5 -> 5; matrix products, arithmetic and copies ran while one was open for 2% -> 2% of each run, Pallas kernels for 25% -> 27%
where the time goes in v8:
time: 66.4 us; the launch traced here: 66.1 us
  starting transfers between devices  29 us (44%)
  Pallas kernels  20.3 us (31%)
  waiting for transfers between devices  14.5 us (22%)
  other arithmetic  1.18 us (2%)
  between operations  1.02 us (2%)
    pallas_call x13, Pallas kernels, call(): pl.pallas_call(kernel, out_shape=[jax.ShapeDtypeStruct(*o) for o in outs]...  20.3 us
    ppermute x10, starting transfers between devices, send(): return lax.ppermute(x, AXES, moves(**way))  16.7 us
    all_to_all x1, waiting for transfers between devices, shards(): swapped = lax.all_to_all(parts, RING, 0, 0, tiled=True)  7.93 us
    all_to_all x1, starting transfers between devices, shards(): swapped = lax.all_to_all(parts, RING, 0, 0, tiled=True)  6.42 us
    all_to_all x1, starting transfers between devices, shards(): mine = lax.all_to_all(shared, RING, 0, 0, tiled=True)  5.95 us
    all_to_all x1, waiting for transfers between devices, shards(): mine = lax.all_to_all(shared, RING, 0, 0, tiled=True)  5.12 us
    ppermute x10, waiting for transfers between devices, send(): return lax.ppermute(x, AXES, moves(**way))  1.48 us
  transfers between devices with their start and end apart: 12, of which 5 were waited for; matrix products, arithmetic and copies ran while one was open for 2% of the time, Pallas kernels for 27%

profile of v8, /device:TPU:1, one launch (start us, length us, event | category | flops | bytes accessed | tf_op | source)
XLA Modules:
  0.0 66.1 jit_solution(17602835882771100829)
XLA Ops:
  0.6 0.0 copy-start.5
  0.6 0.0 copy-start.4
  0.7 0.0 copy-start.3
  0.7 1.5 %collective-permute-start = (bf16[16,32,256]{2,1,0:T(8,128)(2,1)}, bf16[16,32,256]{2,1,0:T(8,128)(2,1)S(1)}, u32[]{:S(2)}, u32[]{:S(2)}) collective-permute-start(bf16[16,32,256]{2,1,0:T(8,128)(2,1)} %fo.1), channel_id=1, source_target_pairs={{0,32},{1,33},{2,34},{3,35},{4,36},{5,37},{6,38},{7,39},{8,40},{9,... | collective-permute-start | bytes 786440 | tf_op jit(solution)/shard_map/ppermute | solution.py:39
  2.2 0.1 collective-permute-start.3
  2.3 1.1 %pad_maximum_fusion.own = bf16[2,16,32,256]{3,2,1,0:T(8,128)(2,1)S(1)} fusion(bf16[1,16,32,256]{3,2,1,0:T(8,128)(2,1)} %bitcast.7, bf16[1,16,32,256]{3,2,1,0:T(8,128)(2,1)} %bitcast.6), kind=kLoop, calls=%fused_computation | loop fusion | flops 262144 | bytes 1048576 | tf_op jit(solution)/shard_map/stack | solution.py:427
  3.4 0.2 collective-permute-done.other.fx
  3.6 8.8 %collective-permute-start.1 = (bf16[32,2,256]{2,1,0:T(2,128)(2,1)S(1)}, bf16[32,2,256]{2,1,0:T(2,128)(2,1)S(1)}, u32[]{:S(2)}, u32[]{:S(2)}) collective-permute-start(bf16[32,2,256]{2,1,0:T(2,128)(2,1)S(1)} %shard_map.85.after), channel_id=1, source_target_pairs={{0,1},{1,2},{2,3},{3,4},{4,5},{5,6},{6,7},{7,8},{8,9},{9,10},{10,1... | collective-permute-start | bytes 98312 | tf_op jit(solution)/shard_map/ppermute | solution.py:39
  12.4 0.0 collective-permute-done.3.cx.other
  12.4 0.3 collective-permute-start.6
  12.8 0.0 copy-done.5
  12.8 0.0 copy-done.4
  12.8 0.1 fusion.2
  12.8 0.0 copy-done.3
  12.9 0.1 collective-permute-start.2
  13.0 1.8 %shard_map.86 = (bf16[16,288,256]{2,1,0:T(8,128)(2,1)S(1)}, bf16[256,512]{1,0:T(8,128)(2,1)S(1)}, bf16[16,256]{1,0:T(8,128)(2,1)S(1)}) custom-call(bf16[9,16,25]{2,1,0:T(8,128)(2,1)S(1)} %select_bitcast_fusion.mo, bf16[2,16,32,256]{3,2,1,0:T(8,128)(2,1)S(1)} %pad_maximum_fusion.own, bf16[32,2,256]{2,1,0:T(2,128)(2,1)S(1)} %shard_map.85.after), custom_call_target="tpu_custom_call" | custom-call | flops 94371840 | bytes 4194304 | tf_op jit(solution)/shard_map/pallas_call | solution.py:61
  14.8 0.0 collective-permute-done.2.mx
  14.8 1.8 %shard_map.87 = (bf16[16,288,256]{2,1,0:T(8,128)(2,1)S(1)}, bf16[256,512]{1,0:T(8,128)(2,1)S(1)}, bf16[16,256]{1,0:T(8,128)(2,1)S(1)}) custom-call(bf16[9,16,25]{2,1,0:T(8,128)(2,1)S(1)} %collective-permute-done.2.mx, bf16[16,32,256]{2,1,0:T(8,128)(2,1)S(1)} %collective-permute-done.3.cx.other, bf16[16,256]{1,0:T(8,128)(2,1)S(1)} %get-tuple-element.26.after.to), custom_call_target="tpu_custom_call" | custom-call | flops 94371840 | bytes 4194304 | tf_op jit(solution)/shard_map/pallas_call | solution.py:61
  16.6 0.0 collective-permute-done.1.near
  16.6 0.6 collective-permute-start.4
  17.1 0.0 collective-permute-done.6.near
  17.1 0.1 collective-permute-start.7
  17.2 0.8 %collective-permute-done.4.far = bf16[32,2,256]{2,1,0:T(2,128)(2,1)S(1)} collective-permute-done((bf16[32,2,256]{2,1,0:T(2,128)(2,1)S(1)}, bf16[32,2,256]{2,1,0:T(2,128)(2,1)S(1)}, u32[]{:S(2)}, u32[]{:S(2)}) %collective-permute-start.4) | collective-permute-done | bytes 32800 | tf_op jit(solution)/shard_map/ppermute | solution.py:39
  18.0 0.4 collective-permute-start.5
  18.4 0.0 collective-permute-done.7.far
  18.4 1.2 %collective-permute-start.8 = (bf16[2,40,256]{2,1,0:T(8,128)(2,1)S(1)}, bf16[2,40,256]{2,1,0:T(8,128)(2,1)S(1)}, u32[]{:S(2)}, u32[]{:S(2)}) collective-permute-start(bf16[2,40,256]{2,1,0:T(8,128)(2,1)S(1)} %shard_map.93), channel_id=1, source_target_pairs={{0,64},{1,65},{2,66},{3,67},{4,68},{5,69},{6,70},{7,71},{8,72},{9,... | collective-permute-start | bytes 122888 | tf_op jit(solution)/shard_map/ppermute | solution.py:39
  19.7 2.4 %shard_map.89.grad = f32[9,128,256]{2,1,0:T(8,128)S(1)} custom-call(bf16[2,16,32,256]{3,2,1,0:T(8,128)(2,1)S(1)} %pad_maximum_fusion.own, bf16[16,32,256]{2,1,0:T(8,128)(2,1)S(1)} %collective-permute-done.other.fx, bf16[32,2,256]{2,1,0:T(2,128)(2,1)S(1)} %collective-permute-done.1.near, bf16[32,2,256]{2,1,0:T(2,128)(2,1)S(1)} %collective-permute-done.4.far, ...), custom_call_target="tpu_custom_call" | custom-call | flops 1811939328 | bytes 7340032 | tf_op jit(solution)/shard_map/pallas_call | solution.py:61
  22.1 0.0 copy-start
  22.1 0.0 copy-start.2
  22.1 0.0 collective-permute-done.5.rows
  22.1 1.4 %shard_map.90 = (bf16[64,9,4,128]{3,2,1,0:T(4,128)(2,1)}, f32[8,128]{1,0:T(8,128)S(1)}) custom-call(bf16[2,16,32,256]{3,2,1,0:T(8,128)(2,1)S(1)} %pad_maximum_fusion.own, bf16[16,32,256]{2,1,0:T(8,128)(2,1)S(1)} %collective-permute-done.other.fx, bf16[16,32,256]{2,1,0:T(8,128)(2,1)S(1)} %collective-permute-done.3.cx.other, ...), custom_call_target="tpu_custom_call" | custom-call | flops 37748736 | bytes 3145728 | tf_op jit(solution)/shard_map/pallas_call | solution.py:61
  23.5 0.0 collective-permute-done.8.rows
  23.5 6.4 %all-to-all-start = ((bf16[64,9,4,128]{3,2,1,0:T(4,128)(2,1)}), bf16[64,9,4,128]{3,2,1,0:T(4,128)(2,1)S(1)}, u32[]{:S(2)}, u32[]{:S(2)}) async-start(bf16[64,9,4,128]{3,2,1,0:T(4,128)(2,1)} %get-tuple-element.37), calls=%async_computation | async-start | bytes 1179648 | tf_op jit(solution)/shard_map/all_to_all | solution.py:513
  30.0 0.0 copy-done
  30.0 0.0 copy-done.2
  30.0 0.0 copy-start.1
  30.0 3.7 %shard_map.91 = (bf16[16,32,256]{2,1,0:T(8,128)(2,1)}, f32[8,128]{1,0:T(8,128)S(1)}) custom-call(bf16[16,32,256]{2,1,0:T(8,128)(2,1)S(1)} %copy-done, bf16[16,32,256]{2,1,0:T(8,128)(2,1)S(1)} %collective-permute-done.other.fx, bf16[32,2,256]{2,1,0:T(2,128)(2,1)S(1)} %collective-permute-done.1.near, bf16[32,2,256]{2,1,0:T(2,128)(2,1)S(1)} %collective-permute-done.4.far, ...), custom_call_target="tpu_custom_call" | custom-call | flops 1207959552 | bytes 8388608 | tf_op jit(solution)/shard_map/pallas_call | solution.py:61
  33.7 7.9 %all-to-all-done.parts = bf16[64,9,4,128]{3,2,1,0:T(4,128)(2,1)S(1)} async-done(((bf16[64,9,4,128]{3,2,1,0:T(4,128)(2,1)}), bf16[64,9,4,128]{3,2,1,0:T(4,128)(2,1)S(1)}, u32[]{:S(2)}, u32[]{:S(2)}) %all-to-all-start) | async-done | bytes 589856 | tf_op jit(solution)/shard_map/all_to_all | solution.py:513
  41.6 1.1 %shard_map.94 = (bf16[64,9,4,128]{3,2,1,0:T(4,128)(2,1)}, f32[8,128]{1,0:T(8,128)S(1)}) custom-call(bf16[64,9,4,128]{3,2,1,0:T(4,128)(2,1)S(1)} %all-to-all-done.parts, f32[8,128]{1,0:T(8,128)S(1)} %get-tuple-element.38.after), custom_call_target="tpu_custom_call" | custom-call | bytes 1048576 | tf_op jit(solution)/shard_map/pallas_call | solution.py:61
  42.7 6.0 %all-to-all-start.1 = ((bf16[64,9,4,128]{3,2,1,0:T(4,128)(2,1)}), bf16[64,9,4,128]{3,2,1,0:T(4,128)(2,1)S(1)}, u32[]{:S(2)}, u32[]{:S(2)}) async-start(bf16[64,9,4,128]{3,2,1,0:T(4,128)(2,1)} %get-tuple-element.39), calls=%async_computation.1 | async-start | bytes 1179648 | tf_op jit(solution)/shard_map/all_to_all | solution.py:539
  48.7 0.0 copy-done.1
  48.7 5.8 %shard_map.95 = (bf16[16,32,256]{2,1,0:T(8,128)(2,1)}, f32[8,128]{1,0:T(8,128)}) custom-call(bf16[16,32,256]{2,1,0:T(8,128)(2,1)S(1)} %copy-done.1, bf16[16,32,256]{2,1,0:T(8,128)(2,1)S(1)} %collective-permute-done.3.cx.other, bf16[32,2,256]{2,1,0:T(2,128)(2,1)S(1)} %collective-permute-done.6.near, bf16[32,2,256]{2,1,0:T(2,128)(2,1)S(1)} %collective-permute-done.7.far, ...), custom_call_target="tpu_custom_call" | custom-call | flops 1971322880 | bytes 8388608 | tf_op jit(solution)/shard_map/pallas_call | solution.py:61
  54.6 5.1 %all-to-all-done.1.mine = bf16[64,9,4,128]{3,2,1,0:T(4,128)(2,1)S(1)} async-done(((bf16[64,9,4,128]{3,2,1,0:T(4,128)(2,1)}), bf16[64,9,4,128]{3,2,1,0:T(4,128)(2,1)S(1)}, u32[]{:S(2)}, u32[]{:S(2)}) %all-to-all-start.1) | async-done | bytes 589856 | tf_op jit(solution)/shard_map/all_to_all | solution.py:539
  59.7 3.5 %collective-permute-start.9 = (bf16[64,9,4,128]{3,2,1,0:T(4,128)(2,1)S(1)}, bf16[64,9,4,128]{3,2,1,0:T(4,128)(2,1)S(1)}, u32[]{:S(2)}, u32[]{:S(2)}) collective-permute-start(bf16[64,9,4,128]{3,2,1,0:T(4,128)(2,1)S(1)} %all-to-all-done.1.mine), channel_id=1, source_target_pairs={{0,32},{1,33},{2,34},{3,35},{4,36},{5,37},{6,38},{7,39},{8,40},{9,... | collective-permute-start | bytes 1769480 | tf_op jit(solution)/shard_map/ppermute | solution.py:39
  63.2 1.1 %shard_map.96.before = f32[9,32,8,256]{3,2,1,0:T(8,128)} custom-call(bf16[64,9,4,128]{3,2,1,0:T(4,128)(2,1)S(1)} %all-to-all-done.1.mine), custom_call_target="tpu_custom_call" | custom-call | bytes 2097152 | tf_op jit(solution)/shard_map/pallas_call | solution.py:61
  64.3 0.5 collective-permute-done.9.theirs
  64.9 1.1 %shard_map.97 = f32[9,32,8,256]{3,2,1,0:T(8,128)} custom-call(bf16[64,9,4,128]{3,2,1,0:T(4,128)(2,1)S(1)} %collective-permute-done.9.theirs, f32[9,32,8,256]{3,2,1,0:T(8,128)} %shard_map.96.before), custom_call_target="tpu_custom_call", output_to_operand_aliasing={{}: (1, {})} | custom-call | bytes 2097152 | tf_op jit(solution)/shard_map/pallas_call | solution.py:61
  (7 shorter events, 0.1 us)
Async XLA Ops:
  0.6 12.1 %copy-start.5 = (s32[16]{0:T(128)S(1)}, s32[16]{0:T(128)}, u32[]{:S(2)}) copy-start(s32[16]{0:T(128)} %param.8) | copy-start | bytes 196
  0.6 12.1 %copy-start.4 = (s32[16]{0:T(128)S(1)}, s32[16]{0:T(128)}, u32[]{:S(2)}) copy-start(s32[16]{0:T(128)} %param.9) | copy-start | bytes 196
  0.7 12.2 %copy-start.3 = (bf16[16,9,25]{2,0,1:T(8,128)(2,1)S(1)}, bf16[16,9,25]{2,0,1:T(8,128)(2,1)}, u32[]{:S(2)}) copy-start(bf16[16,9,25]{2,0,1:T(8,128)(2,1)} %param.7) | copy-start | bytes 21604
  0.7 2.9 %collective-permute-start = (bf16[16,32,256]{2,1,0:T(8,128)(2,1)}, bf16[16,32,256]{2,1,0:T(8,128)(2,1)S(1)}, u32[]{:S(2)}, u32[]{:S(2)}) collective-permute-start(bf16[16,32,256]{2,1,0:T(8,128)(2,1)} %fo.1), channel_id=1, source_target_pairs={{0,32},{1,33},{2,34},{3,35},{4,36},{5,37},{6,38},{7,39},{8,40},{9,... | collective-permute-start | bytes 786440 | tf_op jit(solution)/shard_map/ppermute | solution.py:39
  2.2 10.2 %collective-permute-start.3 = (bf16[16,32,256]{2,1,0:T(8,128)(2,1)}, bf16[16,32,256]{2,1,0:T(8,128)(2,1)S(1)}, u32[]{:S(2)}, u32[]{:S(2)}) collective-permute-start(bf16[16,32,256]{2,1,0:T(8,128)(2,1)} %co.1), channel_id=1, source_target_pairs={{0,32},{1,33},{2,34},{3,35},{4,36},{5,37},{6,38},{7,39},{8,40},{9,... | collective-permute-start | bytes 786440 | tf_op jit(solution)/shard_map/ppermute | solution.py:39
  3.6 13.0 %collective-permute-start.1 = (bf16[32,2,256]{2,1,0:T(2,128)(2,1)S(1)}, bf16[32,2,256]{2,1,0:T(2,128)(2,1)S(1)}, u32[]{:S(2)}, u32[]{:S(2)}) collective-permute-start(bf16[32,2,256]{2,1,0:T(2,128)(2,1)S(1)} %shard_map.85.after), channel_id=1, source_target_pairs={{0,1},{1,2},{2,3},{3,4},{4,5},{5,6},{6,7},{7,8},{8,9},{9,10},{10,1... | collective-permute-start | bytes 98312 | tf_op jit(solution)/shard_map/ppermute | solution.py:39
  12.4 4.7 %collective-permute-start.6 = (bf16[32,2,256]{2,1,0:T(2,128)(2,1)S(1)}, bf16[32,2,256]{2,1,0:T(2,128)(2,1)S(1)}, u32[]{:S(2)}, u32[]{:S(2)}) collective-permute-start(bf16[32,2,256]{2,1,0:T(2,128)(2,1)S(1)} %shard_map.92), channel_id=1, source_target_pairs={{0,1},{1,2},{2,3},{3,4},{4,5},{5,6},{6,7},{7,8},{8,9},{9,10},{10,1... | collective-permute-start | bytes 98312 | tf_op jit(solution)/shard_map/ppermute | solution.py:39
  12.9 1.9 %collective-permute-start.2 = (bf16[9,16,25]{2,1,0:T(8,128)(2,1)S(1)}, bf16[9,16,25]{2,1,0:T(8,128)(2,1)S(1)}, u32[]{:S(2)}, u32[]{:S(2)}) collective-permute-start(bf16[9,16,25]{2,1,0:T(8,128)(2,1)S(1)} %select_bitcast_fusion.mo), channel_id=1, source_target_pairs={{0,32},{1,33},{2,34},{3,35},{4,36},{5,37},{6,38},{7,39},{8,40},{9,... | collective-permute-start | bytes 21608 | tf_op jit(solution)/shard_map/ppermute | solution.py:39
  16.6 1.4 %collective-permute-start.4 = (bf16[32,2,256]{2,1,0:T(2,128)(2,1)S(1)}, bf16[32,2,256]{2,1,0:T(2,128)(2,1)S(1)}, u32[]{:S(2)}, u32[]{:S(2)}) collective-permute-start(bf16[32,2,256]{2,1,0:T(2,128)(2,1)S(1)} %collective-permute-done.1.near), channel_id=1, source_target_pairs={{0,32},{1,33},{2,34},{3,35},{4,36},{5,37},{6,38},{7,39},{8,40},{9,... | collective-permute-start | bytes 98312 | tf_op jit(solution)/shard_map/ppermute | solution.py:39
  17.1 1.3 %collective-permute-start.7 = (bf16[32,2,256]{2,1,0:T(2,128)(2,1)S(1)}, bf16[32,2,256]{2,1,0:T(2,128)(2,1)S(1)}, u32[]{:S(2)}, u32[]{:S(2)}) collective-permute-start(bf16[32,2,256]{2,1,0:T(2,128)(2,1)S(1)} %collective-permute-done.6.near), channel_id=1, source_target_pairs={{0,32},{1,33},{2,34},{3,35},{4,36},{5,37},{6,38},{7,39},{8,40},{9,... | collective-permute-start | bytes 98312 | tf_op jit(solution)/shard_map/ppermute | solution.py:39
  18.0 4.1 %collective-permute-start.5 = (bf16[2,40,256]{2,1,0:T(8,128)(2,1)S(1)}, bf16[2,40,256]{2,1,0:T(8,128)(2,1)S(1)}, u32[]{:S(2)}, u32[]{:S(2)}) collective-permute-start(bf16[2,40,256]{2,1,0:T(8,128)(2,1)S(1)} %shard_map.88), channel_id=1, source_target_pairs={{0,64},{1,65},{2,66},{3,67},{4,68},{5,69},{6,70},{7,71},{8,72},{9,... | collective-permute-start | bytes 122888 | tf_op jit(solution)/shard_map/ppermute | solution.py:39
  18.4 5.1 %collective-permute-start.8 = (bf16[2,40,256]{2,1,0:T(8,128)(2,1)S(1)}, bf16[2,40,256]{2,1,0:T(8,128)(2,1)S(1)}, u32[]{:S(2)}, u32[]{:S(2)}) collective-permute-start(bf16[2,40,256]{2,1,0:T(8,128)(2,1)S(1)} %shard_map.93), channel_id=1, source_target_pairs={{0,64},{1,65},{2,66},{3,67},{4,68},{5,69},{6,70},{7,71},{8,72},{9,... | collective-permute-start | bytes 122888 | tf_op jit(solution)/shard_map/ppermute | solution.py:39
  22.1 7.9 %copy-start = (bf16[16,32,256]{2,1,0:T(8,128)(2,1)S(1)}, bf16[16,32,256]{2,1,0:T(8,128)(2,1)}, u32[]{:S(2)}) copy-start(bf16[16,32,256]{2,1,0:T(8,128)(2,1)} %fo.1) | copy-start | bytes 786436
  22.1 7.9 %copy-start.2 = (bf16[9,256,256]{2,1,0:T(8,128)(2,1)S(1)}, bf16[9,256,256]{2,1,0:T(8,128)(2,1)}, u32[]{:S(2)}) copy-start(bf16[9,256,256]{2,1,0:T(8,128)(2,1)} %param.10) | copy-start | bytes 3538948
  23.5 18.1 %all-to-all-start = ((bf16[64,9,4,128]{3,2,1,0:T(4,128)(2,1)}), bf16[64,9,4,128]{3,2,1,0:T(4,128)(2,1)S(1)}, u32[]{:S(2)}, u32[]{:S(2)}) async-start(bf16[64,9,4,128]{3,2,1,0:T(4,128)(2,1)} %get-tuple-element.37), calls=%async_computation | async-start | bytes 1179648 | tf_op jit(solution)/shard_map/all_to_all | solution.py:513
  30.0 18.7 %copy-start.1 = (bf16[16,32,256]{2,1,0:T(8,128)(2,1)S(1)}, bf16[16,32,256]{2,1,0:T(8,128)(2,1)}, u32[]{:S(2)}) copy-start(bf16[16,32,256]{2,1,0:T(8,128)(2,1)} %co.1) | copy-start | bytes 786436
  42.7 16.9 %all-to-all-start.1 = ((bf16[64,9,4,128]{3,2,1,0:T(4,128)(2,1)}), bf16[64,9,4,128]{3,2,1,0:T(4,128)(2,1)S(1)}, u32[]{:S(2)}, u32[]{:S(2)}) async-start(bf16[64,9,4,128]{3,2,1,0:T(4,128)(2,1)} %get-tuple-element.39), calls=%async_computation.1 | async-start | bytes 1179648 | tf_op jit(solution)/shard_map/all_to_all | solution.py:539
  59.7 5.2 %collective-permute-start.9 = (bf16[64,9,4,128]{3,2,1,0:T(4,128)(2,1)S(1)}, bf16[64,9,4,128]{3,2,1,0:T(4,128)(2,1)S(1)}, u32[]{:S(2)}, u32[]{:S(2)}) collective-permute-start(bf16[64,9,4,128]{3,2,1,0:T(4,128)(2,1)S(1)} %all-to-all-done.1.mine), channel_id=1, source_target_pairs={{0,32},{1,33},{2,34},{3,35},{4,36},{5,37},{6,38},{7,39},{8,40},{9,... | collective-permute-start | bytes 1769480 | tf_op jit(solution)/shard_map/ppermute | solution.py:39

commit v9 on v8

--- a/solution.py
+++ b/solution.py
@@ -511,32 +511,6 @@
 
     parts, rows_c = lax.optimization_barrier((parts, rows_c))
     swapped = lax.all_to_all(parts, RING, 0, 0, tiled=True)
-    mixed, after = call(
-        mixed_kernel,
-        [block, TOKEN],
-        (feature, fx, *sides[0], rows_f, mo, mixing, after),
-        scratch=[
-            pltpu.VMEM((36, SLOTS, CHAN), bf16),
-            pltpu.VMEM((512, BASIS * CHAN), bf16),
-            pltpu.VMEM((BASIS * CHAN, CHAN), bf16),
-            pltpu.VMEM((ROWS, BASIS * CELLS, CHAN), bf16),
-            lines,
-            pltpu.SemaphoreType.DMA,
-        ],
-        hbm=(6,),
-        flops=2 * 16 * 288 * 256 * 256 + 2 * 512 * 2304 * 256,
-        traffic=8 * 2**20,
-    )
-    shared, after = call(
-        functools.partial(sum_kernel, 1.0 / math.sqrt(64 * 1024)),
-        [((64, *CHUNK), bf16), TOKEN],
-        (swapped, after),
-        scratch=[pltpu.VMEM((8, *CHUNK), bf16), pltpu.SemaphoreType.DMA((8,))],
-        to=(0,),
-        traffic=2**20,
-    )
-
-    mine = lax.all_to_all(shared, RING, 0, 0, tiled=True)
     grad_feature, after = call(
         feature_kernel,
         [block, TOKEN],
@@ -554,7 +528,33 @@
         flops=2 * 960 * 2304 * 256 + 2 * 20 * 160 * 512 * 256,
         traffic=8 * 2**20,
     )
-    mine, grad_feature = lax.optimization_barrier((mine, grad_feature))
+    shared, after = call(
+        functools.partial(sum_kernel, 1.0 / math.sqrt(64 * 1024)),
+        [((64, *CHUNK), bf16), TOKEN],
+        (swapped, after),
+        scratch=[pltpu.VMEM((8, *CHUNK), bf16), pltpu.SemaphoreType.DMA((8,))],
+        to=(0,),
+        traffic=2**20,
+    )
+
+    mine = lax.all_to_all(shared, RING, 0, 0, tiled=True)
+    mixed, after = call(
+        mixed_kernel,
+        [block, TOKEN],
+        (feature, fx, *sides[0], rows_f, mo, mixing, after),
+        scratch=[
+            pltpu.VMEM((36, SLOTS, CHAN), bf16),
+            pltpu.VMEM((512, BASIS * CHAN), bf16),
+            pltpu.VMEM((BASIS * CHAN, CHAN), bf16),
+            pltpu.VMEM((ROWS, BASIS * CELLS, CHAN), bf16),
+            lines,
+            pltpu.SemaphoreType.DMA,
+        ],
+        hbm=(6,),
+        flops=2 * 16 * 288 * 256 * 256 + 2 * 512 * 2304 * 256,
+        traffic=8 * 2**20,
+    )
+    mine, mixed = lax.optimization_barrier((mine, mixed))
     theirs = send(mine, core=True)
     whole = ((BASIS, 32, 8, CHAN), f32)
     stage = [pltpu.VMEM((BASIS, 16, 8, CHAN), f32), pltpu.SemaphoreType.DMA((BASIS,))]

time: 66.4 us -> 66.4 us (level)
    all_to_all x1, waiting for transfers between devices: 7.93 us -> 5.73 us  [shards(): swapped = lax.all_to_all(parts, RING, 0, 0, tiled=True)]
    all_to_all x1, waiting for transfers between devices: 5.12 us -> 7.3 us  [shards(): mine = lax.all_to_all(shared, RING, 0, 0, tiled=True)]
where the time goes in v9:
time: 66.4 us; the launch traced here: 66.1 us
  starting transfers between devices  29 us (44%)
  Pallas kernels  20.4 us (31%)
  waiting for transfers between devices  14.5 us (22%)
  other arithmetic  1.18 us (2%)
  between operations  1.02 us (2%)
    pallas_call x13, Pallas kernels, call(): pl.pallas_call(kernel, out_shape=[jax.ShapeDtypeStruct(*o) for o in outs]...  20.4 us
    ppermute x10, starting transfers between devices, send(): return lax.ppermute(x, AXES, moves(**way))  16.7 us
    all_to_all x1, waiting for transfers between devices, shards(): mine = lax.all_to_all(shared, RING, 0, 0, tiled=True)  7.3 us
    all_to_all x1, starting transfers between devices, shards(): swapped = lax.all_to_all(parts, RING, 0, 0, tiled=True)  6.42 us
    all_to_all x1, starting transfers between devices, shards(): mine = lax.all_to_all(shared, RING, 0, 0, tiled=True)  5.95 us
    all_to_all x1, waiting for transfers between devices, shards(): swapped = lax.all_to_all(parts, RING, 0, 0, tiled=True)  5.73 us
    ppermute x10, waiting for transfers between devices, send(): return lax.ppermute(x, AXES, moves(**way))  1.48 us
  transfers between devices with their start and end apart: 12, of which 5 were waited for; matrix products, arithmetic and copies ran while one was open for 2% of the time, Pallas kernels for 27%

profile of v9, /device:TPU:1, one launch (start us, length us, event | category | flops | bytes accessed | tf_op | source)
XLA Modules:
  0.0 66.1 jit_solution(12116742096461650110)
XLA Ops:
  0.6 0.0 copy-start.5
  0.6 0.0 copy-start.4
  0.7 0.0 copy-start.3
  0.7 1.5 %collective-permute-start = (bf16[16,32,256]{2,1,0:T(8,128)(2,1)}, bf16[16,32,256]{2,1,0:T(8,128)(2,1)S(1)}, u32[]{:S(2)}, u32[]{:S(2)}) collective-permute-start(bf16[16,32,256]{2,1,0:T(8,128)(2,1)} %fo.1), channel_id=1, source_target_pairs={{0,32},{1,33},{2,34},{3,35},{4,36},{5,37},{6,38},{7,39},{8,40},{9,... | collective-permute-start | bytes 786440 | tf_op jit(solution)/shard_map/ppermute | solution.py:39
  2.2 0.1 collective-permute-start.1
  2.3 1.1 %pad_maximum_fusion.own = bf16[2,16,32,256]{3,2,1,0:T(8,128)(2,1)S(1)} fusion(bf16[1,16,32,256]{3,2,1,0:T(8,128)(2,1)} %bitcast.6, bf16[1,16,32,256]{3,2,1,0:T(8,128)(2,1)} %bitcast.7), kind=kLoop, calls=%fused_computation | loop fusion | flops 262144 | bytes 1048576 | tf_op jit(solution)/shard_map/stack | solution.py:427
  3.4 0.2 collective-permute-done.other.fx
  3.6 8.8 %collective-permute-start.2 = (bf16[32,2,256]{2,1,0:T(2,128)(2,1)S(1)}, bf16[32,2,256]{2,1,0:T(2,128)(2,1)S(1)}, u32[]{:S(2)}, u32[]{:S(2)}) collective-permute-start(bf16[32,2,256]{2,1,0:T(2,128)(2,1)S(1)} %shard_map.85.after), channel_id=1, source_target_pairs={{0,1},{1,2},{2,3},{3,4},{4,5},{5,6},{6,7},{7,8},{8,9},{9,10},{10,1... | collective-permute-start | bytes 98312 | tf_op jit(solution)/shard_map/ppermute | solution.py:39
  12.4 0.0 collective-permute-done.1.cx.other
  12.4 0.3 collective-permute-start.6
  12.8 0.0 copy-done.5
  12.8 0.0 copy-done.4
  12.8 0.1 fusion.2
  12.8 0.0 copy-done.3
  12.9 0.1 collective-permute-start.3
  13.0 1.8 %shard_map.86 = (bf16[16,288,256]{2,1,0:T(8,128)(2,1)S(1)}, bf16[256,512]{1,0:T(8,128)(2,1)S(1)}, bf16[16,256]{1,0:T(8,128)(2,1)S(1)}) custom-call(bf16[9,16,25]{2,1,0:T(8,128)(2,1)S(1)} %select_bitcast_fusion.mo, bf16[2,16,32,256]{3,2,1,0:T(8,128)(2,1)S(1)} %pad_maximum_fusion.own, bf16[32,2,256]{2,1,0:T(2,128)(2,1)S(1)} %shard_map.85.after), custom_call_target="tpu_custom_call" | custom-call | flops 94371840 | bytes 4194304 | tf_op jit(solution)/shard_map/pallas_call | solution.py:61
  14.8 0.0 collective-permute-done.3.mx
  14.8 1.8 %shard_map.87 = (bf16[16,288,256]{2,1,0:T(8,128)(2,1)S(1)}, bf16[256,512]{1,0:T(8,128)(2,1)S(1)}, bf16[16,256]{1,0:T(8,128)(2,1)S(1)}) custom-call(bf16[9,16,25]{2,1,0:T(8,128)(2,1)S(1)} %collective-permute-done.3.mx, bf16[16,32,256]{2,1,0:T(8,128)(2,1)S(1)} %collective-permute-done.1.cx.other, bf16[16,256]{1,0:T(8,128)(2,1)S(1)} %get-tuple-element.26.after.to), custom_call_target="tpu_custom_call" | custom-call | flops 94371840 | bytes 4194304 | tf_op jit(solution)/shard_map/pallas_call | solution.py:61
  16.6 0.0 collective-permute-done.2.near
  16.6 0.6 collective-permute-start.4
  17.1 0.0 collective-permute-done.6.near
  17.1 0.1 collective-permute-start.7
  17.2 0.8 %collective-permute-done.4.far = bf16[32,2,256]{2,1,0:T(2,128)(2,1)S(1)} collective-permute-done((bf16[32,2,256]{2,1,0:T(2,128)(2,1)S(1)}, bf16[32,2,256]{2,1,0:T(2,128)(2,1)S(1)}, u32[]{:S(2)}, u32[]{:S(2)}) %collective-permute-start.4) | collective-permute-done | bytes 32800 | tf_op jit(solution)/shard_map/ppermute | solution.py:39
  18.0 0.4 collective-permute-start.5
  18.4 0.0 collective-permute-done.7.far
  18.4 1.2 %collective-permute-start.8 = (bf16[2,40,256]{2,1,0:T(8,128)(2,1)S(1)}, bf16[2,40,256]{2,1,0:T(8,128)(2,1)S(1)}, u32[]{:S(2)}, u32[]{:S(2)}) collective-permute-start(bf16[2,40,256]{2,1,0:T(8,128)(2,1)S(1)} %shard_map.92), channel_id=1, source_target_pairs={{0,64},{1,65},{2,66},{3,67},{4,68},{5,69},{6,70},{7,71},{8,72},{9,... | collective-permute-start | bytes 122888 | tf_op jit(solution)/shard_map/ppermute | solution.py:39
  19.7 2.4 %shard_map.89.grad = f32[9,128,256]{2,1,0:T(8,128)S(1)} custom-call(bf16[2,16,32,256]{3,2,1,0:T(8,128)(2,1)S(1)} %pad_maximum_fusion.own, bf16[16,32,256]{2,1,0:T(8,128)(2,1)S(1)} %collective-permute-done.other.fx, bf16[32,2,256]{2,1,0:T(2,128)(2,1)S(1)} %collective-permute-done.2.near, bf16[32,2,256]{2,1,0:T(2,128)(2,1)S(1)} %collective-permute-done.4.far, ...), custom_call_target="tpu_custom_call" | custom-call | flops 1811939328 | bytes 7340032 | tf_op jit(solution)/shard_map/pallas_call | solution.py:61
  22.1 0.0 copy-start
  22.1 0.0 copy-start.2
  22.1 0.0 collective-permute-done.5.rows
  22.1 1.4 %shard_map.90 = (bf16[64,9,4,128]{3,2,1,0:T(4,128)(2,1)}, f32[8,128]{1,0:T(8,128)S(1)}) custom-call(bf16[2,16,32,256]{3,2,1,0:T(8,128)(2,1)S(1)} %pad_maximum_fusion.own, bf16[16,32,256]{2,1,0:T(8,128)(2,1)S(1)} %collective-permute-done.other.fx, bf16[16,32,256]{2,1,0:T(8,128)(2,1)S(1)} %collective-permute-done.1.cx.other, ...), custom_call_target="tpu_custom_call" | custom-call | flops 37748736 | bytes 3145728 | tf_op jit(solution)/shard_map/pallas_call | solution.py:61
  23.5 0.0 collective-permute-done.8.rows
  23.5 6.4 %all-to-all-start = ((bf16[64,9,4,128]{3,2,1,0:T(4,128)(2,1)}), bf16[64,9,4,128]{3,2,1,0:T(4,128)(2,1)S(1)}, u32[]{:S(2)}, u32[]{:S(2)}) async-start(bf16[64,9,4,128]{3,2,1,0:T(4,128)(2,1)} %get-tuple-element.35), calls=%async_computation | async-start | bytes 1179648 | tf_op jit(solution)/shard_map/all_to_all | solution.py:513
  30.0 0.0 copy-done
  30.0 0.0 copy-done.2
  30.0 0.0 copy-start.1
  30.0 5.9 %shard_map.93 = (bf16[16,32,256]{2,1,0:T(8,128)(2,1)}, f32[8,128]{1,0:T(8,128)S(1)}) custom-call(bf16[16,32,256]{2,1,0:T(8,128)(2,1)S(1)} %copy-done, bf16[16,32,256]{2,1,0:T(8,128)(2,1)S(1)} %collective-permute-done.1.cx.other, bf16[32,2,256]{2,1,0:T(2,128)(2,1)S(1)} %collective-permute-done.6.near, bf16[32,2,256]{2,1,0:T(2,128)(2,1)S(1)} %collective-permute-done.7.far, ...), custom_call_target="tpu_custom_call" | custom-call | flops 1971322880 | bytes 8388608 | tf_op jit(solution)/shard_map/pallas_call | solution.py:61
  35.9 5.7 %all-to-all-done.parts = bf16[64,9,4,128]{3,2,1,0:T(4,128)(2,1)S(1)} async-done(((bf16[64,9,4,128]{3,2,1,0:T(4,128)(2,1)}), bf16[64,9,4,128]{3,2,1,0:T(4,128)(2,1)S(1)}, u32[]{:S(2)}, u32[]{:S(2)}) %all-to-all-start) | async-done | bytes 589856 | tf_op jit(solution)/shard_map/all_to_all | solution.py:513
  41.6 1.1 %shard_map.94 = (bf16[64,9,4,128]{3,2,1,0:T(4,128)(2,1)}, f32[8,128]{1,0:T(8,128)S(1)}) custom-call(bf16[64,9,4,128]{3,2,1,0:T(4,128)(2,1)S(1)} %all-to-all-done.parts, f32[8,128]{1,0:T(8,128)S(1)} %get-tuple-element.38.after), custom_call_target="tpu_custom_call" | custom-call | bytes 1048576 | tf_op jit(solution)/shard_map/pallas_call | solution.py:61
  42.7 6.0 %all-to-all-start.1 = ((bf16[64,9,4,128]{3,2,1,0:T(4,128)(2,1)}), bf16[64,9,4,128]{3,2,1,0:T(4,128)(2,1)S(1)}, u32[]{:S(2)}, u32[]{:S(2)}) async-start(bf16[64,9,4,128]{3,2,1,0:T(4,128)(2,1)} %get-tuple-element.39), calls=%async_computation.1 | async-start | bytes 1179648 | tf_op jit(solution)/shard_map/all_to_all | solution.py:540
  48.7 0.0 copy-done.1
  48.7 3.7 %shard_map.95 = (bf16[16,32,256]{2,1,0:T(8,128)(2,1)}, f32[8,128]{1,0:T(8,128)}) custom-call(bf16[16,32,256]{2,1,0:T(8,128)(2,1)S(1)} %copy-done.1, bf16[16,32,256]{2,1,0:T(8,128)(2,1)S(1)} %collective-permute-done.other.fx, bf16[32,2,256]{2,1,0:T(2,128)(2,1)S(1)} %collective-permute-done.2.near, bf16[32,2,256]{2,1,0:T(2,128)(2,1)S(1)} %collective-permute-done.4.far, ...), custom_call_target="tpu_custom_call" | custom-call | flops 1207959552 | bytes 8388608 | tf_op jit(solution)/shard_map/pallas_call | solution.py:61
  52.4 7.3 %all-to-all-done.1.mine = bf16[64,9,4,128]{3,2,1,0:T(4,128)(2,1)S(1)} async-done(((bf16[64,9,4,128]{3,2,1,0:T(4,128)(2,1)}), bf16[64,9,4,128]{3,2,1,0:T(4,128)(2,1)S(1)}, u32[]{:S(2)}, u32[]{:S(2)}) %all-to-all-start.1) | async-done | bytes 589856 | tf_op jit(solution)/shard_map/all_to_all | solution.py:540
  59.7 3.5 %collective-permute-start.9 = (bf16[64,9,4,128]{3,2,1,0:T(4,128)(2,1)S(1)}, bf16[64,9,4,128]{3,2,1,0:T(4,128)(2,1)S(1)}, u32[]{:S(2)}, u32[]{:S(2)}) collective-permute-start(bf16[64,9,4,128]{3,2,1,0:T(4,128)(2,1)S(1)} %all-to-all-done.1.mine), channel_id=1, source_target_pairs={{0,32},{1,33},{2,34},{3,35},{4,36},{5,37},{6,38},{7,39},{8,40},{9,... | collective-permute-start | bytes 1769480 | tf_op jit(solution)/shard_map/ppermute | solution.py:39
  63.2 1.1 %shard_map.96.before = f32[9,32,8,256]{3,2,1,0:T(8,128)} custom-call(bf16[64,9,4,128]{3,2,1,0:T(4,128)(2,1)S(1)} %all-to-all-done.1.mine), custom_call_target="tpu_custom_call" | custom-call | bytes 2097152 | tf_op jit(solution)/shard_map/pallas_call | solution.py:61
  64.3 0.5 collective-permute-done.9.theirs
  64.9 1.1 %shard_map.97 = f32[9,32,8,256]{3,2,1,0:T(8,128)} custom-call(bf16[64,9,4,128]{3,2,1,0:T(4,128)(2,1)S(1)} %collective-permute-done.9.theirs, f32[9,32,8,256]{3,2,1,0:T(8,128)} %shard_map.96.before), custom_call_target="tpu_custom_call", output_to_operand_aliasing={{}: (1, {})} | custom-call | bytes 2097152 | tf_op jit(solution)/shard_map/pallas_call | solution.py:61
  (7 shorter events, 0.1 us)
Async XLA Ops:
  0.6 12.1 %copy-start.5 = (s32[16]{0:T(128)S(1)}, s32[16]{0:T(128)}, u32[]{:S(2)}) copy-start(s32[16]{0:T(128)} %param.8) | copy-start | bytes 196
  0.6 12.1 %copy-start.4 = (s32[16]{0:T(128)S(1)}, s32[16]{0:T(128)}, u32[]{:S(2)}) copy-start(s32[16]{0:T(128)} %param.9) | copy-start | bytes 196
  0.7 12.2 %copy-start.3 = (bf16[16,9,25]{2,0,1:T(8,128)(2,1)S(1)}, bf16[16,9,25]{2,0,1:T(8,128)(2,1)}, u32[]{:S(2)}) copy-start(bf16[16,9,25]{2,0,1:T(8,128)(2,1)} %param.7) | copy-start | bytes 21604
  0.7 2.9 %collective-permute-start = (bf16[16,32,256]{2,1,0:T(8,128)(2,1)}, bf16[16,32,256]{2,1,0:T(8,128)(2,1)S(1)}, u32[]{:S(2)}, u32[]{:S(2)}) collective-permute-start(bf16[16,32,256]{2,1,0:T(8,128)(2,1)} %fo.1), channel_id=1, source_target_pairs={{0,32},{1,33},{2,34},{3,35},{4,36},{5,37},{6,38},{7,39},{8,40},{9,... | collective-permute-start | bytes 786440 | tf_op jit(solution)/shard_map/ppermute | solution.py:39
  2.2 10.2 %collective-permute-start.1 = (bf16[16,32,256]{2,1,0:T(8,128)(2,1)}, bf16[16,32,256]{2,1,0:T(8,128)(2,1)S(1)}, u32[]{:S(2)}, u32[]{:S(2)}) collective-permute-start(bf16[16,32,256]{2,1,0:T(8,128)(2,1)} %co.1), channel_id=1, source_target_pairs={{0,32},{1,33},{2,34},{3,35},{4,36},{5,37},{6,38},{7,39},{8,40},{9,... | collective-permute-start | bytes 786440 | tf_op jit(solution)/shard_map/ppermute | solution.py:39
  3.6 13.0 %collective-permute-start.2 = (bf16[32,2,256]{2,1,0:T(2,128)(2,1)S(1)}, bf16[32,2,256]{2,1,0:T(2,128)(2,1)S(1)}, u32[]{:S(2)}, u32[]{:S(2)}) collective-permute-start(bf16[32,2,256]{2,1,0:T(2,128)(2,1)S(1)} %shard_map.85.after), channel_id=1, source_target_pairs={{0,1},{1,2},{2,3},{3,4},{4,5},{5,6},{6,7},{7,8},{8,9},{9,10},{10,1... | collective-permute-start | bytes 98312 | tf_op jit(solution)/shard_map/ppermute | solution.py:39
  12.4 4.7 %collective-permute-start.6 = (bf16[32,2,256]{2,1,0:T(2,128)(2,1)S(1)}, bf16[32,2,256]{2,1,0:T(2,128)(2,1)S(1)}, u32[]{:S(2)}, u32[]{:S(2)}) collective-permute-start(bf16[32,2,256]{2,1,0:T(2,128)(2,1)S(1)} %shard_map.91), channel_id=1, source_target_pairs={{0,1},{1,2},{2,3},{3,4},{4,5},{5,6},{6,7},{7,8},{8,9},{9,10},{10,1... | collective-permute-start | bytes 98312 | tf_op jit(solution)/shard_map/ppermute | solution.py:39
  12.9 1.9 %collective-permute-start.3 = (bf16[9,16,25]{2,1,0:T(8,128)(2,1)S(1)}, bf16[9,16,25]{2,1,0:T(8,128)(2,1)S(1)}, u32[]{:S(2)}, u32[]{:S(2)}) collective-permute-start(bf16[9,16,25]{2,1,0:T(8,128)(2,1)S(1)} %select_bitcast_fusion.mo), channel_id=1, source_target_pairs={{0,32},{1,33},{2,34},{3,35},{4,36},{5,37},{6,38},{7,39},{8,40},{9,... | collective-permute-start | bytes 21608 | tf_op jit(solution)/shard_map/ppermute | solution.py:39
  16.6 1.4 %collective-permute-start.4 = (bf16[32,2,256]{2,1,0:T(2,128)(2,1)S(1)}, bf16[32,2,256]{2,1,0:T(2,128)(2,1)S(1)}, u32[]{:S(2)}, u32[]{:S(2)}) collective-permute-start(bf16[32,2,256]{2,1,0:T(2,128)(2,1)S(1)} %collective-permute-done.2.near), channel_id=1, source_target_pairs={{0,32},{1,33},{2,34},{3,35},{4,36},{5,37},{6,38},{7,39},{8,40},{9,... | collective-permute-start | bytes 98312 | tf_op jit(solution)/shard_map/ppermute | solution.py:39
  17.1 1.3 %collective-permute-start.7 = (bf16[32,2,256]{2,1,0:T(2,128)(2,1)S(1)}, bf16[32,2,256]{2,1,0:T(2,128)(2,1)S(1)}, u32[]{:S(2)}, u32[]{:S(2)}) collective-permute-start(bf16[32,2,256]{2,1,0:T(2,128)(2,1)S(1)} %collective-permute-done.6.near), channel_id=1, source_target_pairs={{0,32},{1,33},{2,34},{3,35},{4,36},{5,37},{6,38},{7,39},{8,40},{9,... | collective-permute-start | bytes 98312 | tf_op jit(solution)/shard_map/ppermute | solution.py:39
  18.0 4.1 %collective-permute-start.5 = (bf16[2,40,256]{2,1,0:T(8,128)(2,1)S(1)}, bf16[2,40,256]{2,1,0:T(8,128)(2,1)S(1)}, u32[]{:S(2)}, u32[]{:S(2)}) collective-permute-start(bf16[2,40,256]{2,1,0:T(8,128)(2,1)S(1)} %shard_map.88), channel_id=1, source_target_pairs={{0,64},{1,65},{2,66},{3,67},{4,68},{5,69},{6,70},{7,71},{8,72},{9,... | collective-permute-start | bytes 122888 | tf_op jit(solution)/shard_map/ppermute | solution.py:39
  18.4 5.1 %collective-permute-start.8 = (bf16[2,40,256]{2,1,0:T(8,128)(2,1)S(1)}, bf16[2,40,256]{2,1,0:T(8,128)(2,1)S(1)}, u32[]{:S(2)}, u32[]{:S(2)}) collective-permute-start(bf16[2,40,256]{2,1,0:T(8,128)(2,1)S(1)} %shard_map.92), channel_id=1, source_target_pairs={{0,64},{1,65},{2,66},{3,67},{4,68},{5,69},{6,70},{7,71},{8,72},{9,... | collective-permute-start | bytes 122888 | tf_op jit(solution)/shard_map/ppermute | solution.py:39
  22.1 7.9 %copy-start = (bf16[16,32,256]{2,1,0:T(8,128)(2,1)S(1)}, bf16[16,32,256]{2,1,0:T(8,128)(2,1)}, u32[]{:S(2)}) copy-start(bf16[16,32,256]{2,1,0:T(8,128)(2,1)} %co.1) | copy-start | bytes 786436
  22.1 7.9 %copy-start.2 = (bf16[9,256,256]{2,1,0:T(8,128)(2,1)S(1)}, bf16[9,256,256]{2,1,0:T(8,128)(2,1)}, u32[]{:S(2)}) copy-start(bf16[9,256,256]{2,1,0:T(8,128)(2,1)} %param.10) | copy-start | bytes 3538948
  23.5 18.1 %all-to-all-start = ((bf16[64,9,4,128]{3,2,1,0:T(4,128)(2,1)}), bf16[64,9,4,128]{3,2,1,0:T(4,128)(2,1)S(1)}, u32[]{:S(2)}, u32[]{:S(2)}) async-start(bf16[64,9,4,128]{3,2,1,0:T(4,128)(2,1)} %get-tuple-element.35), calls=%async_computation | async-start | bytes 1179648 | tf_op jit(solution)/shard_map/all_to_all | solution.py:513
  30.0 18.7 %copy-start.1 = (bf16[16,32,256]{2,1,0:T(8,128)(2,1)S(1)}, bf16[16,32,256]{2,1,0:T(8,128)(2,1)}, u32[]{:S(2)}) copy-start(bf16[16,32,256]{2,1,0:T(8,128)(2,1)} %fo.1) | copy-start | bytes 786436
  42.7 16.9 %all-to-all-start.1 = ((bf16[64,9,4,128]{3,2,1,0:T(4,128)(2,1)}), bf16[64,9,4,128]{3,2,1,0:T(4,128)(2,1)S(1)}, u32[]{:S(2)}, u32[]{:S(2)}) async-start(bf16[64,9,4,128]{3,2,1,0:T(4,128)(2,1)} %get-tuple-element.39), calls=%async_computation.1 | async-start | bytes 1179648 | tf_op jit(solution)/shard_map/all_to_all | solution.py:540
  59.7 5.2 %collective-permute-start.9 = (bf16[64,9,4,128]{3,2,1,0:T(4,128)(2,1)S(1)}, bf16[64,9,4,128]{3,2,1,0:T(4,128)(2,1)S(1)}, u32[]{:S(2)}, u32[]{:S(2)}) collective-permute-start(bf16[64,9,4,128]{3,2,1,0:T(4,128)(2,1)S(1)} %all-to-all-done.1.mine), channel_id=1, source_target_pairs={{0,32},{1,33},{2,34},{3,35},{4,36},{5,37},{6,38},{7,39},{8,40},{9,... | collective-permute-start | bytes 1769480 | tf_op jit(solution)/shard_map/ppermute | solution.py:39

commit v10 on v7

--- a/solution.py
+++ b/solution.py
@@ -304,10 +304,13 @@
 
 def sum_kernel(scale, parts, after, out, token, copies, sems):
     mark(token)
-    total = jnp.sum(parts[...].astype(f32), axis=0) * scale
-    copies[...] = jnp.broadcast_to(total.astype(bf16)[None], copies.shape)
+    for k in range(BASIS):
+        total = parts[0, k].astype(f32)
+        for j in range(1, 64):
+            total = total + parts[j, k].astype(f32)
+        copies[:, k] = jnp.broadcast_to((total * scale).astype(bf16)[None], (16, 4, HALF))
     sends = [
-        pltpu.make_async_copy(copies, out.at[i * 8 : (i + 1) * 8], sems.at[i]) for i in range(8)
+        pltpu.make_async_copy(copies, out.at[i * 16 : (i + 1) * 16], sems.at[i]) for i in range(4)
     ]
     for x in sends:
         x.start()
@@ -530,7 +533,7 @@
         functools.partial(sum_kernel, 1.0 / math.sqrt(64 * 1024)),
         [((64, *CHUNK), bf16), TOKEN],
         (swapped, after),
-        scratch=[pltpu.VMEM((8, *CHUNK), bf16), pltpu.SemaphoreType.DMA((8,))],
+        scratch=[pltpu.VMEM((16, *CHUNK), bf16), pltpu.SemaphoreType.DMA((4,))],
         to=(0,),
         traffic=2**20,
     )

time: 66.3 us -> 66.2 us (level)
  no operation moved by 1% of the time
where the time goes in v10:
time: 66.2 us; the launch traced here: 65.9 us
  starting transfers between devices  29.5 us (45%)
  Pallas kernels  20.3 us (31%)
  waiting for transfers between devices  13.9 us (21%)
  other arithmetic  1.18 us (2%)
  between operations  1.02 us (2%)
    pallas_call x13, Pallas kernels, call(): pl.pallas_call(kernel, out_shape=[jax.ShapeDtypeStruct(*o) for o in outs]...  20.3 us
    ppermute x10, starting transfers between devices, send(): return lax.ppermute(x, AXES, moves(**way))  16.6 us
    all_to_all x1, waiting for transfers between devices, shards(): swapped = lax.all_to_all(parts, RING, 0, 0, tiled=True)  7.3 us
    all_to_all x1, starting transfers between devices, shards(): mine = lax.all_to_all(shared, RING, 0, 0, tiled=True)  6.48 us
    all_to_all x1, starting transfers between devices, shards(): swapped = lax.all_to_all(parts, RING, 0, 0, tiled=True)  6.4 us
    all_to_all x1, waiting for transfers between devices, shards(): mine = lax.all_to_all(shared, RING, 0, 0, tiled=True)  5.17 us
    ppermute x10, waiting for transfers between devices, send(): return lax.ppermute(x, AXES, moves(**way))  1.48 us
  transfers between devices with their start and end apart: 12, of which 5 were waited for; matrix products, arithmetic and copies ran while one was open for 2% of the time, Pallas kernels for 25%

profile of v10, /device:TPU:1, one launch (start us, length us, event | category | flops | bytes accessed | tf_op | source)
XLA Modules:
  0.0 65.9 jit_solution(465858173032359407)
XLA Ops:
  0.6 0.0 copy-start.5
  0.6 0.0 copy-start.4
  0.7 0.0 copy-start.3
  0.7 1.5 %collective-permute-start = (bf16[16,32,256]{2,1,0:T(8,128)(2,1)}, bf16[16,32,256]{2,1,0:T(8,128)(2,1)S(1)}, u32[]{:S(2)}, u32[]{:S(2)}) collective-permute-start(bf16[16,32,256]{2,1,0:T(8,128)(2,1)} %fo.1), channel_id=1, source_target_pairs={{0,32},{1,33},{2,34},{3,35},{4,36},{5,37},{6,38},{7,39},{8,40},{9,... | collective-permute-start | bytes 786440 | tf_op jit(solution)/shard_map/ppermute | solution.py:39
  2.2 0.1 collective-permute-start.3
  2.3 1.1 %pad_maximum_fusion.own = bf16[2,16,32,256]{3,2,1,0:T(8,128)(2,1)S(1)} fusion(bf16[1,16,32,256]{3,2,1,0:T(8,128)(2,1)} %bitcast.7, bf16[1,16,32,256]{3,2,1,0:T(8,128)(2,1)} %bitcast.6), kind=kLoop, calls=%fused_computation | loop fusion | flops 262144 | bytes 1048576 | tf_op jit(solution)/shard_map/stack | solution.py:430
  3.4 0.2 collective-permute-done.other.fx
  3.6 8.8 %collective-permute-start.1 = (bf16[32,2,256]{2,1,0:T(2,128)(2,1)S(1)}, bf16[32,2,256]{2,1,0:T(2,128)(2,1)S(1)}, u32[]{:S(2)}, u32[]{:S(2)}) collective-permute-start(bf16[32,2,256]{2,1,0:T(2,128)(2,1)S(1)} %shard_map.85.after), channel_id=1, source_target_pairs={{0,1},{1,2},{2,3},{3,4},{4,5},{5,6},{6,7},{7,8},{8,9},{9,10},{10,1... | collective-permute-start | bytes 98312 | tf_op jit(solution)/shard_map/ppermute | solution.py:39
  12.4 0.0 collective-permute-done.3.cx.other
  12.4 0.3 collective-permute-start.6
  12.8 0.0 copy-done.5
  12.8 0.0 copy-done.4
  12.8 0.1 fusion.2
  12.8 0.0 copy-done.3
  12.9 0.1 collective-permute-start.2
  13.0 1.8 %shard_map.86 = (bf16[16,288,256]{2,1,0:T(8,128)(2,1)S(1)}, bf16[256,512]{1,0:T(8,128)(2,1)S(1)}, bf16[16,256]{1,0:T(8,128)(2,1)S(1)}) custom-call(bf16[9,16,25]{2,1,0:T(8,128)(2,1)S(1)} %select_bitcast_fusion.mo, bf16[2,16,32,256]{3,2,1,0:T(8,128)(2,1)S(1)} %pad_maximum_fusion.own, bf16[32,2,256]{2,1,0:T(2,128)(2,1)S(1)} %shard_map.85.after), custom_call_target="tpu_custom_call" | custom-call | flops 94371840 | bytes 4194304 | tf_op jit(solution)/shard_map/pallas_call | solution.py:61
  14.8 0.0 collective-permute-done.2.mx
  14.8 1.8 %shard_map.87 = (bf16[16,288,256]{2,1,0:T(8,128)(2,1)S(1)}, bf16[256,512]{1,0:T(8,128)(2,1)S(1)}, bf16[16,256]{1,0:T(8,128)(2,1)S(1)}) custom-call(bf16[9,16,25]{2,1,0:T(8,128)(2,1)S(1)} %collective-permute-done.2.mx, bf16[16,32,256]{2,1,0:T(8,128)(2,1)S(1)} %collective-permute-done.3.cx.other, bf16[16,256]{1,0:T(8,128)(2,1)S(1)} %get-tuple-element.24.after.to), custom_call_target="tpu_custom_call" | custom-call | flops 94371840 | bytes 4194304 | tf_op jit(solution)/shard_map/pallas_call | solution.py:61
  16.6 0.0 collective-permute-done.1.near
  16.6 0.6 collective-permute-start.4
  17.1 0.0 collective-permute-done.6.near
  17.1 0.1 collective-permute-start.7
  17.2 0.8 %collective-permute-done.4.far = bf16[32,2,256]{2,1,0:T(2,128)(2,1)S(1)} collective-permute-done((bf16[32,2,256]{2,1,0:T(2,128)(2,1)S(1)}, bf16[32,2,256]{2,1,0:T(2,128)(2,1)S(1)}, u32[]{:S(2)}, u32[]{:S(2)}) %collective-permute-start.4) | collective-permute-done | bytes 32800 | tf_op jit(solution)/shard_map/ppermute | solution.py:39
  18.0 0.4 collective-permute-start.5
  18.4 0.0 collective-permute-done.7.far
  18.4 1.2 %collective-permute-start.8 = (bf16[2,40,256]{2,1,0:T(8,128)(2,1)S(1)}, bf16[2,40,256]{2,1,0:T(8,128)(2,1)S(1)}, u32[]{:S(2)}, u32[]{:S(2)}) collective-permute-start(bf16[2,40,256]{2,1,0:T(8,128)(2,1)S(1)} %shard_map.90), channel_id=1, source_target_pairs={{0,64},{1,65},{2,66},{3,67},{4,68},{5,69},{6,70},{7,71},{8,72},{9,... | collective-permute-start | bytes 122888 | tf_op jit(solution)/shard_map/ppermute | solution.py:39
  19.7 2.5 %shard_map.91.grad = f32[9,128,256]{2,1,0:T(8,128)S(1)} custom-call(bf16[2,16,32,256]{3,2,1,0:T(8,128)(2,1)S(1)} %pad_maximum_fusion.own, bf16[16,32,256]{2,1,0:T(8,128)(2,1)S(1)} %collective-permute-done.other.fx, bf16[32,2,256]{2,1,0:T(2,128)(2,1)S(1)} %collective-permute-done.1.near, bf16[32,2,256]{2,1,0:T(2,128)(2,1)S(1)} %collective-permute-done.4.far, ...), custom_call_target="tpu_custom_call" | custom-call | flops 1811939328 | bytes 7340032 | tf_op jit(solution)/shard_map/pallas_call | solution.py:61
  22.1 0.0 copy-start
  22.1 0.0 copy-start.2
  22.1 0.0 collective-permute-done.5.rows
  22.1 0.0 collective-permute-done.8.after.rows
  22.2 1.4 %shard_map.92 = (bf16[64,9,4,128]{3,2,1,0:T(4,128)(2,1)}, f32[8,128]{1,0:T(8,128)S(1)}) custom-call(bf16[2,16,32,256]{3,2,1,0:T(8,128)(2,1)S(1)} %pad_maximum_fusion.own, bf16[16,32,256]{2,1,0:T(8,128)(2,1)S(1)} %collective-permute-done.other.fx, bf16[16,32,256]{2,1,0:T(8,128)(2,1)S(1)} %collective-permute-done.3.cx.other, ...), custom_call_target="tpu_custom_call" | custom-call | flops 37748736 | bytes 3145728 | tf_op jit(solution)/shard_map/pallas_call | solution.py:61
  23.5 6.4 %all-to-all-start = ((bf16[64,9,4,128]{3,2,1,0:T(4,128)(2,1)}), bf16[64,9,4,128]{3,2,1,0:T(4,128)(2,1)S(1)}, u32[]{:S(2)}, u32[]{:S(2)}) async-start(bf16[64,9,4,128]{3,2,1,0:T(4,128)(2,1)} %get-tuple-element.34), calls=%async_computation | async-start | bytes 1179648 | tf_op jit(solution)/shard_map/all_to_all | solution.py:515
  30.0 0.0 copy-done
  30.0 0.0 copy-done.2
  30.0 0.0 copy-start.1
  30.0 3.7 %shard_map.93 = (bf16[16,32,256]{2,1,0:T(8,128)(2,1)}, f32[8,128]{1,0:T(8,128)S(1)}) custom-call(bf16[16,32,256]{2,1,0:T(8,128)(2,1)S(1)} %copy-done, bf16[16,32,256]{2,1,0:T(8,128)(2,1)S(1)} %collective-permute-done.other.fx, bf16[32,2,256]{2,1,0:T(2,128)(2,1)S(1)} %collective-permute-done.1.near, bf16[32,2,256]{2,1,0:T(2,128)(2,1)S(1)} %collective-permute-done.4.far, ...), custom_call_target="tpu_custom_call" | custom-call | flops 1207959552 | bytes 8388608 | tf_op jit(solution)/shard_map/pallas_call | solution.py:61
  33.7 7.3 %all-to-all-done.parts = bf16[64,9,4,128]{3,2,1,0:T(4,128)(2,1)S(1)} async-done(((bf16[64,9,4,128]{3,2,1,0:T(4,128)(2,1)}), bf16[64,9,4,128]{3,2,1,0:T(4,128)(2,1)S(1)}, u32[]{:S(2)}, u32[]{:S(2)}) %all-to-all-start) | async-done | bytes 589856 | tf_op jit(solution)/shard_map/all_to_all | solution.py:515
  41.0 1.0 %shard_map.94 = (bf16[64,9,4,128]{3,2,1,0:T(4,128)(2,1)}, f32[8,128]{1,0:T(8,128)S(1)}) custom-call(bf16[64,9,4,128]{3,2,1,0:T(4,128)(2,1)S(1)} %all-to-all-done.parts, f32[8,128]{1,0:T(8,128)S(1)} %get-tuple-element.35.after), custom_call_target="tpu_custom_call" | custom-call | bytes 1048576 | tf_op jit(solution)/shard_map/pallas_call | solution.py:61
  42.0 6.5 %all-to-all-start.1 = ((bf16[64,9,4,128]{3,2,1,0:T(4,128)(2,1)}), bf16[64,9,4,128]{3,2,1,0:T(4,128)(2,1)S(1)}, u32[]{:S(2)}, u32[]{:S(2)}) async-start(bf16[64,9,4,128]{3,2,1,0:T(4,128)(2,1)} %get-tuple-element.36), calls=%async_computation.1 | async-start | bytes 1179648 | tf_op jit(solution)/shard_map/all_to_all | solution.py:541
  48.5 0.0 copy-done.1
  48.5 5.8 %shard_map.95 = (bf16[16,32,256]{2,1,0:T(8,128)(2,1)}, f32[8,128]{1,0:T(8,128)}) custom-call(bf16[16,32,256]{2,1,0:T(8,128)(2,1)S(1)} %copy-done.1, bf16[16,32,256]{2,1,0:T(8,128)(2,1)S(1)} %collective-permute-done.3.cx.other, bf16[32,2,256]{2,1,0:T(2,128)(2,1)S(1)} %collective-permute-done.6.near, bf16[32,2,256]{2,1,0:T(2,128)(2,1)S(1)} %collective-permute-done.7.far, ...), custom_call_target="tpu_custom_call" | custom-call | flops 1971322880 | bytes 8388608 | tf_op jit(solution)/shard_map/pallas_call | solution.py:61
  54.4 5.2 %all-to-all-done.1.mine = bf16[64,9,4,128]{3,2,1,0:T(4,128)(2,1)S(1)} async-done(((bf16[64,9,4,128]{3,2,1,0:T(4,128)(2,1)}), bf16[64,9,4,128]{3,2,1,0:T(4,128)(2,1)S(1)}, u32[]{:S(2)}, u32[]{:S(2)}) %all-to-all-start.1) | async-done | bytes 589856 | tf_op jit(solution)/shard_map/all_to_all | solution.py:541
  59.5 3.5 %collective-permute-start.9 = (bf16[64,9,4,128]{3,2,1,0:T(4,128)(2,1)S(1)}, bf16[64,9,4,128]{3,2,1,0:T(4,128)(2,1)S(1)}, u32[]{:S(2)}, u32[]{:S(2)}) collective-permute-start(bf16[64,9,4,128]{3,2,1,0:T(4,128)(2,1)S(1)} %all-to-all-done.1.mine), channel_id=1, source_target_pairs={{0,32},{1,33},{2,34},{3,35},{4,36},{5,37},{6,38},{7,39},{8,40},{9,... | collective-permute-start | bytes 1769480 | tf_op jit(solution)/shard_map/ppermute | solution.py:39
  63.0 1.1 %shard_map.96.before = f32[9,32,8,256]{3,2,1,0:T(8,128)} custom-call(bf16[64,9,4,128]{3,2,1,0:T(4,128)(2,1)S(1)} %all-to-all-done.1.mine), custom_call_target="tpu_custom_call" | custom-call | bytes 2097152 | tf_op jit(solution)/shard_map/pallas_call | solution.py:61
  64.1 0.5 collective-permute-done.9.theirs
  64.7 1.1 %shard_map.97 = f32[9,32,8,256]{3,2,1,0:T(8,128)} custom-call(bf16[64,9,4,128]{3,2,1,0:T(4,128)(2,1)S(1)} %collective-permute-done.9.theirs, f32[9,32,8,256]{3,2,1,0:T(8,128)} %shard_map.96.before), custom_call_target="tpu_custom_call", output_to_operand_aliasing={{}: (1, {})} | custom-call | bytes 2097152 | tf_op jit(solution)/shard_map/pallas_call | solution.py:61
  (7 shorter events, 0.1 us)
Async XLA Ops:
  0.6 12.1 %copy-start.5 = (s32[16]{0:T(128)S(1)}, s32[16]{0:T(128)}, u32[]{:S(2)}) copy-start(s32[16]{0:T(128)} %param.8) | copy-start | bytes 196
  0.6 12.1 %copy-start.4 = (s32[16]{0:T(128)S(1)}, s32[16]{0:T(128)}, u32[]{:S(2)}) copy-start(s32[16]{0:T(128)} %param.9) | copy-start | bytes 196
  0.7 12.2 %copy-start.3 = (bf16[16,9,25]{2,0,1:T(8,128)(2,1)S(1)}, bf16[16,9,25]{2,0,1:T(8,128)(2,1)}, u32[]{:S(2)}) copy-start(bf16[16,9,25]{2,0,1:T(8,128)(2,1)} %param.7) | copy-start | bytes 21604
  0.7 2.9 %collective-permute-start = (bf16[16,32,256]{2,1,0:T(8,128)(2,1)}, bf16[16,32,256]{2,1,0:T(8,128)(2,1)S(1)}, u32[]{:S(2)}, u32[]{:S(2)}) collective-permute-start(bf16[16,32,256]{2,1,0:T(8,128)(2,1)} %fo.1), channel_id=1, source_target_pairs={{0,32},{1,33},{2,34},{3,35},{4,36},{5,37},{6,38},{7,39},{8,40},{9,... | collective-permute-start | bytes 786440 | tf_op jit(solution)/shard_map/ppermute | solution.py:39
  2.2 10.2 %collective-permute-start.3 = (bf16[16,32,256]{2,1,0:T(8,128)(2,1)}, bf16[16,32,256]{2,1,0:T(8,128)(2,1)S(1)}, u32[]{:S(2)}, u32[]{:S(2)}) collective-permute-start(bf16[16,32,256]{2,1,0:T(8,128)(2,1)} %co.1), channel_id=1, source_target_pairs={{0,32},{1,33},{2,34},{3,35},{4,36},{5,37},{6,38},{7,39},{8,40},{9,... | collective-permute-start | bytes 786440 | tf_op jit(solution)/shard_map/ppermute | solution.py:39
  3.6 13.0 %collective-permute-start.1 = (bf16[32,2,256]{2,1,0:T(2,128)(2,1)S(1)}, bf16[32,2,256]{2,1,0:T(2,128)(2,1)S(1)}, u32[]{:S(2)}, u32[]{:S(2)}) collective-permute-start(bf16[32,2,256]{2,1,0:T(2,128)(2,1)S(1)} %shard_map.85.after), channel_id=1, source_target_pairs={{0,1},{1,2},{2,3},{3,4},{4,5},{5,6},{6,7},{7,8},{8,9},{9,10},{10,1... | collective-permute-start | bytes 98312 | tf_op jit(solution)/shard_map/ppermute | solution.py:39
  12.4 4.7 %collective-permute-start.6 = (bf16[32,2,256]{2,1,0:T(2,128)(2,1)S(1)}, bf16[32,2,256]{2,1,0:T(2,128)(2,1)S(1)}, u32[]{:S(2)}, u32[]{:S(2)}) collective-permute-start(bf16[32,2,256]{2,1,0:T(2,128)(2,1)S(1)} %shard_map.89), channel_id=1, source_target_pairs={{0,1},{1,2},{2,3},{3,4},{4,5},{5,6},{6,7},{7,8},{8,9},{9,10},{10,1... | collective-permute-start | bytes 98312 | tf_op jit(solution)/shard_map/ppermute | solution.py:39
  12.9 1.9 %collective-permute-start.2 = (bf16[9,16,25]{2,1,0:T(8,128)(2,1)S(1)}, bf16[9,16,25]{2,1,0:T(8,128)(2,1)S(1)}, u32[]{:S(2)}, u32[]{:S(2)}) collective-permute-start(bf16[9,16,25]{2,1,0:T(8,128)(2,1)S(1)} %select_bitcast_fusion.mo), channel_id=1, source_target_pairs={{0,32},{1,33},{2,34},{3,35},{4,36},{5,37},{6,38},{7,39},{8,40},{9,... | collective-permute-start | bytes 21608 | tf_op jit(solution)/shard_map/ppermute | solution.py:39
  16.6 1.4 %collective-permute-start.4 = (bf16[32,2,256]{2,1,0:T(2,128)(2,1)S(1)}, bf16[32,2,256]{2,1,0:T(2,128)(2,1)S(1)}, u32[]{:S(2)}, u32[]{:S(2)}) collective-permute-start(bf16[32,2,256]{2,1,0:T(2,128)(2,1)S(1)} %collective-permute-done.1.near), channel_id=1, source_target_pairs={{0,32},{1,33},{2,34},{3,35},{4,36},{5,37},{6,38},{7,39},{8,40},{9,... | collective-permute-start | bytes 98312 | tf_op jit(solution)/shard_map/ppermute | solution.py:39
  17.1 1.3 %collective-permute-start.7 = (bf16[32,2,256]{2,1,0:T(2,128)(2,1)S(1)}, bf16[32,2,256]{2,1,0:T(2,128)(2,1)S(1)}, u32[]{:S(2)}, u32[]{:S(2)}) collective-permute-start(bf16[32,2,256]{2,1,0:T(2,128)(2,1)S(1)} %collective-permute-done.6.near), channel_id=1, source_target_pairs={{0,32},{1,33},{2,34},{3,35},{4,36},{5,37},{6,38},{7,39},{8,40},{9,... | collective-permute-start | bytes 98312 | tf_op jit(solution)/shard_map/ppermute | solution.py:39
  18.0 4.1 %collective-permute-start.5 = (bf16[2,40,256]{2,1,0:T(8,128)(2,1)S(1)}, bf16[2,40,256]{2,1,0:T(8,128)(2,1)S(1)}, u32[]{:S(2)}, u32[]{:S(2)}) collective-permute-start(bf16[2,40,256]{2,1,0:T(8,128)(2,1)S(1)} %shard_map.88), channel_id=1, source_target_pairs={{0,64},{1,65},{2,66},{3,67},{4,68},{5,69},{6,70},{7,71},{8,72},{9,... | collective-permute-start | bytes 122888 | tf_op jit(solution)/shard_map/ppermute | solution.py:39
  18.4 3.7 %collective-permute-start.8 = (bf16[2,40,256]{2,1,0:T(8,128)(2,1)S(1)}, bf16[2,40,256]{2,1,0:T(8,128)(2,1)S(1)}, u32[]{:S(2)}, u32[]{:S(2)}) collective-permute-start(bf16[2,40,256]{2,1,0:T(8,128)(2,1)S(1)} %shard_map.90), channel_id=1, source_target_pairs={{0,64},{1,65},{2,66},{3,67},{4,68},{5,69},{6,70},{7,71},{8,72},{9,... | collective-permute-start | bytes 122888 | tf_op jit(solution)/shard_map/ppermute | solution.py:39
  22.1 7.8 %copy-start = (bf16[16,32,256]{2,1,0:T(8,128)(2,1)S(1)}, bf16[16,32,256]{2,1,0:T(8,128)(2,1)}, u32[]{:S(2)}) copy-start(bf16[16,32,256]{2,1,0:T(8,128)(2,1)} %fo.1) | copy-start | bytes 786436
  22.1 7.8 %copy-start.2 = (bf16[9,256,256]{2,1,0:T(8,128)(2,1)S(1)}, bf16[9,256,256]{2,1,0:T(8,128)(2,1)}, u32[]{:S(2)}) copy-start(bf16[9,256,256]{2,1,0:T(8,128)(2,1)} %param.10) | copy-start | bytes 3538948
  23.5 17.4 %all-to-all-start = ((bf16[64,9,4,128]{3,2,1,0:T(4,128)(2,1)}), bf16[64,9,4,128]{3,2,1,0:T(4,128)(2,1)S(1)}, u32[]{:S(2)}, u32[]{:S(2)}) async-start(bf16[64,9,4,128]{3,2,1,0:T(4,128)(2,1)} %get-tuple-element.34), calls=%async_computation | async-start | bytes 1179648 | tf_op jit(solution)/shard_map/all_to_all | solution.py:515
  30.0 18.5 %copy-start.1 = (bf16[16,32,256]{2,1,0:T(8,128)(2,1)S(1)}, bf16[16,32,256]{2,1,0:T(8,128)(2,1)}, u32[]{:S(2)}) copy-start(bf16[16,32,256]{2,1,0:T(8,128)(2,1)} %co.1) | copy-start | bytes 786436
  42.0 17.5 %all-to-all-start.1 = ((bf16[64,9,4,128]{3,2,1,0:T(4,128)(2,1)}), bf16[64,9,4,128]{3,2,1,0:T(4,128)(2,1)S(1)}, u32[]{:S(2)}, u32[]{:S(2)}) async-start(bf16[64,9,4,128]{3,2,1,0:T(4,128)(2,1)} %get-tuple-element.36), calls=%async_computation.1 | async-start | bytes 1179648 | tf_op jit(solution)/shard_map/all_to_all | solution.py:541
  59.5 5.1 %collective-permute-start.9 = (bf16[64,9,4,128]{3,2,1,0:T(4,128)(2,1)S(1)}, bf16[64,9,4,128]{3,2,1,0:T(4,128)(2,1)S(1)}, u32[]{:S(2)}, u32[]{:S(2)}) collective-permute-start(bf16[64,9,4,128]{3,2,1,0:T(4,128)(2,1)S(1)} %all-to-all-done.1.mine), channel_id=1, source_target_pairs={{0,32},{1,33},{2,34},{3,35},{4,36},{5,37},{6,38},{7,39},{8,40},{9,... | collective-permute-start | bytes 1769480 | tf_op jit(solution)/shard_map/ppermute | solution.py:39
